TPU v7x, 32 devices: a whole 2x2x4 slice. The times are simulated.
32 devices in a mesh: ka: 4 (over x, core), grid: 8 (over z, y).
Axes of the slice: x: 2, y: 2, z: 4, core: 2. Of those that a mesh axis runs over, the one named last changes fastest.
Arguments:
- orbitals: bfloat16 [4, 2, 512, 8192], P('ka', None, None, 'grid'), may hold values from -6 to 6
- potential: float32 [3, 2, 8192], P(None, None, 'grid'), may hold values from -6 to 6
- partners: int32 [3, 4], replicated, may hold values from 0 to 3, each once within a row
- occupied: int32 [4], replicated, may hold values from 128 to 512
Outputs:
- sources: bfloat16 [3, 4, 2, 512, 8192], P(None, 'ka', None, None, 'grid')
- density: float32 [3, 8192], P(None, 'grid')
Inputs may be any that keep to these rules, and one draw needn't show every extreme that they name: `partners`: each row is a permutation of the 4 k-points.
All inputs are finite; a program needn't handle non-finite values.
Results may differ from a plain program's by a relative error of at most 0.0051.
Values may be sent and summed in bfloat16 or wider, within the bound.
No kernel may reach another device: no remote copies, remote signals or barrier semaphores. Data moves between devices by JAX's collectives and lax.ppermute only.
A program may use at most 128 MiB of HBM per device.

v0:
```python
import jax
import jax.numpy as jnp
from jax import lax
from jax.sharding import PartitionSpec as P


def shards(orbitals, potential, partners, occupied):
    local_count = orbitals.shape[0]
    band_count = orbitals.shape[2]
    point_count = orbitals.shape[3]
    q_count = potential.shape[0]
    k_count = partners.shape[1]
    volume_weight = 1.0 / (point_count * lax.axis_size("grid"))
    density_weight = 2.0 / (k_count * band_count)
    local_ids = lax.axis_index("ka") * local_count + jnp.arange(local_count, dtype=jnp.int32)
    k_table = jnp.arange(k_count, dtype=jnp.int32)
    local_pick = (local_ids[:, None] == k_table[None, :]).astype(jnp.int32)
    own_counts = jnp.sum(local_pick * occupied[None, :], axis=1)
    partner_ids = jnp.sum(local_pick[None, :, :] * partners[:, None, :], axis=2)
    partner_hits = (partner_ids[:, :, None] == k_table[None, None, :]).astype(jnp.int32)
    partner_counts = jnp.sum(partner_hits * occupied[None, None, :], axis=2)
    band_ids = jnp.arange(band_count, dtype=jnp.int32)
    picked = jnp.take(
        lax.all_to_all(orbitals, "ka", split_axis=2, concat_axis=0, tiled=True), partners, axis=0
    )
    fetched = lax.all_to_all(picked, "ka", split_axis=1, concat_axis=3, tiled=True)
    own_real = orbitals[:, 0].astype(jnp.float32)
    own_imag = orbitals[:, 1].astype(jnp.float32)

    def apply_field(q_index):
        real_field = potential[q_index, 0][None, None, :]
        imag_field = potential[q_index, 1][None, None, :]
        applied_real = real_field * own_real - imag_field * own_imag
        applied_imag = real_field * own_imag + imag_field * own_real
        return jnp.stack([applied_real, applied_imag], axis=1).astype(jnp.bfloat16)

    def intersection(partner_orbit, applied):
        swapped = jnp.stack([applied[:, 1], -applied[:, 0]], axis=1)
        over_real = jnp.einsum(
            "kcmg,kcng->kmn", partner_orbit, applied, preferred_element_type=jnp.float32
        )
        over_imag = jnp.einsum(
            "kcmg,kcng->kmn", partner_orbit, swapped, preferred_element_type=jnp.float32
        )
        return volume_weight * jnp.stack([over_real, over_imag], axis=1)

    applied_all = [apply_field(q_index) for q_index in range(q_count)]
    partial_all = jnp.stack(
        [intersection(fetched[q_index], applied_all[q_index]) for q_index in range(q_count)]
    )
    summed_all = lax.psum(partial_all, "grid")
    summed = [summed_all[q_index] for q_index in range(q_count)]
    own_mask = (band_ids[None, :] < own_counts[:, None]).astype(jnp.float32)
    source_list = []
    density_list = []
    for q_index in range(q_count):
        partner_orbit = fetched[q_index]
        applied = applied_all[q_index]
        partner_mask = (band_ids[None, :] < partner_counts[q_index][:, None]).astype(jnp.float32)
        masked = (summed[q_index] * partner_mask[:, None, :, None]).astype(jnp.bfloat16)
        weight_real = jnp.stack([masked[:, 0], -masked[:, 1]], axis=1)
        weight_imag = jnp.stack([masked[:, 1], masked[:, 0]], axis=1)
        mixed_real = jnp.einsum(
            "kcmg,kcmn->kng", partner_orbit, weight_real, preferred_element_type=jnp.float32
        )
        mixed_imag = jnp.einsum(
            "kcmg,kcmn->kng", partner_orbit, weight_imag, preferred_element_type=jnp.float32
        )
        projected_real = applied[:, 0].astype(jnp.float32) - mixed_real
        projected_imag = applied[:, 1].astype(jnp.float32) - mixed_imag
        source_list.append(jnp.stack([projected_real, projected_imag], axis=1).astype(jnp.bfloat16))
        density_term = jnp.sum(
            own_mask[:, :, None] * (own_real * projected_real + own_imag * projected_imag),
            axis=(0, 1),
        )
        density_list.append(density_weight * density_term)
    density = lax.psum(jnp.stack(density_list), "ka")
    return (jnp.stack(source_list), density)


def solution(mesh):
    return jax.shard_map(
        shards,
        mesh=mesh,
        in_specs=(P("ka", None, None, "grid"), P(None, None, "grid"), P(), P()),
        out_specs=(P(None, "ka", None, None, "grid"), P(None, "grid")),
        check_vma=False,
    )
```

profile of v0, /device:TPU:0, one launch (start us, length us, event | category | flops | bytes accessed | tf_op | source)
XLA Modules:
  0.0 410.3 jit_solution(8783927622742305312)
XLA Ops:
  7.2 5.1 %copy.56 = bf16[1,2,512,1024]{3,1,0,2:T(2,128)(2,1)} copy(bf16[1,2,512,1024]{3,2,1,0:T(8,128)(2,1)} %param.4) | data formatting | bytes 4194304 | tf_op args[0]
  12.2 4.3 %all-to-all-start = ((bf16[1,2,512,1024]{3,1,0,2:T(2,128)(2,1)}), bf16[1,2,512,1024]{3,1,0,2:T(2,128)(2,1)S(1)}, u32[]{:S(2)}, u32[]{:S(2)}) async-start(bf16[1,2,512,1024]{3,1,0,2:T(2,128)(2,1)} %copy.56), calls=%async_computation | async-start | bytes 4194304 | tf_op jit(solution)/shard_map/all_to_all | solution.py:24
  16.8 25.5 %all-to-all-done = bf16[1,2,512,1024]{3,1,0,2:T(2,128)(2,1)S(1)} async-done(((bf16[1,2,512,1024]{3,1,0,2:T(2,128)(2,1)}), bf16[1,2,512,1024]{3,1,0,2:T(2,128)(2,1)S(1)}, u32[]{:S(2)}, u32[]{:S(2)}) %all-to-all-start) | async-done | bytes 2097184 | tf_op jit(solution)/shard_map/all_to_all | solution.py:24
  42.3 1.3 copy-done.3
  43.6 2.2 copy.78
  45.8 4.2 %gather_fusion = bf16[12,2,128,1024]{3,2,1,0:T(8,128)(2,1)} fusion(bf16[4,2,128,1024]{3,2,1,0:T(8,128)(2,1)S(1)} %bitcast.206, s32[1024]{0:T(1024)S(1)} %pad_clamp_fusion), kind=kCustom, calls=%fused_computation | custom fusion | bytes 12582960 | tf_op jit(solution)/shard_map/jit(_take)/gather | solution.py:23
  50.0 3.4 broadcast_select_fusion
  53.4 3.4 copy.59
  56.9 5.3 %all-to-all-start.1 = ((bf16[3,4,2,128,1024]{4,3,2,0,1:T(8,128)(2,1)}), bf16[3,4,2,128,1024]{4,3,2,0,1:T(8,128)(2,1)}, u32[]{:S(2)}, u32[]{:S(2)}) async-start(bf16[3,4,2,128,1024]{4,3,2,0,1:T(8,128)(2,1)} %copy.59), calls=%async_computation.1 | async-start | bytes 12582912 | tf_op jit(solution)/shard_map/all_to_all | solution.py:26
  62.5 2.4 fusion.18
  64.9 3.4 fusion.96
  68.3 64.6 %all-to-all-done.1 = bf16[3,4,2,128,1024]{4,3,2,0,1:T(8,128)(2,1)} async-done(((bf16[3,4,2,128,1024]{4,3,2,0,1:T(8,128)(2,1)}), bf16[3,4,2,128,1024]{4,3,2,0,1:T(8,128)(2,1)}, u32[]{:S(2)}, u32[]{:S(2)}) %all-to-all-start.1) | async-done | bytes 6291488 | tf_op jit(solution)/shard_map/all_to_all | solution.py:26
  132.9 3.9 fusion.102
  137.4 1.8 copy-done.10
  144.5 1.3 fusion.63
  149.6 3.6 pad_maximum_fusion
  158.2 207.7 %all-reduce.2.cloned.1.call-done = f32[3,1,2,512,512]{4,3,2,1,0:T(8,128)} async-done(((f32[3,1,2,512,512]{4,3,2,1,0:T(8,128)}), f32[3,1,2,512,512]{4,3,2,1,0:T(8,128)}) %all-reduce.2.cloned.1.call-update) | async-done | bytes 6291472 | tf_op jit(solution)/shard_map/psum | solution.py:51
  365.9 3.4 fusion.32
  369.4 1.5 copy-done.7
  373.5 1.5 copy-done.5
  377.7 1.5 copy-done.2
  380.5 4.8 %fusion.8 = (f32[1024]{0:T(1024)S(1)}, f32[1024]{0:T(1024)S(1)}, f32[1024]{0:T(1024)S(1)}, bf16[1,1,1,512,1024]{4,3,2,1,0:T(8,128)(2,1)}, bf16[1,1,1,512,1024]{4...) fusion(f32[512,1024]{1,0:T(8,128)S(1)} %convert_subtract_fusion, ...), kind=kOutput, calls=%fused_computation.26 | convolution fusion | flops 1087370240 | bytes 23083008 | tf_op jit(solution)/shard_map/kcmg,kcmn->kng/dot_general | solution.py:63
  385.4 11.8 %psum.15 = f32[3,1024]{1,0:T(4,128)} all-reduce(f32[3,1024]{1,0:T(4,128)S(1)} %pad_maximum_fusion.1), channel_id=1, replica_groups=mesh['ka'=4,'grid'=8] {'ka'}, use_global_device_ids=true, to_apply=%region_7.8 | all-reduce | flops 3072 | bytes 24576 | tf_op jit(solution)/shard_map/psum | solution.py:77
  397.1 6.3 %maximum_maximum_fusion = bf16[3,1,2,512,1024]{4,3,2,1,0:T(8,128)(2,1)} fusion(bf16[1,1,1,512,1024]{4,3,2,1,0:T(8,128)(2,1)} %get-tuple-element.18, bf16[1,1,1,512,1024]{4,3,2,1,0:T(8,128)(2,1)} %get-tuple-element.17, bf16[1,1,1,512,1024]{4,3,2,1,0:T(8,128)(2,1)} %get-tuple-element.20, bf16[1,1,1,512,1024]{4,3,2,1,0:T(8,128)(2,1)} %get-tuple-element.19, ...), kind=kLoop, calls=%fused_computation.2 | loop fusion | flops 15728640 | bytes 12582912 | tf_op jit(solution)/shard_map/stack | solution.py:78
  (79 shorter events, 21.6 us)
Async XLA Ops:
  12.2 4.3 %copy-start.22 = (s32[3,4]{1,0:T(4,128)S(1)}, s32[3,4]{1,0:T(4,128)}, u32[]{:S(2)}) copy-start(s32[3,4]{1,0:T(4,128)} %param.6) | copy-start | bytes 148
  12.2 30.0 %all-to-all-start = ((bf16[1,2,512,1024]{3,1,0,2:T(2,128)(2,1)}), bf16[1,2,512,1024]{3,1,0,2:T(2,128)(2,1)S(1)}, u32[]{:S(2)}, u32[]{:S(2)}) async-start(bf16[1,2,512,1024]{3,1,0,2:T(2,128)(2,1)} %copy.56), calls=%async_computation | async-start | bytes 4194304 | tf_op jit(solution)/shard_map/all_to_all | solution.py:24
  42.3 1.3 copy-start.3
  56.9 5.6 %copy-start.21 = (f32[3,2,1024]{2,1,0:T(2,128)S(1)}, f32[3,2,1024]{2,1,0:T(2,128)}, u32[]{:S(2)}) copy-start(f32[3,2,1024]{2,1,0:T(2,128)} %param.5) | copy-start | bytes 73732
  56.9 5.6 %copy-start = (bf16[1,2,512,1024]{3,2,1,0:T(8,128)(2,1)S(1)}, bf16[1,2,512,1024]{3,2,1,0:T(8,128)(2,1)}, u32[]{:S(2)}) copy-start(bf16[1,2,512,1024]{3,2,1,0:T(8,128)(2,1)} %param.4) | copy-start | bytes 6291460
  56.9 76.1 %all-to-all-start.1 = ((bf16[3,4,2,128,1024]{4,3,2,0,1:T(8,128)(2,1)}), bf16[3,4,2,128,1024]{4,3,2,0,1:T(8,128)(2,1)}, u32[]{:S(2)}, u32[]{:S(2)}) async-start(bf16[3,4,2,128,1024]{4,3,2,0,1:T(8,128)(2,1)} %copy.59), calls=%async_computation.1 | async-start | bytes 12582912 | tf_op jit(solution)/shard_map/all_to_all | solution.py:26
  62.2 303.6 %all-reduce.2.cloned.1.call-start = ((), (), s32[]{:S(2)}) async-start(), calls=%async_computation.2 | async-start | bytes 12582912 | tf_op jit(solution)/shard_map/psum | solution.py:51
  137.0 4.6 %copy-start.4 = (bf16[1,1,2,4,128,1024]{5,4,3,2,1,0:T(8,128)(2,1)}, bf16[1,1,2,4,128,1024]{5,4,3,2,1,0:T(8,128)(2,1)S(1)}, u32[]{:S(2)}) copy-start(bf16[1,1,2,4,128,1024]{5,4,3,2,1,0:T(8,128)(2,1)S(1)} %copy.61) | copy-start | bytes 6291460
  137.2 7.2 %copy-start.1 = (bf16[1,1,2,4,128,1024]{5,4,3,2,1,0:T(8,128)(2,1)}, bf16[1,1,2,4,128,1024]{5,4,3,2,1,0:T(8,128)(2,1)S(1)}, u32[]{:S(2)}) copy-start(bf16[1,1,2,4,128,1024]{5,4,3,2,1,0:T(8,128)(2,1)S(1)} %copy.60) | copy-start | bytes 6291460
  137.2 2.0 copy-start.10
  137.2 3.1 copy-start.20
  137.4 9.9 %copy-start.6 = (bf16[1,1,2,4,128,1024]{5,4,3,2,1,0:T(8,128)(2,1)}, bf16[1,1,2,4,128,1024]{5,4,3,2,1,0:T(8,128)(2,1)S(1)}, u32[]{:S(2)}) copy-start(bf16[1,1,2,4,128,1024]{5,4,3,2,1,0:T(8,128)(2,1)S(1)} %copy.62) | copy-start | bytes 6291460
  140.3 1.3 copy-start.12
  141.6 1.3 copy-start.8
  141.7 1.5 copy-start.19
  144.5 1.3 copy-start.14
  144.5 1.5 copy-start.18
  146.0 1.3 copy-start.16
  365.9 3.5 copy-start.17
  369.2 1.6 copy-start.7
  372.1 1.4 copy-start.13
  373.4 1.6 copy-start.5
  376.3 1.4 copy-start.9
  377.6 1.6 copy-start.2
  (3 other events, 3.2 us)
Sparse Core Ops, SparseCore 0:
  153.4 212.3 all-reduce.1
where the time goes:
time: 411 us; the launch traced here: 410 us
  waiting for transfers between devices  298 us (73%)
  local copies, waits for them, and re-layouts  29.8 us (7%)
  other arithmetic  27.6 us (7%)
  matrix products  18.9 us (5%)
  between operations  14.5 us (4%)
  blocking collectives  11.8 us (3%)
  starting transfers between devices  9.91 us (2%)
    psum x1, waiting for transfers between devices, shards(): summed_all = lax.psum(partial_all, 'grid')  208 us
    all_to_all x1, waiting for transfers between devices, shards(): lax.all_to_all(picked, 'ka', split_axis=1, concat_axis=3, tiled=True)  64.6 us
    all_to_all x1, waiting for transfers between devices, shards(): lax.all_to_all(orbitals, 'ka', split_axis=2, concat_axis=0, tiled=True)  25.5 us
    unnamed x49, local copies, waits for them, and re-layouts  14.8 us
    psum x1, blocking collectives, shards(): density = lax.psum(jnp.stack(density_list), 'ka')  11.8 us
  transfers between devices with their start and end apart: 3, of which 3 were waited for; matrix products, arithmetic and copies ran while one was open for 3% of the time, Pallas kernels for 0%

commit v1 on v0

v1 whole, which is shorter than its diff:
```python
import functools

import jax
import jax.numpy as jnp
from jax import lax
from jax.experimental import pallas as pl
from jax.experimental.pallas import tpu as pltpu
from jax.sharding import PartitionSpec as P

VMEM_LIMIT = 56 * 1024 * 1024
PLAN = ((0, 2, "all"), (2, 4, "each"))


def swap(value, axis, bit):
    size = lax.axis_size(axis)
    return lax.ppermute(value, axis, [(i, i ^ bit) for i in range(size)])


def axis_bits(axis):
    size = lax.axis_size(axis)
    return [1 << b for b in range(size.bit_length() - 1)]


def apply_field(orbitals, potential):
    real = orbitals[0].astype(jnp.float32)
    imag = orbitals[1].astype(jnp.float32)
    u = potential[:, 0][:, None, :]
    v = potential[:, 1][:, None, :]
    return jnp.stack([u * real - v * imag, u * imag + v * real], axis=1).astype(jnp.bfloat16)


def nt_dot(left, right):
    return lax.dot_general(left, right, (((1,), (1,)), ((), ())), preferred_element_type=jnp.float32)


def overlap(applied_ref, partner, out_ref):
    a_real, a_imag = applied_ref[0, 0], applied_ref[0, 1]
    p_real, p_imag = partner[0], partner[1]
    out_ref[0, 0] = (nt_dot(a_real, p_real) + nt_dot(a_imag, p_imag)).astype(out_ref.dtype)
    out_ref[0, 1] = (nt_dot(a_imag, p_real) - nt_dot(a_real, p_imag)).astype(out_ref.dtype)


def send_kernel(count, picks_ref, half_ref, applied_ref, *refs):
    sources, (out_ref, pick_ref) = refs[:count], refs[count:]
    pick = picks_ref[pl.program_id(0)]
    for j in range(count):
        @pl.when(pick == j)
        def _():
            pick_ref[0] = sources[j][...]
    overlap(applied_ref, pick_ref[0], out_ref)


def keep_kernel(half_ref, applied_ref, pick_ref, out_ref):
    overlap(applied_ref, pick_ref[0], out_ref)


def overlap_send(q0, q_count, start, picks, half, applied, sources):
    _, _, bands, points = applied.shape
    width = sources[-1][0].shape[1]
    rows = bands // 2
    specs = []
    for array, is_whole in sources:
        row = start // width if is_whole else 0
        specs.append(pl.BlockSpec((2, width, points), lambda q, p, h, row=row: (0, row, 0), pipeline_mode=pl.Buffered(1)))
    return pl.pallas_call(
        functools.partial(send_kernel, len(sources)),
        grid_spec=pltpu.PrefetchScalarGridSpec(
            num_scalar_prefetch=2,
            grid=(q_count,),
            in_specs=[pl.BlockSpec((1, 2, rows, points), lambda q, p, h: (q0 + q, 0, h[0], 0))] + specs,
            out_specs=[
                pl.BlockSpec((1, 2, rows, width), lambda q, p, h: (q, 0, 0, 0)),
                pl.BlockSpec((1, 2, width, points), lambda q, p, h: (q, 0, 0, 0)),
            ],
        ),
        out_shape=[
            jax.ShapeDtypeStruct((q_count, 2, rows, width), jnp.bfloat16),
            jax.ShapeDtypeStruct((q_count, 2, width, points), jnp.bfloat16),
        ],
        compiler_params=pltpu.CompilerParams(vmem_limit_bytes=VMEM_LIMIT),
        cost_estimate=pl.CostEstimate(
            flops=8 * q_count * rows * width * points,
            bytes_accessed=q_count * 4 * points * (rows + width) + 4 * len(sources) * width * points,
            transcendentals=0,
        ),
    )(picks, half, applied, *[array for array, _ in sources])


def overlap_keep(q0, half, applied, picked):
    q_count, _, width, points = picked.shape
    rows = applied.shape[2] // 2
    return pl.pallas_call(
        keep_kernel,
        grid_spec=pltpu.PrefetchScalarGridSpec(
            num_scalar_prefetch=1,
            grid=(q_count,),
            in_specs=[
                pl.BlockSpec((1, 2, rows, points), lambda q, h: (q0 + q, 0, h[0], 0)),
                pl.BlockSpec((1, 2, width, points), lambda q, h: (q, 0, 0, 0)),
            ],
            out_specs=pl.BlockSpec((1, 2, rows, width), lambda q, h: (q, 0, 0, 0)),
        ),
        out_shape=jax.ShapeDtypeStruct((q_count, 2, rows, width), jnp.float32),
        compiler_params=pltpu.CompilerParams(vmem_limit_bytes=VMEM_LIMIT),
        cost_estimate=pl.CostEstimate(
            flops=8 * q_count * rows * width * points,
            bytes_accessed=q_count * 4 * points * (rows + width),
            transcendentals=0,
        ),
    )(half, applied, picked)


def mix_kernel(chunk_count, weight_scale, count_ref, applied_ref, own_ref, *refs):
    weights = refs[:chunk_count]
    partners = refs[chunk_count:2 * chunk_count]
    source_ref, density_ref = refs[-2:]
    block = own_ref.shape[1]
    real = applied_ref[0, 0].astype(jnp.float32)
    imag = applied_ref[0, 1].astype(jnp.float32)
    for weight, partner in zip(weights, partners):
        w_real, w_imag = weight[0, 0], weight[0, 1]
        p_real, p_imag = partner[0, 0], partner[0, 1]
        real -= jnp.dot(w_real, p_real, preferred_element_type=jnp.float32)
        real += jnp.dot(w_imag, p_imag, preferred_element_type=jnp.float32)
        imag -= jnp.dot(w_imag, p_real, preferred_element_type=jnp.float32)
        imag -= jnp.dot(w_real, p_imag, preferred_element_type=jnp.float32)
    source_ref[0, 0, 0] = real.astype(jnp.bfloat16)
    source_ref[0, 0, 1] = imag.astype(jnp.bfloat16)
    term = own_ref[0].astype(jnp.float32) * real + own_ref[1].astype(jnp.float32) * imag
    ids = pl.program_id(0) * block + lax.broadcasted_iota(jnp.int32, (block, 1), 0)
    term = jnp.where(ids < count_ref[0], term, 0.0)
    total = weight_scale * jnp.sum(term, axis=0, keepdims=True)

    @pl.when(pl.program_id(0) == 0)
    def _():
        density_ref[...] = jnp.zeros_like(density_ref)

    density_ref[...] += total


def mix(q, count, applied, orbitals, weights, partners, buffer, weight_scale):
    q_total, _, bands, points = applied.shape
    block = bands // 4
    n = len(weights)
    specs = [
        pl.BlockSpec((1, 2, block, points), lambda i, c: (q, 0, i, 0)),
        pl.BlockSpec((2, block, points), lambda i, c: (0, i, 0)),
    ]
    arrays = [applied, orbitals]
    for at, weight in weights:
        specs.append(pl.BlockSpec((1, 2, block, weight.shape[3]), lambda i, c, at=at: (at, 0, i, 0)))
        arrays.append(weight)
    for at, partner in partners:
        specs.append(pl.BlockSpec((1,) + partner.shape[1:], lambda i, c, at=at: (at, 0, 0, 0)))
        arrays.append(partner)
    aliases = {}
    if buffer is not None:
        specs.append(pl.BlockSpec(memory_space=pl.ANY))
        arrays.append(buffer)
        aliases = {len(arrays): 0}
    return pl.pallas_call(
        functools.partial(mix_kernel, n, weight_scale),
        grid_spec=pltpu.PrefetchScalarGridSpec(
            num_scalar_prefetch=1,
            grid=(bands // block,),
            in_specs=specs,
            out_specs=[
                pl.BlockSpec((1, 1, 2, block, points), lambda i, c: (q, 0, 0, i, 0)),
                pl.BlockSpec((1, points), lambda i, c: (0, 0)),
            ],
        ),
        out_shape=[
            jax.ShapeDtypeStruct((q_total, 1, 2, bands, points), jnp.bfloat16),
            jax.ShapeDtypeStruct((1, points), jnp.float32),
        ],
        input_output_aliases=aliases,
        compiler_params=pltpu.CompilerParams(vmem_limit_bytes=VMEM_LIMIT),
        cost_estimate=pl.CostEstimate(
            flops=8 * bands * bands * points, bytes_accessed=16 * bands * points, transcendentals=0
        ),
    )(count, *arrays)


def shards(orbitals, potential, partners, occupied):
    own = orbitals[0]
    bands, points = own.shape[1:]
    q_count = potential.shape[0]
    k_count = partners.shape[1]
    k_index = lax.axis_index("ka")
    g_index = lax.axis_index("grid")
    ka_bits = axis_bits("ka")[::-1]
    grid_bits = axis_bits("grid")
    volume_weight = 1.0 / (points * lax.axis_size("grid"))
    density_weight = 2.0 / (k_count * bands)
    k_table = jnp.arange(k_count, dtype=jnp.int32)
    partner_ids = jnp.sum((k_table == k_index) * partners, axis=1)
    partner_counts = jnp.sum((partner_ids[:, None] == k_table[None, :]) * occupied[None, :], axis=1)
    own_count = jnp.sum((k_table == k_index) * occupied)[None]
    picks = partner_ids ^ k_index

    sent = []
    for first, last, _ in PLAN:
        start, stop = first * bands // 4, last * bands // 4
        have = {0: own[:, start:stop]}
        for bit in ka_bits[:-1]:
            for rel in list(have):
                have[rel ^ bit] = swap(have[rel], "ka", bit)
        sent.append((start, stop, have))
    sibling = swap(own, "ka", ka_bits[-1])
    applied = apply_field(own, potential)

    def bit_of(bit):
        return (g_index // bit) % 2

    first_bit = bit_of(grid_bits[0])
    keep_half = first_bit[None].astype(jnp.int32)
    send_half = 1 - keep_half

    def reduce_scatter(keep, arriving):
        for bit in grid_bits[1:]:
            mine = bit_of(bit)
            half = keep.shape[2] // 2

            def part(which):
                return lax.dynamic_slice_in_dim(keep, which * half, half, 2) + lax.dynamic_slice_in_dim(
                    arriving, which * half, half, 2
                ).astype(jnp.float32)

            leaving = part(1 - mine).astype(jnp.bfloat16)
            keep, arriving = part(mine), swap(leaving, "grid", bit)
        return keep + arriving.astype(jnp.float32)

    def all_gather(piece):
        for bit in grid_bits[::-1]:
            other = swap(piece, "grid", bit)
            upper = bit_of(bit) == 1
            piece = jnp.concatenate([jnp.where(upper, other, piece), jnp.where(upper, piece, other)], axis=2)
        return piece

    weights = [[] for _ in range(q_count)]
    picked = [[] for _ in range(q_count)]
    for (start, stop, have), (_, _, mode) in zip(sent, PLAN):
        for rel in list(have):
            if rel:
                have[rel ^ ka_bits[-1]] = swap(have[rel], "ka", ka_bits[-1])
        have[ka_bits[-1]] = None
        sources = []
        for rel in range(len(have)):
            whole = {0: own, ka_bits[-1]: sibling}.get(rel)
            sources.append((have[rel], False) if whole is None else (whole, True))
        groups = [(0, q_count)] if mode == "all" else [(q, 1) for q in range(q_count)]
        for q0, count in groups:
            leaving, chosen = overlap_send(q0, count, start, picks[q0:q0 + count], send_half, applied, sources)
            arriving = swap(leaving, "grid", grid_bits[0])
            keep = overlap_keep(q0, keep_half, applied, chosen)
            total = reduce_scatter(keep, arriving)
            limits = partner_counts[q0:q0 + count][:, None, None, None]
            mask = (start + jnp.arange(stop - start, dtype=jnp.int32)) < limits
            piece = jnp.where(mask, volume_weight * total, 0.0).astype(jnp.bfloat16)
            whole = all_gather(piece)
            for q in range(q0, q0 + count):
                weights[q].append((q - q0, whole))
                picked[q].append((q - q0, chosen))

    buffer = None
    density = []
    for q in range(q_count):
        buffer, term = mix(q, own_count, applied, own, weights[q], picked[q], buffer, density_weight)
        density.append(term)
    density = jnp.concatenate(density, axis=0)
    parts = [density] + [swap_by(density, d) for d in range(1, lax.axis_size("ka"))]
    while len(parts) > 1:
        half = len(parts) // 2
        parts = [parts[i] + parts[i + half] for i in range(half)]
    return buffer, parts[0]


def swap_by(value, distance):
    return swap(value, "ka", distance)


def solution(mesh):
    return jax.shard_map(
        shards,
        mesh=mesh,
        in_specs=(P("ka", None, None, "grid"), P(None, None, "grid"), P(), P()),
        out_specs=(P(None, "ka", None, None, "grid"), P(None, "grid")),
        check_vma=False,
    )
```

time: 411 us -> 221 us (0.54)
  waiting for transfers between devices: 298 us -> 98.7 us
  Pallas kernels: 0 us -> 59.7 us
  starting transfers between devices: 9.91 us -> 33.5 us
  local copies, waits for them, and re-layouts: 29.8 us -> 6.41 us
  matrix products: 18.9 us -> 0 us
  between operations: 14.5 us -> 1.15 us
  blocking collectives: 11.8 us -> 0 us
  other arithmetic: 27.6 us -> 20.6 us
    psum x1 -> x0, waiting for transfers between devices: 208 us -> none  [shards(): summed_all = lax.psum(partial_all, 'grid')]
    ppermute x0 -> x32, waiting for transfers between devices: none -> 98.7 us  [swap(): return lax.ppermute(value, axis, [(i, i ^ bit) for i in range(size)])]
    all_to_all x2 -> x0, waiting for transfers between devices: 90 us -> none  [the longest x1 64.6 us: shards(): lax.all_to_all(picked, 'ka', split_axis=1, concat_axis=3, tiled=True)]
    pallas_call x0 -> x11, Pallas kernels: none -> 59.7 us  [the longest x3 23.2 us: mix(): pl.pallas_call(functools.partial(mix_kernel, n, weight_scale), grid_spec=...]
    ppermute x0 -> x32, starting transfers between devices: none -> 33.5 us  [swap(): return lax.ppermute(value, axis, [(i, i ^ bit) for i in range(size)])]
    dot_general x12 -> x0, matrix products: 18.9 us -> none  [the longest x3 7.4 us: shards(): jnp.einsum('kcmg,kcmn->kng', partner_orbit, weight_real, preferred_elemen...]
    unnamed x49 -> x27, local copies, waits for them, and re-layouts: 14.8 us -> 1.99 us
    psum x1 -> x0, blocking collectives: 11.8 us -> none  [shards(): density = lax.psum(jnp.stack(density_list), 'ka')]
  transfers between devices with their start and end apart: 3 -> 32, of which waited for: 3 -> 16; matrix products, arithmetic and copies ran while one was open for 3% -> 10% of each run, Pallas kernels for 0% -> 17%
where the time goes in v1:
time: 221 us; the launch traced here: 220 us
  waiting for transfers between devices  98.7 us (45%)
  Pallas kernels  59.7 us (27%)
  starting transfers between devices  33.5 us (15%)
  other arithmetic  20.6 us (9%)
  local copies, waits for them, and re-layouts  6.41 us (3%)
    ppermute x32, waiting for transfers between devices, swap(): return lax.ppermute(value, axis, [(i, i ^ bit) for i in range(size)])  98.7 us
    ppermute x32, starting transfers between devices, swap(): return lax.ppermute(value, axis, [(i, i ^ bit) for i in range(size)])  33.5 us
    pallas_call x3, Pallas kernels, mix(): pl.pallas_call(functools.partial(mix_kernel, n, weight_scale), grid_spec=...  23.2 us
    pallas_call x4, Pallas kernels, overlap_send(): pl.pallas_call(functools.partial(send_kernel, len(sources)), grid_spec=pl...  21.4 us
    pallas_call x4, Pallas kernels, overlap_keep(): pl.pallas_call(keep_kernel, grid_spec=pltpu.PrefetchScalarGridSpec(num_sc...  15 us
  transfers between devices with their start and end apart: 32, of which 16 were waited for; matrix products, arithmetic and copies ran while one was open for 10% of the time, Pallas kernels for 17%

profile of v1, /device:TPU:0, one launch (start us, length us, event | category | flops | bytes accessed | tf_op | source)
XLA Modules:
  0.0 220.0 jit_solution(9787575606917268450)
XLA Ops:
  1.2 3.1 %fusion.4 = (bf16[2,256,1024]{2,1,0:T(8,128)(2,1)}, bf16[2,256,1024]{2,1,0:T(8,128)(2,1)}) fusion(bf16[2,512,1024]{2,1,0:T(8,128)(2,1)} %bitcast.17), kind=kLoop, calls=%fused_computation.73 | loop fusion | bytes 4194304 | tf_op jit(solution)/shard_map/slice | solution.py:204
  4.3 2.6 %collective-permute-start.9 = (bf16[2,256,1024]{2,1,0:T(8,128)(2,1)}, bf16[2,256,1024]{2,1,0:T(8,128)(2,1)S(1)}, u32[]{:S(2)}, u32[]{:S(2)}) collective-permute-start(bf16[2,256,1024]{2,1,0:T(8,128)(2,1)} %get-tuple-element.34), channel_id=1, source_target_pairs={{0,16},{8,24},{16,0},{24,8},{1,17},{9,25},{17,1},{25,9},{2,18},{10... | collective-permute-start | bytes 3145736 | tf_op jit(solution)/shard_map/ppermute | solution.py:16
  11.9 19.2 %collective-permute-done.9.refs_2_ = bf16[2,256,1024]{2,1,0:T(8,128)(2,1)S(1)} collective-permute-done((bf16[2,256,1024]{2,1,0:T(8,128)(2,1)}, bf16[2,256,1024]{2,1,0:T(8,128)(2,1)S(1)}, u32[]{:S(2)}, u32[]{:S(2)}) %collective-permute-start.9) | collective-permute-done | bytes 1048608 | tf_op jit(solution)/shard_map/ppermute | solution.py:16
  32.5 20.9 %collective-permute-done.1.refs_2_ = bf16[2,256,1024]{2,1,0:T(8,128)(2,1)} collective-permute-done((bf16[2,256,1024]{2,1,0:T(8,128)(2,1)}, bf16[2,256,1024]{2,1,0:T(8,128)(2,1)}, u32[]{:S(2)}, u32[]{:S(2)}) %collective-permute-start.1) | collective-permute-done | bytes 1048608 | tf_op jit(solution)/shard_map/ppermute | solution.py:16
  54.0 3.3 %subtract_convert_fusion = (bf16[3,1,512,1024]{3,2,1,0:T(8,128)(2,1)S(1)}, bf16[3,1,512,1024]{3,2,1,0:T(8,128)(2,1)S(1)}) fusion(f32[512,1024]{1,0:T(8,128)} %get-tuple-element.37, f32[3,1024]{1,0:T(4,128)S(1)} %get-tuple-element.76, f32[512,1024]{1,0:T(8,128)} %get-tuple-element.36, f32[3,1024]{1,0:T(4,128)S(1)} %get-tuple-element.77), kind=kLoop, calls=%fused_computation.2 | loop fusion | flops 12582912 | bytes 10510336 | tf_op jit(solution)/shard_map/convert.2
  57.3 3.2 %pad_maximum_fusion.applied_ref = bf16[3,2,512,1024]{3,2,1,0:T(8,128)(2,1)} fusion(bf16[3,1,512,1024]{3,2,1,0:T(8,128)(2,1)S(1)} %get-tuple-element.31, bf16[3,1,512,1024]{3,2,1,0:T(8,128)(2,1)S(1)} %get-tuple-element.30), kind=kLoop, calls=%fused_computation | loop fusion | flops 3145728 | bytes 12582912 | tf_op jit(solution)/shard_map/stack | solution.py:29
  61.5 4.6 %shard_map.65 = (bf16[1,2,256,256]{3,2,1,0:T(8,128)(2,1)}, bf16[1,2,256,1024]{3,2,1,0:T(8,128)(2,1)}) custom-call(s32[1]{0:T(128)} %get-tuple-element.73.picks_ref, s32[1]{0:T(128)S(6)} %sub.54.half_ref, bf16[3,2,512,1024]{3,2,1,0:T(8,128)(2,1)} %pad_maximum_fusion.applied_ref, bf16[2,512,1024]{2,1,0:T(8,128)(2,1)} %bitcast.18, ...), custom_call_target="tpu_custom_call" | custom-call | flops 536870912 | bytes 6291456 | tf_op jit(solution)/shard_map/pallas_call | solution.py:65
  67.9 4.7 %shard_map.63 = (bf16[1,2,256,256]{3,2,1,0:T(8,128)(2,1)}, bf16[1,2,256,1024]{3,2,1,0:T(8,128)(2,1)}) custom-call(s32[1]{0:T(128)} %get-tuple-element.74.picks_ref, s32[1]{0:T(128)S(6)} %sub.54.half_ref, bf16[3,2,512,1024]{3,2,1,0:T(8,128)(2,1)} %pad_maximum_fusion.applied_ref, bf16[2,512,1024]{2,1,0:T(8,128)(2,1)} %bitcast.19, ...), custom_call_target="tpu_custom_call" | custom-call | flops 536870912 | bytes 6291456 | tf_op jit(solution)/shard_map/pallas_call | solution.py:65
  72.8 4.8 %shard_map.61 = (bf16[1,2,256,256]{3,2,1,0:T(8,128)(2,1)}, bf16[1,2,256,1024]{3,2,1,0:T(8,128)(2,1)}) custom-call(s32[1]{0:T(128)} %get-tuple-element.75.picks_ref, s32[1]{0:T(128)S(6)} %sub.54.half_ref, bf16[3,2,512,1024]{3,2,1,0:T(8,128)(2,1)} %pad_maximum_fusion.applied_ref, bf16[2,512,1024]{2,1,0:T(8,128)(2,1)} %bitcast.20, ...), custom_call_target="tpu_custom_call" | custom-call | flops 536870912 | bytes 6291456 | tf_op jit(solution)/shard_map/pallas_call | solution.py:65
  80.4 7.2 %shard_map.59 = (bf16[3,2,256,256]{3,2,1,0:T(8,128)(2,1)}, bf16[3,2,256,1024]{3,2,1,0:T(8,128)(2,1)}) custom-call(s32[3]{0:T(128)} %copy-done.10, s32[1]{0:T(128)S(6)} %sub.54.half_ref, bf16[3,2,512,1024]{3,2,1,0:T(8,128)(2,1)} %pad_maximum_fusion.applied_ref, bf16[2,512,1024]{2,1,0:T(8,128)(2,1)} %bitcast.21, ...), custom_call_target="tpu_custom_call" | custom-call | flops 1610612736 | bytes 10485760 | tf_op jit(solution)/shard_map/pallas_call | solution.py:65
  87.9 5.7 %shard_map.60 = f32[3,2,256,256]{3,2,1,0:T(8,128)} custom-call(s32[1]{0:T(128)} %bitcast.4.half_ref, bf16[3,2,512,1024]{3,2,1,0:T(8,128)(2,1)} %pad_maximum_fusion.applied_ref, bf16[3,2,256,1024]{3,2,1,0:T(8,128)(2,1)} %get-tuple-element.16.pick_ref.refs_2_), custom_call_target="tpu_custom_call" | custom-call | flops 1610612736 | bytes 6291456 | tf_op jit(solution)/shard_map/pallas_call | solution.py:92
  93.6 3.1 %shard_map.66 = f32[1,2,256,256]{3,2,1,0:T(8,128)} custom-call(s32[1]{0:T(128)} %bitcast.4.half_ref, bf16[3,2,512,1024]{3,2,1,0:T(8,128)(2,1)} %pad_maximum_fusion.applied_ref, bf16[1,2,256,1024]{3,2,1,0:T(8,128)(2,1)} %get-tuple-element.22.pick_ref.refs_3_), custom_call_target="tpu_custom_call" | custom-call | flops 536870912 | bytes 2097152 | tf_op jit(solution)/shard_map/pallas_call | solution.py:92
  96.7 3.1 %shard_map.64 = f32[1,2,256,256]{3,2,1,0:T(8,128)} custom-call(s32[1]{0:T(128)} %bitcast.4.half_ref, bf16[3,2,512,1024]{3,2,1,0:T(8,128)(2,1)} %pad_maximum_fusion.applied_ref, bf16[1,2,256,1024]{3,2,1,0:T(8,128)(2,1)} %get-tuple-element.20.pick_ref.refs_3_), custom_call_target="tpu_custom_call" | custom-call | flops 536870912 | bytes 2097152 | tf_op jit(solution)/shard_map/pallas_call | solution.py:92
  99.8 3.2 %shard_map.62 = f32[1,2,256,256]{3,2,1,0:T(8,128)} custom-call(s32[1]{0:T(128)} %bitcast.4.half_ref, bf16[3,2,512,1024]{3,2,1,0:T(8,128)(2,1)} %pad_maximum_fusion.applied_ref, bf16[1,2,256,1024]{3,2,1,0:T(8,128)(2,1)} %get-tuple-element.18.pick_ref.refs_3_), custom_call_target="tpu_custom_call" | custom-call | flops 536870912 | bytes 2097152 | tf_op jit(solution)/shard_map/pallas_call | solution.py:92
  109.4 3.0 %collective-permute-start.25 = (bf16[1,2,64,256]{3,2,1,0:T(8,128)(2,1)S(1)}, bf16[1,2,64,256]{3,2,1,0:T(8,128)(2,1)S(1)}, u32[]{:S(2)}, u32[]{:S(2)}) collective-permute-start(bf16[1,2,64,256]{3,2,1,0:T(8,128)(2,1)S(1)} %add_convert_fusion.6), channel_id=1, source_target_pairs={{0,4},{1,5},{2,6},{3,7},{4,0},{5,1},{6,2},{7,3},{8,12},{9,13},{10,... | collective-permute-start | bytes 196616 | tf_op jit(solution)/shard_map/ppermute | solution.py:16
  118.9 3.9 %collective-permute-done.19 = bf16[1,2,64,256]{3,2,1,0:T(8,128)(2,1)S(1)} collective-permute-done((bf16[1,2,64,256]{3,2,1,0:T(8,128)(2,1)S(1)}, bf16[1,2,64,256]{3,2,1,0:T(8,128)(2,1)S(1)}, u32[]{:S(2)}, u32[]{:S(2)}) %collective-permute-start.19) | collective-permute-done | bytes 65568 | tf_op jit(solution)/shard_map/ppermute | solution.py:16
  131.7 12.4 %collective-permute-done.4 = bf16[3,2,128,256]{3,2,1,0:T(8,128)(2,1)S(1)} collective-permute-done((bf16[3,2,128,256]{3,2,1,0:T(8,128)(2,1)S(1)}, bf16[3,2,128,256]{3,2,1,0:T(8,128)(2,1)S(1)}, u32[]{:S(2)}, u32[]{:S(2)}) %collective-permute-start.4) | collective-permute-done | bytes 393248 | tf_op jit(solution)/shard_map/ppermute | solution.py:16
  146.1 10.5 %collective-permute-done.5 = bf16[3,2,64,256]{3,2,1,0:T(8,128)(2,1)S(1)} collective-permute-done((bf16[3,2,64,256]{3,2,1,0:T(8,128)(2,1)S(1)}, bf16[3,2,64,256]{3,2,1,0:T(8,128)(2,1)S(1)}, u32[]{:S(2)}, u32[]{:S(2)}) %collective-permute-start.5) | collective-permute-done | bytes 196640 | tf_op jit(solution)/shard_map/ppermute | solution.py:16
  158.9 5.0 %collective-permute-done.6 = bf16[3,2,64,256]{3,2,1,0:T(8,128)(2,1)S(1)} collective-permute-done((bf16[3,2,64,256]{3,2,1,0:T(8,128)(2,1)S(1)}, bf16[3,2,64,256]{3,2,1,0:T(8,128)(2,1)S(1)}, u32[]{:S(2)}, u32[]{:S(2)}) %collective-permute-start.6) | collective-permute-done | bytes 196640 | tf_op jit(solution)/shard_map/ppermute | solution.py:16
  166.1 5.6 %collective-permute-done.7 = bf16[3,2,128,256]{3,2,1,0:T(8,128)(2,1)S(1)} collective-permute-done((bf16[3,2,128,256]{3,2,1,0:T(8,128)(2,1)S(1)}, bf16[3,2,128,256]{3,2,1,0:T(8,128)(2,1)S(1)}, u32[]{:S(2)}, u32[]{:S(2)}) %collective-permute-start.7) | collective-permute-done | bytes 393248 | tf_op jit(solution)/shard_map/ppermute | solution.py:16
  176.6 10.8 %collective-permute-done.8 = bf16[3,2,256,256]{3,2,1,0:T(8,128)(2,1)S(1)} collective-permute-done((bf16[3,2,256,256]{3,2,1,0:T(8,128)(2,1)S(1)}, bf16[3,2,256,256]{3,2,1,0:T(8,128)(2,1)S(1)}, u32[]{:S(2)}, u32[]{:S(2)}) %collective-permute-start.8) | collective-permute-done | bytes 786464 | tf_op jit(solution)/shard_map/ppermute | solution.py:16
  189.0 7.7 %shard_map.67 = (bf16[3,1,2,512,1024]{4,3,2,1,0:T(8,128)(2,1)}, f32[1,1024]{1,0:T(1,128)}) custom-call(s32[1]{0:T(128)} %bitcast.count_ref, bf16[3,2,512,1024]{3,2,1,0:T(8,128)(2,1)} %pad_maximum_fusion.applied_ref, bf16[2,512,1024]{2,1,0:T(8,128)(2,1)} %bitcast.22, bf16[3,2,512,256]{3,2,1,0:T(8,128)(2,1)} %pad_maximum_fusion.1.refs_0_, ...), custom_call_target="tpu_custom_call" | custom-call | flops 2147483648 | bytes 8388608 | tf_op jit(solution)/shard_map/pallas_call | solution.py:161
  196.7 7.7 %shard_map.68 = (bf16[3,1,2,512,1024]{4,3,2,1,0:T(8,128)(2,1)}, f32[1,1024]{1,0:T(1,128)}) custom-call(s32[1]{0:T(128)} %bitcast.count_ref, bf16[3,2,512,1024]{3,2,1,0:T(8,128)(2,1)} %pad_maximum_fusion.applied_ref, bf16[2,512,1024]{2,1,0:T(8,128)(2,1)} %bitcast.23, ...), custom_call_target="tpu_custom_call", output_to_operand_aliasing={{0}: (7, {})} | custom-call | flops 2147483648 | bytes 8388608 | tf_op jit(solution)/shard_map/pallas_call | solution.py:161
  204.5 7.8 %shard_map.69 = (bf16[3,1,2,512,1024]{4,3,2,1,0:T(8,128)(2,1)}, f32[1,1024]{1,0:T(1,128)}) custom-call(s32[1]{0:T(128)} %bitcast.count_ref, bf16[3,2,512,1024]{3,2,1,0:T(8,128)(2,1)} %pad_maximum_fusion.applied_ref, bf16[2,512,1024]{2,1,0:T(8,128)(2,1)} %bitcast.24, ...), custom_call_target="tpu_custom_call", output_to_operand_aliasing={{0}: (7, {})} | custom-call | flops 2147483648 | bytes 8388608 | tf_op jit(solution)/shard_map/pallas_call | solution.py:161
  (132 shorter events, 55.8 us)
Async XLA Ops:
  0.7 59.8 %collective-permute-start = (bf16[2,512,1024]{2,1,0:T(8,128)(2,1)}, bf16[2,512,1024]{2,1,0:T(8,128)(2,1)}, u32[]{:S(2)}, u32[]{:S(2)}) collective-permute-start(bf16[2,512,1024]{2,1,0:T(8,128)(2,1)} %bitcast.16), channel_id=1, source_target_pairs={{0,8},{8,0},{16,24},{24,16},{1,9},{9,1},{17,25},{25,17},{2,10},{10... | collective-permute-start | bytes 6291464 | tf_op jit(solution)/shard_map/ppermute | solution.py:16
  4.3 26.8 %collective-permute-start.9 = (bf16[2,256,1024]{2,1,0:T(8,128)(2,1)}, bf16[2,256,1024]{2,1,0:T(8,128)(2,1)S(1)}, u32[]{:S(2)}, u32[]{:S(2)}) collective-permute-start(bf16[2,256,1024]{2,1,0:T(8,128)(2,1)} %get-tuple-element.34), channel_id=1, source_target_pairs={{0,16},{8,24},{16,0},{24,8},{1,17},{9,25},{17,1},{25,9},{2,18},{10... | collective-permute-start | bytes 3145736 | tf_op jit(solution)/shard_map/ppermute | solution.py:16
  6.9 46.4 %collective-permute-start.1 = (bf16[2,256,1024]{2,1,0:T(8,128)(2,1)}, bf16[2,256,1024]{2,1,0:T(8,128)(2,1)}, u32[]{:S(2)}, u32[]{:S(2)}) collective-permute-start(bf16[2,256,1024]{2,1,0:T(8,128)(2,1)} %get-tuple-element.35), channel_id=1, source_target_pairs={{0,16},{8,24},{16,0},{24,8},{1,17},{9,25},{17,1},{25,9},{2,18},{10... | collective-permute-start | bytes 3145736 | tf_op jit(solution)/shard_map/ppermute | solution.py:16
  31.1 29.4 %collective-permute-start.10 = (bf16[2,256,1024]{2,1,0:T(8,128)(2,1)S(1)}, bf16[2,256,1024]{2,1,0:T(8,128)(2,1)S(1)}, u32[]{:S(2)}, u32[]{:S(2)}) collective-permute-start(bf16[2,256,1024]{2,1,0:T(8,128)(2,1)S(1)} %collective-permute-done.9.refs_2_), channel_id=1, source_target_pairs={{0,8},{8,0},{16,24},{24,16},{1,9},{9,1},{17,25},{25,17},{2,10},{10... | collective-permute-start | bytes 3145736 | tf_op jit(solution)/shard_map/ppermute | solution.py:16
  53.4 26.1 %collective-permute-start.2 = (bf16[2,256,1024]{2,1,0:T(8,128)(2,1)}, bf16[2,256,1024]{2,1,0:T(8,128)(2,1)S(1)}, u32[]{:S(2)}, u32[]{:S(2)}) collective-permute-start(bf16[2,256,1024]{2,1,0:T(8,128)(2,1)} %collective-permute-done.1.refs_2_), channel_id=1, source_target_pairs={{0,8},{8,0},{16,24},{24,16},{1,9},{9,1},{17,25},{25,17},{2,10},{10... | collective-permute-start | bytes 3145736 | tf_op jit(solution)/shard_map/ppermute | solution.py:16
  66.1 36.8 %collective-permute-start.23 = (bf16[1,2,256,256]{3,2,1,0:T(8,128)(2,1)}, bf16[1,2,256,256]{3,2,1,0:T(8,128)(2,1)S(1)}, u32[]{:S(2)}, u32[]{:S(2)}) collective-permute-start(bf16[1,2,256,256]{3,2,1,0:T(8,128)(2,1)} %get-tuple-element.23), channel_id=1, source_target_pairs={{0,1},{1,0},{2,3},{3,2},{4,5},{5,4},{6,7},{7,6},{8,9},{9,8},{10,11... | collective-permute-start | bytes 786440 | tf_op jit(solution)/shard_map/ppermute | solution.py:16
  72.6 32.3 %collective-permute-start.17 = (bf16[1,2,256,256]{3,2,1,0:T(8,128)(2,1)}, bf16[1,2,256,256]{3,2,1,0:T(8,128)(2,1)S(1)}, u32[]{:S(2)}, u32[]{:S(2)}) collective-permute-start(bf16[1,2,256,256]{3,2,1,0:T(8,128)(2,1)} %get-tuple-element.21), channel_id=1, source_target_pairs={{0,1},{1,0},{2,3},{3,2},{4,5},{5,4},{6,7},{7,6},{8,9},{9,8},{10,11... | collective-permute-start | bytes 786440 | tf_op jit(solution)/shard_map/ppermute | solution.py:16
  77.7 27.6 %collective-permute-start.11 = (bf16[1,2,256,256]{3,2,1,0:T(8,128)(2,1)}, bf16[1,2,256,256]{3,2,1,0:T(8,128)(2,1)S(1)}, u32[]{:S(2)}, u32[]{:S(2)}) collective-permute-start(bf16[1,2,256,256]{3,2,1,0:T(8,128)(2,1)} %get-tuple-element.19), channel_id=1, source_target_pairs={{0,1},{1,0},{2,3},{3,2},{4,5},{5,4},{6,7},{7,6},{8,9},{9,8},{10,11... | collective-permute-start | bytes 786440 | tf_op jit(solution)/shard_map/ppermute | solution.py:16
  87.7 41.3 %collective-permute-start.3 = (bf16[3,2,256,256]{3,2,1,0:T(8,128)(2,1)}, bf16[3,2,256,256]{3,2,1,0:T(8,128)(2,1)S(1)}, u32[]{:S(2)}, u32[]{:S(2)}) collective-permute-start(bf16[3,2,256,256]{3,2,1,0:T(8,128)(2,1)} %get-tuple-element.17), channel_id=1, source_target_pairs={{0,1},{1,0},{2,3},{3,2},{4,5},{5,4},{6,7},{7,6},{8,9},{9,8},{10,11... | collective-permute-start | bytes 2359304 | tf_op jit(solution)/shard_map/ppermute | solution.py:16
  104.9 7.9 %collective-permute-start.18 = (bf16[1,2,128,256]{3,2,1,0:T(8,128)(2,1)S(1)}, bf16[1,2,128,256]{3,2,1,0:T(8,128)(2,1)S(1)}, u32[]{:S(2)}, u32[]{:S(2)}) collective-permute-start(bf16[1,2,128,256]{3,2,1,0:T(8,128)(2,1)S(1)} %get-tuple-element.42), channel_id=1, source_target_pairs={{0,2},{1,3},{2,0},{3,1},{4,6},{5,7},{6,4},{7,5},{8,10},{9,11},{10,... | collective-permute-start | bytes 393224 | tf_op jit(solution)/shard_map/ppermute | solution.py:16
  106.3 9.4 %collective-permute-start.12 = (bf16[1,2,128,256]{3,2,1,0:T(8,128)(2,1)S(1)}, bf16[1,2,128,256]{3,2,1,0:T(8,128)(2,1)S(1)}, u32[]{:S(2)}, u32[]{:S(2)}) collective-permute-start(bf16[1,2,128,256]{3,2,1,0:T(8,128)(2,1)S(1)} %get-tuple-element.44), channel_id=1, source_target_pairs={{0,2},{1,3},{2,0},{3,1},{4,6},{5,7},{6,4},{7,5},{8,10},{9,11},{10,... | collective-permute-start | bytes 393224 | tf_op jit(solution)/shard_map/ppermute | solution.py:16
  109.4 8.4 %collective-permute-start.25 = (bf16[1,2,64,256]{3,2,1,0:T(8,128)(2,1)S(1)}, bf16[1,2,64,256]{3,2,1,0:T(8,128)(2,1)S(1)}, u32[]{:S(2)}, u32[]{:S(2)}) collective-permute-start(bf16[1,2,64,256]{3,2,1,0:T(8,128)(2,1)S(1)} %add_convert_fusion.6), channel_id=1, source_target_pairs={{0,4},{1,5},{2,6},{3,7},{4,0},{5,1},{6,2},{7,3},{8,12},{9,13},{10,... | collective-permute-start | bytes 196616 | tf_op jit(solution)/shard_map/ppermute | solution.py:16
  112.9 9.9 %collective-permute-start.19 = (bf16[1,2,64,256]{3,2,1,0:T(8,128)(2,1)S(1)}, bf16[1,2,64,256]{3,2,1,0:T(8,128)(2,1)S(1)}, u32[]{:S(2)}, u32[]{:S(2)}) collective-permute-start(bf16[1,2,64,256]{3,2,1,0:T(8,128)(2,1)S(1)} %add_convert_fusion.7), channel_id=1, source_target_pairs={{0,4},{1,5},{2,6},{3,7},{4,0},{5,1},{6,2},{7,3},{8,12},{9,13},{10,... | collective-permute-start | bytes 196616 | tf_op jit(solution)/shard_map/ppermute | solution.py:16
  115.8 9.1 %collective-permute-start.13 = (bf16[1,2,64,256]{3,2,1,0:T(8,128)(2,1)S(1)}, bf16[1,2,64,256]{3,2,1,0:T(8,128)(2,1)S(1)}, u32[]{:S(2)}, u32[]{:S(2)}) collective-permute-start(bf16[1,2,64,256]{3,2,1,0:T(8,128)(2,1)S(1)} %add_convert_fusion.8), channel_id=1, source_target_pairs={{0,4},{1,5},{2,6},{3,7},{4,0},{5,1},{6,2},{7,3},{8,12},{9,13},{10,... | collective-permute-start | bytes 196616 | tf_op jit(solution)/shard_map/ppermute | solution.py:16
  117.9 9.2 %collective-permute-start.26 = (bf16[1,2,64,256]{3,2,1,0:T(8,128)(2,1)S(1)}, bf16[1,2,64,256]{3,2,1,0:T(8,128)(2,1)S(1)}, u32[]{:S(2)}, u32[]{:S(2)}) collective-permute-start(bf16[1,2,64,256]{3,2,1,0:T(8,128)(2,1)S(1)} %select_convert_fusion.1), channel_id=1, source_target_pairs={{0,4},{1,5},{2,6},{3,7},{4,0},{5,1},{6,2},{7,3},{8,12},{9,13},{10,... | collective-permute-start | bytes 196616 | tf_op jit(solution)/shard_map/ppermute | solution.py:16
  127.1 17.2 %collective-permute-start.27 = (bf16[1,2,128,256]{3,2,1,0:T(8,128)(2,1)S(1)}, bf16[1,2,128,256]{3,2,1,0:T(8,128)(2,1)S(1)}, u32[]{:S(2)}, u32[]{:S(2)}) collective-permute-start(bf16[1,2,128,256]{3,2,1,0:T(8,128)(2,1)S(1)} %pad_maximum_fusion.12), channel_id=1, source_target_pairs={{0,2},{1,3},{2,0},{3,1},{4,6},{5,7},{6,4},{7,5},{8,10},{9,11},{10,... | collective-permute-start | bytes 393224 | tf_op jit(solution)/shard_map/ppermute | solution.py:16
  129.2 15.0 %collective-permute-start.4 = (bf16[3,2,128,256]{3,2,1,0:T(8,128)(2,1)S(1)}, bf16[3,2,128,256]{3,2,1,0:T(8,128)(2,1)S(1)}, u32[]{:S(2)}, u32[]{:S(2)}) collective-permute-start(bf16[3,2,128,256]{3,2,1,0:T(8,128)(2,1)S(1)} %get-tuple-element.32), channel_id=1, source_target_pairs={{0,2},{1,3},{2,0},{3,1},{4,6},{5,7},{6,4},{7,5},{8,10},{9,11},{10,... | collective-permute-start | bytes 1179656 | tf_op jit(solution)/shard_map/ppermute | solution.py:16
  129.5 27.3 %collective-permute-start.21 = (bf16[1,2,128,256]{3,2,1,0:T(8,128)(2,1)S(1)}, bf16[1,2,128,256]{3,2,1,0:T(8,128)(2,1)S(1)}, u32[]{:S(2)}, u32[]{:S(2)}) collective-permute-start(bf16[1,2,128,256]{3,2,1,0:T(8,128)(2,1)S(1)} %pad_maximum_fusion.11), channel_id=1, source_target_pairs={{0,2},{1,3},{2,0},{3,1},{4,6},{5,7},{6,4},{7,5},{8,10},{9,11},{10,... | collective-permute-start | bytes 393224 | tf_op jit(solution)/shard_map/ppermute | solution.py:16
  131.4 32.6 %collective-permute-start.15 = (bf16[1,2,128,256]{3,2,1,0:T(8,128)(2,1)S(1)}, bf16[1,2,128,256]{3,2,1,0:T(8,128)(2,1)S(1)}, u32[]{:S(2)}, u32[]{:S(2)}) collective-permute-start(bf16[1,2,128,256]{3,2,1,0:T(8,128)(2,1)S(1)} %pad_maximum_fusion.10), channel_id=1, source_target_pairs={{0,2},{1,3},{2,0},{3,1},{4,6},{5,7},{6,4},{7,5},{8,10},{9,11},{10,... | collective-permute-start | bytes 393224 | tf_op jit(solution)/shard_map/ppermute | solution.py:16
  144.2 12.4 %collective-permute-start.5 = (bf16[3,2,64,256]{3,2,1,0:T(8,128)(2,1)S(1)}, bf16[3,2,64,256]{3,2,1,0:T(8,128)(2,1)S(1)}, u32[]{:S(2)}, u32[]{:S(2)}) collective-permute-start(bf16[3,2,64,256]{3,2,1,0:T(8,128)(2,1)S(1)} %add_convert_fusion.2), channel_id=1, source_target_pairs={{0,4},{1,5},{2,6},{3,7},{4,0},{5,1},{6,2},{7,3},{8,12},{9,13},{10,... | collective-permute-start | bytes 589832 | tf_op jit(solution)/shard_map/ppermute | solution.py:16
  144.4 21.6 %collective-permute-start.28 = (bf16[1,2,256,256]{3,2,1,0:T(8,128)(2,1)S(1)}, bf16[1,2,256,256]{3,2,1,0:T(8,128)(2,1)S(1)}, u32[]{:S(2)}, u32[]{:S(2)}) collective-permute-start(bf16[1,2,256,256]{3,2,1,0:T(8,128)(2,1)S(1)} %pad_maximum_fusion.9), channel_id=1, source_target_pairs={{0,1},{1,0},{2,3},{3,2},{4,5},{5,4},{6,7},{7,6},{8,9},{9,8},{10,11... | collective-permute-start | bytes 786440 | tf_op jit(solution)/shard_map/ppermute | solution.py:16
  156.9 17.0 %collective-permute-start.22 = (bf16[1,2,256,256]{3,2,1,0:T(8,128)(2,1)S(1)}, bf16[1,2,256,256]{3,2,1,0:T(8,128)(2,1)S(1)}, u32[]{:S(2)}, u32[]{:S(2)}) collective-permute-start(bf16[1,2,256,256]{3,2,1,0:T(8,128)(2,1)S(1)} %pad_maximum_fusion.8), channel_id=1, source_target_pairs={{0,1},{1,0},{2,3},{3,2},{4,5},{5,4},{6,7},{7,6},{8,9},{9,8},{10,11... | collective-permute-start | bytes 786440 | tf_op jit(solution)/shard_map/ppermute | solution.py:16
  164.1 11.6 %collective-permute-start.16 = (bf16[1,2,256,256]{3,2,1,0:T(8,128)(2,1)S(1)}, bf16[1,2,256,256]{3,2,1,0:T(8,128)(2,1)S(1)}, u32[]{:S(2)}, u32[]{:S(2)}) collective-permute-start(bf16[1,2,256,256]{3,2,1,0:T(8,128)(2,1)S(1)} %pad_maximum_fusion.7), channel_id=1, source_target_pairs={{0,1},{1,0},{2,3},{3,2},{4,5},{5,4},{6,7},{7,6},{8,9},{9,8},{10,11... | collective-permute-start | bytes 786440 | tf_op jit(solution)/shard_map/ppermute | solution.py:16
  172.0 15.4 %collective-permute-start.8 = (bf16[3,2,256,256]{3,2,1,0:T(8,128)(2,1)S(1)}, bf16[3,2,256,256]{3,2,1,0:T(8,128)(2,1)S(1)}, u32[]{:S(2)}, u32[]{:S(2)}) collective-permute-start(bf16[3,2,256,256]{3,2,1,0:T(8,128)(2,1)S(1)} %pad_maximum_fusion.2), channel_id=1, source_target_pairs={{0,1},{1,0},{2,3},{3,2},{4,5},{5,4},{6,7},{7,6},{8,9},{9,8},{10,11... | collective-permute-start | bytes 2359304 | tf_op jit(solution)/shard_map/ppermute | solution.py:16
  (21 other events, 176.0 us)

commit v2 on v1

v2 whole, which is shorter than its diff:
```python
import functools

import jax
import jax.numpy as jnp
from jax import lax
from jax.experimental import pallas as pl
from jax.experimental.pallas import tpu as pltpu
from jax.sharding import PartitionSpec as P

SMALL_COST = pl.CostEstimate(flops=1, bytes_accessed=1, transcendentals=0)
VMEM_LIMIT = 24 * 1024 * 1024
LAG = 0.3
PACE = 0.6
PLAN = ((0, 1, True), (1, 1, True), (2, 1, True), (3, 1, True))


def swap(value, axis, bit):
    size = lax.axis_size(axis)
    return lax.ppermute(value, axis, [(i, i ^ bit) for i in range(size)])


def after(value, *others):
    return lax.optimization_barrier((value,) + others)[0]


def axis_bits(axis):
    size = lax.axis_size(axis)
    return [1 << b for b in range(size.bit_length() - 1)]


def overlap_kernel(count, picks_ref, half_ref, own_ref, field_ref, *refs):
    sources = refs[:count]
    send_ref, keep_ref, pick_ref, full, turned = refs[-5:]
    pick = picks_ref[pl.program_id(0)]
    for j in range(count):
        @pl.when(pick == j)
        def _():
            pick_ref[0] = sources[j][...]
    _, bands, points = own_ref.shape
    width = pick_ref.shape[2]
    rows = bands // 2
    u, v = field_ref[0, 0:1], field_ref[0, 1:2]
    p_real, p_imag = pick_ref[0, 0].astype(jnp.float32), pick_ref[0, 1].astype(jnp.float32)
    turned[:width] = (u * p_real + v * p_imag).astype(jnp.bfloat16)
    turned[width:] = (u * p_imag - v * p_real).astype(jnp.bfloat16)
    both = lax.dot_general(
        own_ref[...].reshape(2 * bands, points),
        turned[...],
        (((1,), (1,)), ((), ())),
        preferred_element_type=jnp.float32,
    )
    full[0] = both[:bands, :width] + both[bands:, width:]
    full[1] = both[bands:, :width] - both[:bands, width:]
    away = pl.multiple_of(half_ref[0] * rows, rows)
    here = pl.multiple_of((1 - half_ref[0]) * rows, rows)
    send_ref[0] = full[:, pl.ds(away, rows), :].astype(send_ref.dtype)
    keep_ref[0] = full[:, pl.ds(here, rows), :]


def overlap(q0, q_count, start, picks, half, own, potential, sources):
    _, bands, points = own.shape
    width = sources[-1][0].shape[1]
    rows = bands // 2
    chunk = start // width
    specs = []
    for array, is_whole in sources:
        row = chunk if is_whole else 0
        specs.append(pl.BlockSpec((2, width, points), lambda q, p, h, row=row: (0, row, 0), pipeline_mode=pl.Buffered(1)))
    arrays = [own, potential] + [array for array, _ in sources]
    return pl.pallas_call(
        functools.partial(overlap_kernel, len(sources)),
        grid_spec=pltpu.PrefetchScalarGridSpec(
            num_scalar_prefetch=2,
            grid=(q_count,),
            in_specs=[
                pl.BlockSpec((2, bands, points), lambda q, p, h: (0, 0, 0), pipeline_mode=pl.Buffered(1)),
                pl.BlockSpec((1, 2, points), lambda q, p, h: (q0 + q, 0, 0)),
            ]
            + specs,
            out_specs=[
                pl.BlockSpec((1, 2, rows, width), lambda q, p, h: (q, 0, 0, 0)),
                pl.BlockSpec((1, 2, rows, width), lambda q, p, h: (q, 0, 0, 0)),
                pl.BlockSpec((1, 2, width, points), lambda q, p, h: (q, 0, 0, 0)),
            ],
            scratch_shapes=[
                pltpu.VMEM((2, bands, width), jnp.float32),
                pltpu.VMEM((2 * width, points), jnp.bfloat16),
            ],
        ),
        out_shape=[
            jax.ShapeDtypeStruct((q_count, 2, rows, width), jnp.bfloat16),
            jax.ShapeDtypeStruct((q_count, 2, rows, width), jnp.float32),
            jax.ShapeDtypeStruct((q_count, 2, width, points), jnp.bfloat16),
        ],
        compiler_params=pltpu.CompilerParams(vmem_limit_bytes=VMEM_LIMIT),
        cost_estimate=SMALL_COST,
    )(picks, half, *arrays)


def mix_kernel(chunk_count, density_scale, count_ref, field_ref, own_ref, *refs):
    weights = refs[:chunk_count]
    partners = refs[chunk_count:2 * chunk_count]
    source_ref, density_ref, left_real, left_imag, right = refs[-5:]
    bands = own_ref.shape[1]

    @pl.when(pl.program_id(0) == 0)
    def _():
        start = 0
        for weight in weights:
            width = weight.shape[3]
            near, far = pl.ds(start, width), pl.ds(start + width, width)
            start += 2 * width
            left_real[:, near] = weight[0, 0]
            left_real[:, far] = -weight[0, 1]
            left_imag[:, near] = weight[0, 1]
            left_imag[:, far] = weight[0, 0]

    start = 0
    for partner in partners:
        width = 2 * partner.shape[2]
        right[pl.ds(start, width), :] = partner[0].reshape(width, partner.shape[3])
        start += width
    u, v = field_ref[0, 0:1], field_ref[0, 1:2]
    a, b = own_ref[0].astype(jnp.float32), own_ref[1].astype(jnp.float32)
    applied_real = (u * a - v * b).astype(jnp.bfloat16).astype(jnp.float32)
    applied_imag = (u * b + v * a).astype(jnp.bfloat16).astype(jnp.float32)
    real = applied_real - jnp.dot(left_real[...], right[...], preferred_element_type=jnp.float32)
    imag = applied_imag - jnp.dot(left_imag[...], right[...], preferred_element_type=jnp.float32)
    source_ref[0, 0, 0] = real.astype(jnp.bfloat16)
    source_ref[0, 0, 1] = imag.astype(jnp.bfloat16)
    term = a * real + b * imag
    ids = lax.broadcasted_iota(jnp.int32, (bands, 1), 0)
    term = jnp.where(ids < count_ref[0], term, 0.0)
    density_ref[...] = density_scale * jnp.sum(term, axis=0, keepdims=True)


def mix(q, count, potential, orbitals, partners, weights, buffer, density_scale):
    q_total = potential.shape[0]
    _, bands, points = orbitals.shape
    block = points // 4
    specs = [
        pl.BlockSpec((1, 2, block), lambda i, c: (q, 0, i)),
        pl.BlockSpec((2, bands, block), lambda i, c: (0, 0, i)),
    ]
    arrays = [potential, orbitals]
    for at, weight in weights:
        specs.append(pl.BlockSpec((1, 2, bands, weight.shape[3]), lambda i, c, at=at: (at, 0, 0, 0)))
        arrays.append(weight)
    for at, partner in partners:
        specs.append(pl.BlockSpec((1, 2, partner.shape[2], block), lambda i, c, at=at: (at, 0, 0, i)))
        arrays.append(partner)
    aliases = {}
    if buffer is not None:
        specs.append(pl.BlockSpec(memory_space=pl.ANY))
        arrays.append(buffer)
        aliases = {len(arrays): 0}
    return pl.pallas_call(
        functools.partial(mix_kernel, len(weights), density_scale),
        grid_spec=pltpu.PrefetchScalarGridSpec(
            num_scalar_prefetch=1,
            grid=(points // block,),
            in_specs=specs,
            out_specs=[
                pl.BlockSpec((1, 1, 2, bands, block), lambda i, c: (q, 0, 0, 0, i)),
                pl.BlockSpec((1, block), lambda i, c: (0, i)),
            ],
            scratch_shapes=[pltpu.VMEM((bands, 2 * bands), jnp.bfloat16)] * 2
            + [pltpu.VMEM((2 * bands, block), jnp.bfloat16)],
        ),
        out_shape=[
            jax.ShapeDtypeStruct((q_total, 1, 2, bands, points), jnp.bfloat16),
            jax.ShapeDtypeStruct((1, points), jnp.float32),
        ],
        input_output_aliases=aliases,
        compiler_params=pltpu.CompilerParams(vmem_limit_bytes=VMEM_LIMIT),
        cost_estimate=SMALL_COST,
    )(count, *arrays)


def shards(orbitals, potential, partners, occupied):
    own = orbitals[0]
    bands, points = own.shape[1:]
    q_count = potential.shape[0]
    k_count = partners.shape[1]
    k_index = lax.axis_index("ka")
    g_index = lax.axis_index("grid")
    ka_bits = axis_bits("ka")[::-1]
    grid_bits = axis_bits("grid")
    volume_weight = 1.0 / (points * lax.axis_size("grid"))
    density_weight = 2.0 / (k_count * bands)
    k_table = jnp.arange(k_count, dtype=jnp.int32)
    partner_ids = jnp.sum((k_table == k_index) * partners, axis=1)
    partner_counts = jnp.sum((partner_ids[:, None] == k_table[None, :]) * occupied[None, :], axis=1)
    own_count = jnp.sum((k_table == k_index) * occupied)[None]
    picks = partner_ids ^ k_index
    last_bit = ka_bits[-1]

    fetched = []
    spans = [(first * bands // 4, count * bands // 4) for first, count, _ in PLAN]
    for start, width in spans:
        have = {0: own[:, start:start + width]}
        for bit in ka_bits[:-1]:
            for rel in list(have):
                have[rel ^ bit] = swap(have[rel], "ka", bit)
        fetched.append(have)
    sibling = swap(own, "ka", last_bit)

    def bit_of(bit):
        return (g_index // bit) % 2

    away_half = (1 - bit_of(grid_bits[0]))[None].astype(jnp.int32)

    groups = []
    for c, (_, _, together) in enumerate(PLAN):
        groups += [(c, 0, q_count)] if together else [(c, q, 1) for q in range(q_count)]
    state = {}
    picked = {}
    previous = own_count

    def run_overlap(i):
        nonlocal previous
        c, q0, count = groups[i]
        have = fetched[c]
        if q0 == 0:
            for rel in list(have):
                if rel:
                    have[rel ^ last_bit] = swap(after(have[rel], previous), "ka", last_bit)
            have[last_bit] = None
        sources = []
        for rel in range(len(have)):
            whole = {0: own, last_bit: sibling}.get(rel)
            sources.append((have[rel], False) if whole is None else (whole, True))
        leaving, keep, picked[i] = overlap(
            q0, count, spans[c][0], picks[q0:q0 + count], away_half, own, after(potential, previous), sources
        )
        previous = leaving
        state[i] = (keep, swap(leaving, "grid", grid_bits[0]))

    def run_scatter(i, bit, full):
        nonlocal previous
        keep, arriving = state[i]
        arriving = after(arriving, previous)
        mine = bit_of(bit)
        half = keep.shape[2] // 2

        def part(which):
            return lax.dynamic_slice_in_dim(keep, which * half, half, 2) + lax.dynamic_slice_in_dim(
                arriving, which * half, half, 2
            ).astype(jnp.float32)

        if full:
            leaving = (keep + arriving.astype(jnp.float32)).astype(jnp.bfloat16)
            kept = leaving
        else:
            leaving = part(1 - mine).astype(jnp.bfloat16)
            kept = part(mine)
        previous = leaving
        state[i] = (kept, swap(leaving, "grid", bit))

    def run_turn(i, bit):
        nonlocal previous
        c, q0, count = groups[i]
        start, width = spans[c]
        keep, arriving = state[i]
        total = keep.astype(jnp.float32) + after(arriving, previous).astype(jnp.float32)
        limits = partner_counts[q0:q0 + count][:, None, None, None]
        mask = (start + jnp.arange(width, dtype=jnp.int32)) < limits
        piece = jnp.where(mask, volume_weight * total, 0.0).astype(jnp.bfloat16)
        previous = piece
        state[i] = (piece, swap(piece, "grid", bit))

    def run_gather(i, done_bit, bit):
        nonlocal previous
        piece, other = state[i]
        upper = bit_of(done_bit) == 1
        other = after(other, previous) if bit is not None else other
        piece = jnp.concatenate([jnp.where(upper, other, piece), jnp.where(upper, piece, other)], axis=2)
        if bit is None:
            state[i] = piece
            return
        previous = piece
        state[i] = (piece, swap(piece, "grid", bit))

    stages = []
    steps = len(grid_bits)
    for i, (c, q0, count) in enumerate(groups):
        first, quarters, _ = PLAN[c]
        at = PACE * (first + quarters) + 0.2 * q0
        scale = quarters * count / q_count
        stages.append((at, i, functools.partial(run_overlap, i)))
        at += 0.85 * scale + LAG
        for s in range(1, steps):
            stages.append((at, i, functools.partial(run_scatter, i, grid_bits[s], s == steps - 1)))
            at += (0.4 if s < steps - 1 else 0.8) * scale + LAG
        stages.append((at, i, functools.partial(run_turn, i, grid_bits[steps - 2])))
        at += 0.4 * scale + LAG
        for s in range(steps - 2, 0, -1):
            stages.append((at, i, functools.partial(run_gather, i, grid_bits[s], grid_bits[s - 1])))
            at += 0.85 * scale + LAG
        stages.append((at, i, functools.partial(run_gather, i, grid_bits[0], None)))
    for _, _, stage in sorted(stages, key=lambda entry: entry[:2]):
        stage()

    buffer = None
    density = []
    for q in range(q_count):
        own_groups = [i for i, (_, q0, n) in enumerate(groups) if q0 <= q < q0 + n]
        weights = [(q - groups[i][1], state[i]) for i in own_groups]
        chosen = [(q - groups[i][1], picked[i]) for i in own_groups]
        buffer, term = mix(q, own_count, potential, own, chosen, weights, buffer, density_weight)
        density.append(term)
    density = jnp.concatenate(density, axis=0)
    parts = [density] + [swap(density, "ka", d) for d in range(1, lax.axis_size("ka"))]
    while len(parts) > 1:
        half = len(parts) // 2
        parts = [parts[i] + parts[i + half] for i in range(half)]
    return buffer, parts[0]


def solution(mesh):
    return jax.shard_map(
        shards,
        mesh=mesh,
        in_specs=(P("ka", None, None, "grid"), P(None, None, "grid"), P(), P()),
        out_specs=(P(None, "ka", None, None, "grid"), P(None, "grid")),
        check_vma=False,
    )
```

time: 221 us -> 163 us (0.74)
  waiting for transfers between devices: 98.7 us -> 72.4 us
  Pallas kernels: 59.7 us -> 37 us
  other arithmetic: 20.6 us -> 8.04 us
  starting transfers between devices: 33.5 us -> 36.2 us
    ppermute x32, waiting for transfers between devices: 98.7 us -> 72.4 us  [swap(): return lax.ppermute(value, axis, [(i, i ^ bit) for i in range(size)])]
    pallas_call x11 -> x7, Pallas kernels: 59.7 us -> 37 us  [the longest x4 19.1 us: overlap(): pl.pallas_call(functools.partial(overlap_kernel, len(sources)), grid_spec...]
    another operation x2 -> x0, other arithmetic: 6.47 us -> none
    concatenate x12 -> x8, other arithmetic: 3.89 us -> 0.32 us  [run_gather(): jnp.concatenate([jnp.where(upper, other, piece), jnp.where(upper, piece,...]
    unnamed x27 -> x26, local copies, waits for them, and re-layouts: 1.99 us -> 5.03 us
    ppermute x32, starting transfers between devices: 33.5 us -> 36.2 us  [swap(): return lax.ppermute(value, axis, [(i, i ^ bit) for i in range(size)])]
    slice x4 -> x1, local copies, waits for them, and re-layouts: 4.42 us -> 2.86 us  [shards(): have = {0: own[:, start:start + width]}]
    convert_element_type x13 -> x12, other arithmetic: 4.25 us -> 5.23 us  [the longest x4 2.73 us: run_scatter(): leaving = part(1 - mine).astype(jnp.bfloat16)]
  transfers between devices with their start and end apart: 32 -> 32, of which waited for: 16 -> 18; matrix products, arithmetic and copies ran while one was open for 10% -> 6% of each run, Pallas kernels for 17% -> 12%
where the time goes in v2:
time: 163 us
  waiting for transfers between devices  72.4 us (44%)
  Pallas kernels  37 us (23%)
  starting transfers between devices  36.2 us (22%)
  other arithmetic  8.04 us (5%)
  local copies, waits for them, and re-layouts  7.89 us (5%)
    ppermute x32, waiting for transfers between devices, swap(): return lax.ppermute(value, axis, [(i, i ^ bit) for i in range(size)])  72.4 us
    ppermute x32, starting transfers between devices, swap(): return lax.ppermute(value, axis, [(i, i ^ bit) for i in range(size)])  36.2 us
    pallas_call x4, Pallas kernels, overlap(): pl.pallas_call(functools.partial(overlap_kernel, len(sources)), grid_spec...  19.1 us
    pallas_call x3, Pallas kernels, mix(): pl.pallas_call(functools.partial(mix_kernel, len(weights), density_scale)...  17.9 us
    unnamed x26, local copies, waits for them, and re-layouts  5.03 us
  transfers between devices with their start and end apart: 32, of which 18 were waited for; matrix products, arithmetic and copies ran while one was open for 6% of the time, Pallas kernels for 12%

profile of v2, /device:TPU:0, one launch (start us, length us, event | category | flops | bytes accessed | tf_op | source)
XLA Modules:
  0.0 162.6 jit_solution(1440988405553387781)
XLA Ops:
  1.2 2.9 %fusion.1 = (bf16[2,128,1024]{2,1,0:T(8,128)(2,1)}, bf16[2,128,1024]{2,1,0:T(8,128)(2,1)}, bf16[2,128,1024]{2,1,0:T(8,128)(2,1)}, bf16[2,128,1024]{2,1,0:T(8,128)(2,1)S(1)}) fusion(bf16[2,512,1024]{2,1,0:T(8,128)(2,1)} %bitcast.4), kind=kLoop, calls=%fused_computation.52 | loop fusion | bytes 4194304 | tf_op jit(solution)/shard_map/slice | solution.py:201
  4.1 2.5 %collective-permute-start.1 = (bf16[2,128,1024]{2,1,0:T(8,128)(2,1)S(1)}, bf16[2,128,1024]{2,1,0:T(8,128)(2,1)S(1)}, u32[]{:S(2)}, u32[]{:S(2)}) collective-permute-start(bf16[2,128,1024]{2,1,0:T(8,128)(2,1)S(1)} %get-tuple-element.89), channel_id=1, source_target_pairs={{0,16},{8,24},{16,0},{24,8},{1,17},{9,25},{17,1},{25,9},{2,18},{10... | collective-permute-start | bytes 1572872 | tf_op jit(solution)/shard_map/ppermute | solution.py:19
  7.2 11.8 %collective-permute-done.1.refs_2_ = bf16[2,128,1024]{2,1,0:T(8,128)(2,1)S(1)} collective-permute-done((bf16[2,128,1024]{2,1,0:T(8,128)(2,1)S(1)}, bf16[2,128,1024]{2,1,0:T(8,128)(2,1)S(1)}, u32[]{:S(2)}, u32[]{:S(2)}) %collective-permute-start.1) | collective-permute-done | bytes 524320 | tf_op jit(solution)/shard_map/ppermute | solution.py:19
  22.8 5.1 %shard_map.59 = (bf16[3,2,256,128]{3,2,1,0:T(8,128)(2,1)}, f32[3,2,256,128]{3,2,1,0:T(8,128)S(1)}, bf16[3,2,128,1024]{3,2,1,0:T(8,128)(2,1)S(1)}) custom-call(s32[3]{0:T(128)S(1)} %broadcast_xor_fusion.picks_ref, s32[1]{0:T(128)} %bitcast.2.half_ref, bf16[2,512,1024]{2,1,0:T(8,128)(2,1)S(1)} %bitcast.5, f32[3,2,1024]{2,1,0:T(2,128)S(1)} %copy-done.5, ...), custom_call_target="tpu_custom_call" | custom-call | flops 1 | bytes 1 | tf_op jit(solution)/shard_map/pallas_call | solution.py:70
  29.0 5.3 %collective-permute-done.4.refs_2_ = bf16[2,128,1024]{2,1,0:T(8,128)(2,1)S(1)} collective-permute-done((bf16[2,128,1024]{2,1,0:T(8,128)(2,1)}, bf16[2,128,1024]{2,1,0:T(8,128)(2,1)S(1)}, u32[]{:S(2)}, u32[]{:S(2)}) %collective-permute-start.4) | collective-permute-done | bytes 524320 | tf_op jit(solution)/shard_map/ppermute | solution.py:19
  37.6 5.1 %shard_map.60 = (bf16[3,2,256,128]{3,2,1,0:T(8,128)(2,1)}, f32[3,2,256,128]{3,2,1,0:T(8,128)S(1)}, bf16[3,2,128,1024]{3,2,1,0:T(8,128)(2,1)S(1)}) custom-call(s32[3]{0:T(128)S(1)} %broadcast_xor_fusion.picks_ref, s32[1]{0:T(128)} %bitcast.2.half_ref, bf16[2,512,1024]{2,1,0:T(8,128)(2,1)S(1)} %bitcast.7, f32[3,2,1024]{2,1,0:T(2,128)S(1)} %copy-done.5, ...), custom_call_target="tpu_custom_call" | custom-call | flops 1 | bytes 1 | tf_op jit(solution)/shard_map/pallas_call | solution.py:70
  44.8 2.9 %collective-permute-done.3 = bf16[3,2,256,128]{3,2,1,0:T(8,128)(2,1)} collective-permute-done((bf16[3,2,256,128]{3,2,1,0:T(8,128)(2,1)}, bf16[3,2,256,128]{3,2,1,0:T(8,128)(2,1)}, u32[]{:S(2)}, u32[]{:S(2)}) %collective-permute-start.3) | collective-permute-done | bytes 393248 | tf_op jit(solution)/shard_map/ppermute | solution.py:19
  52.3 4.6 %shard_map.61 = (bf16[3,2,256,128]{3,2,1,0:T(8,128)(2,1)S(1)}, f32[3,2,256,128]{3,2,1,0:T(8,128)S(1)}, bf16[3,2,128,1024]{3,2,1,0:T(8,128)(2,1)S(1)}) custom-call(s32[3]{0:T(128)S(1)} %broadcast_xor_fusion.picks_ref, s32[1]{0:T(128)} %bitcast.2.half_ref, bf16[2,512,1024]{2,1,0:T(8,128)(2,1)S(1)} %bitcast.9, f32[3,2,1024]{2,1,0:T(2,128)S(1)} %copy-done.5, ...), custom_call_target="tpu_custom_call" | custom-call | flops 1 | bytes 1 | tf_op jit(solution)/shard_map/pallas_call | solution.py:70
  56.9 5.4 %collective-permute-done.7 = bf16[3,2,256,128]{3,2,1,0:T(8,128)(2,1)} collective-permute-done((bf16[3,2,256,128]{3,2,1,0:T(8,128)(2,1)}, bf16[3,2,256,128]{3,2,1,0:T(8,128)(2,1)}, u32[]{:S(2)}, u32[]{:S(2)}) %collective-permute-start.7) | collective-permute-done | bytes 393248 | tf_op jit(solution)/shard_map/ppermute | solution.py:19
  67.8 4.3 %shard_map.62 = (bf16[3,2,256,128]{3,2,1,0:T(8,128)(2,1)S(1)}, f32[3,2,256,128]{3,2,1,0:T(8,128)S(1)}, bf16[3,2,128,1024]{3,2,1,0:T(8,128)(2,1)S(1)}) custom-call(s32[3]{0:T(128)S(1)} %broadcast_xor_fusion.picks_ref, s32[1]{0:T(128)} %bitcast.2.half_ref, bf16[2,512,1024]{2,1,0:T(8,128)(2,1)S(1)} %bitcast.11, f32[3,2,1024]{2,1,0:T(2,128)S(1)} %copy-done.5, ...), custom_call_target="tpu_custom_call" | custom-call | flops 1 | bytes 1 | tf_op jit(solution)/shard_map/pallas_call | solution.py:70
  73.6 2.7 %collective-permute-start.12 = (bf16[3,2,128,128]{3,2,1,0:T(8,128)(2,1)S(1)}, bf16[3,2,128,128]{3,2,1,0:T(8,128)(2,1)S(1)}, u32[]{:S(2)}, u32[]{:S(2)}) collective-permute-start(bf16[3,2,128,128]{3,2,1,0:T(8,128)(2,1)S(1)} %add_convert_fusion.5), channel_id=1, source_target_pairs={{0,4},{1,5},{2,6},{3,7},{4,0},{5,1},{6,2},{7,3},{8,12},{9,13},{10,... | collective-permute-start | bytes 589832 | tf_op jit(solution)/shard_map/ppermute | solution.py:19
  79.2 2.7 %collective-permute-start.17 = (bf16[3,2,128,128]{3,2,1,0:T(8,128)(2,1)S(1)}, bf16[3,2,128,128]{3,2,1,0:T(8,128)(2,1)S(1)}, u32[]{:S(2)}, u32[]{:S(2)}) collective-permute-start(bf16[3,2,128,128]{3,2,1,0:T(8,128)(2,1)S(1)} %add_convert_fusion.3), channel_id=1, source_target_pairs={{0,4},{1,5},{2,6},{3,7},{4,0},{5,1},{6,2},{7,3},{8,12},{9,13},{10,... | collective-permute-start | bytes 589832 | tf_op jit(solution)/shard_map/ppermute | solution.py:19
  81.9 3.5 %collective-permute-done.13 = bf16[3,2,256,128]{3,2,1,0:T(8,128)(2,1)S(1)} collective-permute-done((bf16[3,2,256,128]{3,2,1,0:T(8,128)(2,1)S(1)}, bf16[3,2,256,128]{3,2,1,0:T(8,128)(2,1)S(1)}, u32[]{:S(2)}, u32[]{:S(2)}) %collective-permute-start.13) | collective-permute-done | bytes 393248 | tf_op jit(solution)/shard_map/ppermute | solution.py:19
  86.0 3.9 %collective-permute-done.12 = bf16[3,2,128,128]{3,2,1,0:T(8,128)(2,1)S(1)} collective-permute-done((bf16[3,2,128,128]{3,2,1,0:T(8,128)(2,1)S(1)}, bf16[3,2,128,128]{3,2,1,0:T(8,128)(2,1)S(1)}, u32[]{:S(2)}, u32[]{:S(2)}) %collective-permute-start.12) | collective-permute-done | bytes 196640 | tf_op jit(solution)/shard_map/ppermute | solution.py:19
  91.1 3.7 %collective-permute-done.17 = bf16[3,2,128,128]{3,2,1,0:T(8,128)(2,1)S(1)} collective-permute-done((bf16[3,2,128,128]{3,2,1,0:T(8,128)(2,1)S(1)}, bf16[3,2,128,128]{3,2,1,0:T(8,128)(2,1)S(1)}, u32[]{:S(2)}, u32[]{:S(2)}) %collective-permute-start.17) | collective-permute-done | bytes 196640 | tf_op jit(solution)/shard_map/ppermute | solution.py:19
  95.0 9.7 %collective-permute-done.16 = bf16[3,2,128,128]{3,2,1,0:T(8,128)(2,1)S(1)} collective-permute-done((bf16[3,2,128,128]{3,2,1,0:T(8,128)(2,1)S(1)}, bf16[3,2,128,128]{3,2,1,0:T(8,128)(2,1)S(1)}, u32[]{:S(2)}, u32[]{:S(2)}) %collective-permute-start.16) | collective-permute-done | bytes 196640 | tf_op jit(solution)/shard_map/ppermute | solution.py:19
  108.2 2.5 %collective-permute-start.24 = (bf16[3,2,128,128]{3,2,1,0:T(8,128)(2,1)S(1)}, bf16[3,2,128,128]{3,2,1,0:T(8,128)(2,1)S(1)}, u32[]{:S(2)}, u32[]{:S(2)}) collective-permute-start(bf16[3,2,128,128]{3,2,1,0:T(8,128)(2,1)S(1)} %select_convert_fusion.1), channel_id=1, source_target_pairs={{0,2},{1,3},{2,0},{3,1},{4,6},{5,7},{6,4},{7,5},{8,10},{9,11},{10,... | collective-permute-start | bytes 589832 | tf_op jit(solution)/shard_map/ppermute | solution.py:19
  110.8 2.7 %collective-permute-start.23 = (bf16[3,2,256,128]{3,2,1,0:T(8,128)(2,1)S(1)}, bf16[3,2,256,128]{3,2,1,0:T(8,128)(2,1)S(1)}, u32[]{:S(2)}, u32[]{:S(2)}) collective-permute-start(bf16[3,2,256,128]{3,2,1,0:T(8,128)(2,1)S(1)} %pad_maximum_fusion.5), channel_id=1, source_target_pairs={{0,1},{1,0},{2,3},{3,2},{4,5},{5,4},{6,7},{7,6},{8,9},{9,8},{10,11... | collective-permute-start | bytes 1179656 | tf_op jit(solution)/shard_map/ppermute | solution.py:19
  118.9 2.5 %collective-permute-done.27 = bf16[3,2,128,128]{3,2,1,0:T(8,128)(2,1)S(1)} collective-permute-done((bf16[3,2,128,128]{3,2,1,0:T(8,128)(2,1)S(1)}, bf16[3,2,128,128]{3,2,1,0:T(8,128)(2,1)S(1)}, u32[]{:S(2)}, u32[]{:S(2)}) %collective-permute-start.27) | collective-permute-done | bytes 196640 | tf_op jit(solution)/shard_map/ppermute | solution.py:19
  125.0 7.9 %collective-permute-done.26 = bf16[3,2,256,128]{3,2,1,0:T(8,128)(2,1)S(1)} collective-permute-done((bf16[3,2,256,128]{3,2,1,0:T(8,128)(2,1)S(1)}, bf16[3,2,256,128]{3,2,1,0:T(8,128)(2,1)S(1)}, u32[]{:S(2)}, u32[]{:S(2)}) %collective-permute-start.26) | collective-permute-done | bytes 393248 | tf_op jit(solution)/shard_map/ppermute | solution.py:19
  133.2 5.2 %collective-permute-done.28 = bf16[3,2,256,128]{3,2,1,0:T(8,128)(2,1)S(1)} collective-permute-done((bf16[3,2,256,128]{3,2,1,0:T(8,128)(2,1)S(1)}, bf16[3,2,256,128]{3,2,1,0:T(8,128)(2,1)S(1)}, u32[]{:S(2)}, u32[]{:S(2)}) %collective-permute-start.28) | collective-permute-done | bytes 393248 | tf_op jit(solution)/shard_map/ppermute | solution.py:19
  138.7 6.0 %shard_map.63 = (bf16[3,1,2,512,1024]{4,3,2,1,0:T(8,128)(2,1)}, f32[1,1024]{1,0:T(1,128)S(1)}) custom-call(s32[1]{0:T(128)} %bitcast.count_ref, f32[3,2,1024]{2,1,0:T(2,128)S(1)} %copy-done.5, bf16[2,512,1024]{2,1,0:T(8,128)(2,1)S(1)} %bitcast.13, bf16[3,2,512,128]{3,2,1,0:T(8,128)(2,1)S(1)} %pad_maximum_fusion.refs_0_, ...), custom_call_target="tpu_custom_call" | custom-call | flops 1 | bytes 1 | tf_op jit(solution)/shard_map/pallas_call | solution.py:157
  144.6 6.0 %shard_map.64 = (bf16[3,1,2,512,1024]{4,3,2,1,0:T(8,128)(2,1)}, f32[1,1024]{1,0:T(1,128)S(1)}) custom-call(s32[1]{0:T(128)} %bitcast.count_ref, f32[3,2,1024]{2,1,0:T(2,128)S(1)} %copy-done.5, bf16[2,512,1024]{2,1,0:T(8,128)(2,1)S(1)} %bitcast.14, bf16[3,2,512,128]{3,2,1,0:T(8,128)(2,1)S(1)} %pad_maximum_fusion.refs_0_, ...), custom_call_target="tpu_custom_call", output_to_operand_aliasing={{0}: (11, {})} | custom-call | flops 1 | bytes 1 | tf_op jit(solution)/shard_map/pallas_call | solution.py:157
  150.6 6.0 %shard_map.65 = (bf16[3,1,2,512,1024]{4,3,2,1,0:T(8,128)(2,1)}, f32[1,1024]{1,0:T(1,128)S(1)}) custom-call(s32[1]{0:T(128)} %bitcast.count_ref, f32[3,2,1024]{2,1,0:T(2,128)S(1)} %copy-done.5, bf16[2,512,1024]{2,1,0:T(8,128)(2,1)S(1)} %bitcast.15, bf16[3,2,512,128]{3,2,1,0:T(8,128)(2,1)S(1)} %pad_maximum_fusion.refs_0_, ...), custom_call_target="tpu_custom_call", output_to_operand_aliasing={{0}: (11, {})} | custom-call | flops 1 | bytes 1 | tf_op jit(solution)/shard_map/pallas_call | solution.py:157
  (112 shorter events, 46.6 us)
Async XLA Ops:
  0.7 21.0 %collective-permute-start = (bf16[2,512,1024]{2,1,0:T(8,128)(2,1)}, bf16[2,512,1024]{2,1,0:T(8,128)(2,1)}, u32[]{:S(2)}, u32[]{:S(2)}) collective-permute-start(bf16[2,512,1024]{2,1,0:T(8,128)(2,1)} %bitcast.3), channel_id=1, source_target_pairs={{0,8},{8,0},{16,24},{24,16},{1,9},{9,1},{17,25},{25,17},{2,10},{10... | collective-permute-start | bytes 6291464 | tf_op jit(solution)/shard_map/ppermute | solution.py:19
  4.1 15.0 %collective-permute-start.1 = (bf16[2,128,1024]{2,1,0:T(8,128)(2,1)S(1)}, bf16[2,128,1024]{2,1,0:T(8,128)(2,1)S(1)}, u32[]{:S(2)}, u32[]{:S(2)}) collective-permute-start(bf16[2,128,1024]{2,1,0:T(8,128)(2,1)S(1)} %get-tuple-element.89), channel_id=1, source_target_pairs={{0,16},{8,24},{16,0},{24,8},{1,17},{9,25},{17,1},{25,9},{2,18},{10... | collective-permute-start | bytes 1572872 | tf_op jit(solution)/shard_map/ppermute | solution.py:19
  19.8 14.5 %collective-permute-start.4 = (bf16[2,128,1024]{2,1,0:T(8,128)(2,1)}, bf16[2,128,1024]{2,1,0:T(8,128)(2,1)S(1)}, u32[]{:S(2)}, u32[]{:S(2)}) collective-permute-start(bf16[2,128,1024]{2,1,0:T(8,128)(2,1)} %get-tuple-element.88), channel_id=1, source_target_pairs={{0,16},{8,24},{16,0},{24,8},{1,17},{9,25},{17,1},{25,9},{2,18},{10... | collective-permute-start | bytes 1572872 | tf_op jit(solution)/shard_map/ppermute | solution.py:19
  34.4 15.0 %collective-permute-start.8 = (bf16[2,128,1024]{2,1,0:T(8,128)(2,1)}, bf16[2,128,1024]{2,1,0:T(8,128)(2,1)}, u32[]{:S(2)}, u32[]{:S(2)}) collective-permute-start(bf16[2,128,1024]{2,1,0:T(8,128)(2,1)} %get-tuple-element.87), channel_id=1, source_target_pairs={{0,16},{8,24},{16,0},{24,8},{1,17},{9,25},{17,1},{25,9},{2,18},{10... | collective-permute-start | bytes 1572872 | tf_op jit(solution)/shard_map/ppermute | solution.py:19
  36.1 11.6 %collective-permute-start.3 = (bf16[3,2,256,128]{3,2,1,0:T(8,128)(2,1)}, bf16[3,2,256,128]{3,2,1,0:T(8,128)(2,1)}, u32[]{:S(2)}, u32[]{:S(2)}) collective-permute-start(bf16[3,2,256,128]{3,2,1,0:T(8,128)(2,1)} %get-tuple-element.47), channel_id=1, source_target_pairs={{0,1},{1,0},{2,3},{3,2},{4,5},{5,4},{6,7},{7,6},{8,9},{9,8},{10,11... | collective-permute-start | bytes 1179656 | tf_op jit(solution)/shard_map/ppermute | solution.py:19
  49.3 14.5 %collective-permute-start.10 = (bf16[2,128,1024]{2,1,0:T(8,128)(2,1)}, bf16[2,128,1024]{2,1,0:T(8,128)(2,1)S(1)}, u32[]{:S(2)}, u32[]{:S(2)}) collective-permute-start(bf16[2,128,1024]{2,1,0:T(8,128)(2,1)} %get-tuple-element.86), channel_id=1, source_target_pairs={{0,16},{8,24},{16,0},{24,8},{1,17},{9,25},{17,1},{25,9},{2,18},{10... | collective-permute-start | bytes 1572872 | tf_op jit(solution)/shard_map/ppermute | solution.py:19
  50.8 11.6 %collective-permute-start.7 = (bf16[3,2,256,128]{3,2,1,0:T(8,128)(2,1)}, bf16[3,2,256,128]{3,2,1,0:T(8,128)(2,1)}, u32[]{:S(2)}, u32[]{:S(2)}) collective-permute-start(bf16[3,2,256,128]{3,2,1,0:T(8,128)(2,1)} %get-tuple-element.50), channel_id=1, source_target_pairs={{0,1},{1,0},{2,3},{3,2},{4,5},{5,4},{6,7},{7,6},{8,9},{9,8},{10,11... | collective-permute-start | bytes 1179656 | tf_op jit(solution)/shard_map/ppermute | solution.py:19
  64.1 8.6 %collective-permute-start.6 = (bf16[3,2,128,128]{3,2,1,0:T(8,128)(2,1)S(1)}, bf16[3,2,128,128]{3,2,1,0:T(8,128)(2,1)S(1)}, u32[]{:S(2)}, u32[]{:S(2)}) collective-permute-start(bf16[3,2,128,128]{3,2,1,0:T(8,128)(2,1)S(1)} %copy-done.10), channel_id=1, source_target_pairs={{0,2},{1,3},{2,0},{3,1},{4,6},{5,7},{6,4},{7,5},{8,10},{9,11},{10,... | collective-permute-start | bytes 589832 | tf_op jit(solution)/shard_map/ppermute | solution.py:19
  65.7 11.9 %collective-permute-start.15 = (bf16[3,2,256,128]{3,2,1,0:T(8,128)(2,1)S(1)}, bf16[3,2,256,128]{3,2,1,0:T(8,128)(2,1)S(1)}, u32[]{:S(2)}, u32[]{:S(2)}) collective-permute-start(bf16[3,2,256,128]{3,2,1,0:T(8,128)(2,1)S(1)} %get-tuple-element.55), channel_id=1, source_target_pairs={{0,1},{1,0},{2,3},{3,2},{4,5},{5,4},{6,7},{7,6},{8,9},{9,8},{10,11... | collective-permute-start | bytes 1179656 | tf_op jit(solution)/shard_map/ppermute | solution.py:19
  67.3 10.9 %collective-permute-start.14 = (bf16[3,2,128,128]{3,2,1,0:T(8,128)(2,1)S(1)}, bf16[3,2,128,128]{3,2,1,0:T(8,128)(2,1)S(1)}, u32[]{:S(2)}, u32[]{:S(2)}) collective-permute-start(bf16[3,2,128,128]{3,2,1,0:T(8,128)(2,1)S(1)} %add_convert_fusion.6), channel_id=1, source_target_pairs={{0,2},{1,3},{2,0},{3,1},{4,6},{5,7},{6,4},{7,5},{8,10},{9,11},{10,... | collective-permute-start | bytes 589832 | tf_op jit(solution)/shard_map/ppermute | solution.py:19
  72.1 13.3 %collective-permute-start.13 = (bf16[3,2,256,128]{3,2,1,0:T(8,128)(2,1)S(1)}, bf16[3,2,256,128]{3,2,1,0:T(8,128)(2,1)S(1)}, u32[]{:S(2)}, u32[]{:S(2)}) collective-permute-start(bf16[3,2,256,128]{3,2,1,0:T(8,128)(2,1)S(1)} %get-tuple-element.59), channel_id=1, source_target_pairs={{0,1},{1,0},{2,3},{3,2},{4,5},{5,4},{6,7},{7,6},{8,9},{9,8},{10,11... | collective-permute-start | bytes 1179656 | tf_op jit(solution)/shard_map/ppermute | solution.py:19
  73.6 16.2 %collective-permute-start.12 = (bf16[3,2,128,128]{3,2,1,0:T(8,128)(2,1)S(1)}, bf16[3,2,128,128]{3,2,1,0:T(8,128)(2,1)S(1)}, u32[]{:S(2)}, u32[]{:S(2)}) collective-permute-start(bf16[3,2,128,128]{3,2,1,0:T(8,128)(2,1)S(1)} %add_convert_fusion.5), channel_id=1, source_target_pairs={{0,4},{1,5},{2,6},{3,7},{4,0},{5,1},{6,2},{7,3},{8,12},{9,13},{10,... | collective-permute-start | bytes 589832 | tf_op jit(solution)/shard_map/ppermute | solution.py:19
  77.7 12.3 %collective-permute-start.18 = (bf16[3,2,128,128]{3,2,1,0:T(8,128)(2,1)S(1)}, bf16[3,2,128,128]{3,2,1,0:T(8,128)(2,1)S(1)}, u32[]{:S(2)}, u32[]{:S(2)}) collective-permute-start(bf16[3,2,128,128]{3,2,1,0:T(8,128)(2,1)S(1)} %add_convert_fusion.4), channel_id=1, source_target_pairs={{0,2},{1,3},{2,0},{3,1},{4,6},{5,7},{6,4},{7,5},{8,10},{9,11},{10,... | collective-permute-start | bytes 589832 | tf_op jit(solution)/shard_map/ppermute | solution.py:19
  79.2 15.6 %collective-permute-start.17 = (bf16[3,2,128,128]{3,2,1,0:T(8,128)(2,1)S(1)}, bf16[3,2,128,128]{3,2,1,0:T(8,128)(2,1)S(1)}, u32[]{:S(2)}, u32[]{:S(2)}) collective-permute-start(bf16[3,2,128,128]{3,2,1,0:T(8,128)(2,1)S(1)} %add_convert_fusion.3), channel_id=1, source_target_pairs={{0,4},{1,5},{2,6},{3,7},{4,0},{5,1},{6,2},{7,3},{8,12},{9,13},{10,... | collective-permute-start | bytes 589832 | tf_op jit(solution)/shard_map/ppermute | solution.py:19
  85.4 21.0 %collective-permute-start.22 = (bf16[3,2,128,128]{3,2,1,0:T(8,128)(2,1)S(1)}, bf16[3,2,128,128]{3,2,1,0:T(8,128)(2,1)S(1)}, u32[]{:S(2)}, u32[]{:S(2)}) collective-permute-start(bf16[3,2,128,128]{3,2,1,0:T(8,128)(2,1)S(1)} %add_convert_fusion.2), channel_id=1, source_target_pairs={{0,2},{1,3},{2,0},{3,1},{4,6},{5,7},{6,4},{7,5},{8,10},{9,11},{10,... | collective-permute-start | bytes 589832 | tf_op jit(solution)/shard_map/ppermute | solution.py:19
  89.9 14.8 %collective-permute-start.16 = (bf16[3,2,128,128]{3,2,1,0:T(8,128)(2,1)S(1)}, bf16[3,2,128,128]{3,2,1,0:T(8,128)(2,1)S(1)}, u32[]{:S(2)}, u32[]{:S(2)}) collective-permute-start(bf16[3,2,128,128]{3,2,1,0:T(8,128)(2,1)S(1)} %select_convert_fusion.3), channel_id=1, source_target_pairs={{0,2},{1,3},{2,0},{3,1},{4,6},{5,7},{6,4},{7,5},{8,10},{9,11},{10,... | collective-permute-start | bytes 589832 | tf_op jit(solution)/shard_map/ppermute | solution.py:19
  90.1 18.0 %collective-permute-start.21 = (bf16[3,2,128,128]{3,2,1,0:T(8,128)(2,1)S(1)}, bf16[3,2,128,128]{3,2,1,0:T(8,128)(2,1)S(1)}, u32[]{:S(2)}, u32[]{:S(2)}) collective-permute-start(bf16[3,2,128,128]{3,2,1,0:T(8,128)(2,1)S(1)} %add_convert_fusion.1), channel_id=1, source_target_pairs={{0,4},{1,5},{2,6},{3,7},{4,0},{5,1},{6,2},{7,3},{8,12},{9,13},{10,... | collective-permute-start | bytes 589832 | tf_op jit(solution)/shard_map/ppermute | solution.py:19
  94.9 15.8 %collective-permute-start.20 = (bf16[3,2,128,128]{3,2,1,0:T(8,128)(2,1)S(1)}, bf16[3,2,128,128]{3,2,1,0:T(8,128)(2,1)S(1)}, u32[]{:S(2)}, u32[]{:S(2)}) collective-permute-start(bf16[3,2,128,128]{3,2,1,0:T(8,128)(2,1)S(1)} %select_convert_fusion.2), channel_id=1, source_target_pairs={{0,2},{1,3},{2,0},{3,1},{4,6},{5,7},{6,4},{7,5},{8,10},{9,11},{10,... | collective-permute-start | bytes 589832 | tf_op jit(solution)/shard_map/ppermute | solution.py:19
  104.8 19.9 %collective-permute-start.19 = (bf16[3,2,256,128]{3,2,1,0:T(8,128)(2,1)S(1)}, bf16[3,2,256,128]{3,2,1,0:T(8,128)(2,1)S(1)}, u32[]{:S(2)}, u32[]{:S(2)}) collective-permute-start(bf16[3,2,256,128]{3,2,1,0:T(8,128)(2,1)S(1)} %pad_maximum_fusion.4), channel_id=1, source_target_pairs={{0,1},{1,0},{2,3},{3,2},{4,5},{5,4},{6,7},{7,6},{8,9},{9,8},{10,11... | collective-permute-start | bytes 1179656 | tf_op jit(solution)/shard_map/ppermute | solution.py:19
  106.5 9.1 %collective-permute-start.25 = (bf16[3,2,128,128]{3,2,1,0:T(8,128)(2,1)S(1)}, bf16[3,2,128,128]{3,2,1,0:T(8,128)(2,1)S(1)}, u32[]{:S(2)}, u32[]{:S(2)}) collective-permute-start(bf16[3,2,128,128]{3,2,1,0:T(8,128)(2,1)S(1)} %add_convert_fusion), channel_id=1, source_target_pairs={{0,4},{1,5},{2,6},{3,7},{4,0},{5,1},{6,2},{7,3},{8,12},{9,13},{10,... | collective-permute-start | bytes 589832 | tf_op jit(solution)/shard_map/ppermute | solution.py:19
  108.2 8.4 %collective-permute-start.24 = (bf16[3,2,128,128]{3,2,1,0:T(8,128)(2,1)S(1)}, bf16[3,2,128,128]{3,2,1,0:T(8,128)(2,1)S(1)}, u32[]{:S(2)}, u32[]{:S(2)}) collective-permute-start(bf16[3,2,128,128]{3,2,1,0:T(8,128)(2,1)S(1)} %select_convert_fusion.1), channel_id=1, source_target_pairs={{0,2},{1,3},{2,0},{3,1},{4,6},{5,7},{6,4},{7,5},{8,10},{9,11},{10,... | collective-permute-start | bytes 589832 | tf_op jit(solution)/shard_map/ppermute | solution.py:19
  110.8 13.7 %collective-permute-start.23 = (bf16[3,2,256,128]{3,2,1,0:T(8,128)(2,1)S(1)}, bf16[3,2,256,128]{3,2,1,0:T(8,128)(2,1)S(1)}, u32[]{:S(2)}, u32[]{:S(2)}) collective-permute-start(bf16[3,2,256,128]{3,2,1,0:T(8,128)(2,1)S(1)} %pad_maximum_fusion.5), channel_id=1, source_target_pairs={{0,1},{1,0},{2,3},{3,2},{4,5},{5,4},{6,7},{7,6},{8,9},{9,8},{10,11... | collective-permute-start | bytes 1179656 | tf_op jit(solution)/shard_map/ppermute | solution.py:19
  116.7 16.2 %collective-permute-start.26 = (bf16[3,2,256,128]{3,2,1,0:T(8,128)(2,1)S(1)}, bf16[3,2,256,128]{3,2,1,0:T(8,128)(2,1)S(1)}, u32[]{:S(2)}, u32[]{:S(2)}) collective-permute-start(bf16[3,2,256,128]{3,2,1,0:T(8,128)(2,1)S(1)} %pad_maximum_fusion.6), channel_id=1, source_target_pairs={{0,1},{1,0},{2,3},{3,2},{4,5},{5,4},{6,7},{7,6},{8,9},{9,8},{10,11... | collective-permute-start | bytes 1179656 | tf_op jit(solution)/shard_map/ppermute | solution.py:19
  121.5 16.9 %collective-permute-start.28 = (bf16[3,2,256,128]{3,2,1,0:T(8,128)(2,1)S(1)}, bf16[3,2,256,128]{3,2,1,0:T(8,128)(2,1)S(1)}, u32[]{:S(2)}, u32[]{:S(2)}) collective-permute-start(bf16[3,2,256,128]{3,2,1,0:T(8,128)(2,1)S(1)} %pad_maximum_fusion.7), channel_id=1, source_target_pairs={{0,1},{1,0},{2,3},{3,2},{4,5},{5,4},{6,7},{7,6},{8,9},{9,8},{10,11... | collective-permute-start | bytes 1179656 | tf_op jit(solution)/shard_map/ppermute | solution.py:19
  (21 other events, 134.6 us)

commit v3 on v2

--- a/solution.py
+++ b/solution.py
@@ -9,9 +9,12 @@
 
 SMALL_COST = pl.CostEstimate(flops=1, bytes_accessed=1, transcendentals=0)
 VMEM_LIMIT = 24 * 1024 * 1024
-LAG = 0.3
-PACE = 0.6
-PLAN = ((0, 1, True), (1, 1, True), (2, 1, True), (3, 1, True))
+TRANSFERS = (2, 2)
+KERNEL, NEAR, FAR, LATENCY = 0.4, 0.4, 0.8, 0.25
+EARLY = 0.1
+TIES = (1, 1, 1)
+WAIT = 0.4
+TURNED = ()
 
 
 def swap(value, axis, bit):
@@ -28,14 +31,14 @@
     return [1 << b for b in range(size.bit_length() - 1)]
 
 
-def overlap_kernel(count, picks_ref, half_ref, own_ref, field_ref, *refs):
-    sources = refs[:count]
+def overlap_kernel(offsets, picks_ref, half_ref, own_ref, field_ref, *refs):
+    sources = refs[:-5]
     send_ref, keep_ref, pick_ref, full, turned = refs[-5:]
     pick = picks_ref[pl.program_id(0)]
-    for j in range(count):
+    for j, first in enumerate(offsets):
         @pl.when(pick == j)
         def _():
-            pick_ref[0] = sources[j][...]
+            pick_ref[0] = sources[j][:, first:first + pick_ref.shape[2], :]
     _, bands, points = own_ref.shape
     width = pick_ref.shape[2]
     rows = bands // 2
@@ -57,26 +60,21 @@
     keep_ref[0] = full[:, pl.ds(here, rows), :]
 
 
-def overlap(q0, q_count, start, picks, half, own, potential, sources):
+def overlap(q0, q_count, width, picks, half, own, potential, sources):
     _, bands, points = own.shape
-    width = sources[-1][0].shape[1]
     rows = bands // 2
-    chunk = start // width
-    specs = []
-    for array, is_whole in sources:
-        row = chunk if is_whole else 0
-        specs.append(pl.BlockSpec((2, width, points), lambda q, p, h, row=row: (0, row, 0), pipeline_mode=pl.Buffered(1)))
+    in_vmem = pl.BlockSpec(memory_space=pltpu.VMEM)
     arrays = [own, potential] + [array for array, _ in sources]
     return pl.pallas_call(
-        functools.partial(overlap_kernel, len(sources)),
+        functools.partial(overlap_kernel, [offset for _, offset in sources]),
         grid_spec=pltpu.PrefetchScalarGridSpec(
             num_scalar_prefetch=2,
             grid=(q_count,),
             in_specs=[
-                pl.BlockSpec((2, bands, points), lambda q, p, h: (0, 0, 0), pipeline_mode=pl.Buffered(1)),
+                in_vmem,
                 pl.BlockSpec((1, 2, points), lambda q, p, h: (q0 + q, 0, 0)),
             ]
-            + specs,
+            + [in_vmem] * len(sources),
             out_specs=[
                 pl.BlockSpec((1, 2, rows, width), lambda q, p, h: (q, 0, 0, 0)),
                 pl.BlockSpec((1, 2, rows, width), lambda q, p, h: (q, 0, 0, 0)),
@@ -97,9 +95,9 @@
     )(picks, half, *arrays)
 
 
-def mix_kernel(chunk_count, density_scale, count_ref, field_ref, own_ref, *refs):
-    weights = refs[:chunk_count]
-    partners = refs[chunk_count:2 * chunk_count]
+def mix_kernel(places, density_scale, count_ref, field_ref, own_ref, *refs):
+    weights = refs[:len(places)]
+    partners = refs[len(places):2 * len(places)]
     source_ref, density_ref, left_real, left_imag, right = refs[-5:]
     bands = own_ref.shape[1]
 
@@ -116,12 +114,14 @@
             left_imag[:, far] = weight[0, 0]
 
     start = 0
-    for partner in partners:
+    block = right.shape[1]
+    here = pl.ds(pl.multiple_of(pl.program_id(0) * block, block), block)
+    for at, partner in zip(places, partners):
         width = 2 * partner.shape[2]
-        right[pl.ds(start, width), :] = partner[0].reshape(width, partner.shape[3])
+        right[pl.ds(start, width), :] = partner[at, :, :, here].reshape(width, block)
         start += width
     u, v = field_ref[0, 0:1], field_ref[0, 1:2]
-    a, b = own_ref[0].astype(jnp.float32), own_ref[1].astype(jnp.float32)
+    a, b = own_ref[0, :, here].astype(jnp.float32), own_ref[1, :, here].astype(jnp.float32)
     applied_real = (u * a - v * b).astype(jnp.bfloat16).astype(jnp.float32)
     applied_imag = (u * b + v * a).astype(jnp.bfloat16).astype(jnp.float32)
     real = applied_real - jnp.dot(left_real[...], right[...], preferred_element_type=jnp.float32)
@@ -137,25 +137,22 @@
 def mix(q, count, potential, orbitals, partners, weights, buffer, density_scale):
     q_total = potential.shape[0]
     _, bands, points = orbitals.shape
-    block = points // 4
+    block = points // 2
+    in_vmem = pl.BlockSpec(memory_space=pltpu.VMEM)
     specs = [
         pl.BlockSpec((1, 2, block), lambda i, c: (q, 0, i)),
-        pl.BlockSpec((2, bands, block), lambda i, c: (0, 0, i)),
+        in_vmem,
     ]
     arrays = [potential, orbitals]
-    for at, weight in weights:
-        specs.append(pl.BlockSpec((1, 2, bands, weight.shape[3]), lambda i, c, at=at: (at, 0, 0, 0)))
-        arrays.append(weight)
-    for at, partner in partners:
-        specs.append(pl.BlockSpec((1, 2, partner.shape[2], block), lambda i, c, at=at: (at, 0, 0, i)))
-        arrays.append(partner)
+    arrays += weights + [partner for _, partner in partners]
+    specs += [in_vmem] * (len(weights) + len(partners))
     aliases = {}
     if buffer is not None:
         specs.append(pl.BlockSpec(memory_space=pl.ANY))
         arrays.append(buffer)
         aliases = {len(arrays): 0}
     return pl.pallas_call(
-        functools.partial(mix_kernel, len(weights), density_scale),
+        functools.partial(mix_kernel, [at for at, _ in partners], density_scale),
         grid_spec=pltpu.PrefetchScalarGridSpec(
             num_scalar_prefetch=1,
             grid=(points // block,),
@@ -196,9 +193,12 @@
     last_bit = ka_bits[-1]
 
     fetched = []
-    spans = [(first * bands // 4, count * bands // 4) for first, count, _ in PLAN]
-    for start, width in spans:
-        have = {0: own[:, start:start + width]}
+    quarter = bands // 4
+    edges = [sum(TRANSFERS[:t]) for t in range(len(TRANSFERS) + 1)]
+    for first, last in zip(edges, edges[1:]):
+        start, width = first * quarter, (last - first) * quarter
+        piece = own[:, start:start + width] if not fetched else after(own, fetched[0][0])[:, start:start + width]
+        have = {0: piece}
         for bit in ka_bits[:-1]:
             for rel in list(have):
                 have[rel ^ bit] = swap(have[rel], "ka", bit)
@@ -208,38 +208,41 @@
     def bit_of(bit):
         return (g_index // bit) % 2
 
-    away_half = (1 - bit_of(grid_bits[0]))[None].astype(jnp.int32)
+    def order_of(i):
+        if i in TURNED and len(grid_bits) > 2:
+            return [grid_bits[1], grid_bits[0]] + grid_bits[2:]
+        return grid_bits
 
     groups = []
-    for c, (_, _, together) in enumerate(PLAN):
-        groups += [(c, 0, q_count)] if together else [(c, q, 1) for q in range(q_count)]
+    for t, (first, last) in enumerate(zip(edges, edges[1:])):
+        groups += [(t, c, 0, q_count) for c in range(first, last)]
     state = {}
     picked = {}
     previous = own_count
 
     def run_overlap(i):
         nonlocal previous
-        c, q0, count = groups[i]
-        have = fetched[c]
-        if q0 == 0:
+        t, c, q0, count = groups[i]
+        have = fetched[t]
+        if last_bit not in have:
             for rel in list(have):
                 if rel:
                     have[rel ^ last_bit] = swap(after(have[rel], previous), "ka", last_bit)
-            have[last_bit] = None
+            have[0], have[last_bit] = own, sibling
         sources = []
         for rel in range(len(have)):
-            whole = {0: own, last_bit: sibling}.get(rel)
-            sources.append((have[rel], False) if whole is None else (whole, True))
+            offset = c if rel in (0, last_bit) else c - edges[t]
+            sources.append((have[rel], offset * quarter))
         leaving, keep, picked[i] = overlap(
-            q0, count, spans[c][0], picks[q0:q0 + count], away_half, own, after(potential, previous), sources
+            q0, count, quarter, picks[q0:q0 + count], 1 - bit_of(order_of(i)[0])[None], own, after(potential, previous), sources
         )
         previous = leaving
-        state[i] = (keep, swap(leaving, "grid", grid_bits[0]))
+        state[i] = (keep, swap(leaving, "grid", order_of(i)[0]))
 
     def run_scatter(i, bit, full):
         nonlocal previous
         keep, arriving = state[i]
-        arriving = after(arriving, previous)
+        arriving = after(arriving, previous) if TIES[0] else arriving
         mine = bit_of(bit)
         half = keep.shape[2] // 2
 
@@ -259,10 +262,10 @@
 
     def run_turn(i, bit):
         nonlocal previous
-        c, q0, count = groups[i]
-        start, width = spans[c]
+        _, c, q0, count = groups[i]
+        start, width = c * quarter, quarter
         keep, arriving = state[i]
-        total = keep.astype(jnp.float32) + after(arriving, previous).astype(jnp.float32)
+        total = keep.astype(jnp.float32) + (after(arriving, previous) if TIES[1] else arriving).astype(jnp.float32)
         limits = partner_counts[q0:q0 + count][:, None, None, None]
         mask = (start + jnp.arange(width, dtype=jnp.int32)) < limits
         piece = jnp.where(mask, volume_weight * total, 0.0).astype(jnp.bfloat16)
@@ -271,42 +274,52 @@
 
     def run_gather(i, done_bit, bit):
         nonlocal previous
+        upper = bit_of(done_bit) == 1
         piece, other = state[i]
-        upper = bit_of(done_bit) == 1
-        other = after(other, previous) if bit is not None else other
+        other = after(other, previous) if bit is not None and TIES[2] else other
         piece = jnp.concatenate([jnp.where(upper, other, piece), jnp.where(upper, piece, other)], axis=2)
         if bit is None:
-            state[i] = piece
+            state[i] = [piece[q:q + 1] for q in range(piece.shape[0])]
             return
         previous = piece
-        state[i] = (piece, swap(piece, "grid", bit))
+        if i == len(groups) - 1 and bit == order_of(i)[0]:
+            parts = [piece[q:q + 1] for q in range(piece.shape[0])]
+            state[i] = [(part, swap(part, "grid", bit)) for part in parts]
+        else:
+            state[i] = (piece, swap(piece, "grid", bit))
 
     stages = []
     steps = len(grid_bits)
-    for i, (c, q0, count) in enumerate(groups):
-        first, quarters, _ = PLAN[c]
-        at = PACE * (first + quarters) + 0.2 * q0
-        scale = quarters * count / q_count
-        stages.append((at, i, functools.partial(run_overlap, i)))
-        at += 0.85 * scale + LAG
+    for i, (t, c, q0, count) in enumerate(groups):
+        bits = order_of(i)
+        at = edges[t + 1] + LATENCY + KERNEL * (c - edges[t])
+        stages.append((at + EARLY, i, functools.partial(run_overlap, i)))
+        at += KERNEL + FAR + WAIT + (FAR - KERNEL) * (c - edges[t])
         for s in range(1, steps):
-            stages.append((at, i, functools.partial(run_scatter, i, grid_bits[s], s == steps - 1)))
-            at += (0.4 if s < steps - 1 else 0.8) * scale + LAG
-        stages.append((at, i, functools.partial(run_turn, i, grid_bits[steps - 2])))
-        at += 0.4 * scale + LAG
+            last = s == steps - 1
+            stages.append((at, i, functools.partial(run_scatter, i, bits[s], last)))
+            at += (FAR if last else NEAR) + LATENCY
+        stages.append((at, i, functools.partial(run_turn, i, bits[steps - 2])))
+        at += NEAR + LATENCY
         for s in range(steps - 2, 0, -1):
-            stages.append((at, i, functools.partial(run_gather, i, grid_bits[s], grid_bits[s - 1])))
-            at += 0.85 * scale + LAG
-        stages.append((at, i, functools.partial(run_gather, i, grid_bits[0], None)))
+            stages.append((at, i, functools.partial(run_gather, i, bits[s], bits[s - 1])))
+            at += FAR + LATENCY
+        if i < len(groups) - 1:
+            stages.append((at, i, functools.partial(run_gather, i, bits[0], None)))
     for _, _, stage in sorted(stages, key=lambda entry: entry[:2]):
         stage()
 
     buffer = None
     density = []
     for q in range(q_count):
-        own_groups = [i for i, (_, q0, n) in enumerate(groups) if q0 <= q < q0 + n]
-        weights = [(q - groups[i][1], state[i]) for i in own_groups]
-        chosen = [(q - groups[i][1], picked[i]) for i in own_groups]
+        own_groups = [i for i, (_, _, q0, n) in enumerate(groups) if q0 <= q < q0 + n]
+        weights = [state[i][q - groups[i][2]] for i in own_groups]
+        piece, other = weights[-1]
+        upper = bit_of(order_of(len(groups) - 1)[0]) == 1
+        if density:
+            other = after(other, density[-1])
+        weights[-1] = jnp.concatenate([jnp.where(upper, other, piece), jnp.where(upper, piece, other)], axis=2)
+        chosen = [(q - groups[i][2], picked[i]) for i in own_groups]
         buffer, term = mix(q, own_count, potential, own, chosen, weights, buffer, density_weight)
         density.append(term)
     density = jnp.concatenate(density, axis=0)

time: 163 us -> 153 us (0.939)
  waiting for transfers between devices: 72.4 us -> 64 us
  starting transfers between devices: 36.2 us -> 31.3 us
  other arithmetic: 8.04 us -> 10.3 us
    ppermute x32 -> x30, waiting for transfers between devices: 72.4 us -> 64 us  [swap(): return lax.ppermute(value, axis, [(i, i ^ bit) for i in range(size)])]
    ppermute x32 -> x30, starting transfers between devices: 36.2 us -> 31.3 us  [swap(): return lax.ppermute(value, axis, [(i, i ^ bit) for i in range(size)])]
    unnamed x26 -> x44, local copies, waits for them, and re-layouts: 5.03 us -> 5.29 us
  transfers between devices with their start and end apart: 32 -> 30, of which waited for: 18 -> 13; matrix products, arithmetic and copies ran while one was open for 6% -> 6% of each run, Pallas kernels for 12% -> 22%
where the time goes in v3:
time: 153 us
  waiting for transfers between devices  64 us (42%)
  Pallas kernels  38.5 us (25%)
  starting transfers between devices  31.3 us (20%)
  other arithmetic  10.3 us (7%)
  local copies, waits for them, and re-layouts  7.84 us (5%)
    ppermute x30, waiting for transfers between devices, swap(): return lax.ppermute(value, axis, [(i, i ^ bit) for i in range(size)])  64 us
    ppermute x30, starting transfers between devices, swap(): return lax.ppermute(value, axis, [(i, i ^ bit) for i in range(size)])  31.3 us
    pallas_call x4, Pallas kernels, overlap(): pl.pallas_call(functools.partial(overlap_kernel, [offset for _, offset in...  22.8 us
    pallas_call x3, Pallas kernels, mix(): pl.pallas_call(functools.partial(mix_kernel, [at for at, _ in partners],...  15.8 us
    unnamed x44, local copies, waits for them, and re-layouts  5.29 us
    convert_element_type x4, other arithmetic, run_scatter(): leaving = part(1 - mine).astype(jnp.bfloat16)  3.77 us
    convert_element_type x4, other arithmetic, run_scatter(): leaving = (keep + arriving.astype(jnp.float32)).astype(jnp.bfloat16)  3.49 us
  transfers between devices with their start and end apart: 30, of which 13 were waited for; matrix products, arithmetic and copies ran while one was open for 6% of the time, Pallas kernels for 22%

profile of v3, /device:TPU:0, one launch (start us, length us, event | category | flops | bytes accessed | tf_op | source)
XLA Modules:
  0.0 153.0 jit_solution(5730862007969062035)
XLA Ops:
  2.1 3.0 %collective-permute-start.1 = (bf16[2,256,1024]{2,1,0:T(8,128)(2,1)S(1)}, bf16[2,256,1024]{2,1,0:T(8,128)(2,1)}, u32[]{:S(2)}, u32[]{:S(2)}) collective-permute-start(bf16[2,256,1024]{2,1,0:T(8,128)(2,1)S(1)} %slice.56), channel_id=1, source_target_pairs={{0,16},{8,24},{16,0},{24,8},{1,17},{9,25},{17,1},{25,9},{2,18},{10... | collective-permute-start | bytes 3145736 | tf_op jit(solution)/shard_map/ppermute | solution.py:22
  5.8 22.6 %collective-permute-done.1.refs_2_ = bf16[2,256,1024]{2,1,0:T(8,128)(2,1)} collective-permute-done((bf16[2,256,1024]{2,1,0:T(8,128)(2,1)S(1)}, bf16[2,256,1024]{2,1,0:T(8,128)(2,1)}, u32[]{:S(2)}, u32[]{:S(2)}) %collective-permute-start.1) | collective-permute-done | bytes 1048608 | tf_op jit(solution)/shard_map/ppermute | solution.py:22
  31.4 6.0 %shard_map.59 = (bf16[3,2,256,128]{3,2,1,0:T(8,128)(2,1)}, f32[3,2,256,128]{3,2,1,0:T(8,128)S(1)}, bf16[3,2,128,1024]{3,2,1,0:T(8,128)(2,1)S(1)}) custom-call(s32[3]{0:T(128)S(1)} %broadcast_xor_fusion.picks_ref, s32[1]{0:T(128)} %bitcast.2.half_ref, bf16[2,512,1024]{2,1,0:T(8,128)(2,1)S(1)} %bitcast.6, f32[3,2,1024]{2,1,0:T(2,128)S(1)} %copy-done.9, ...), custom_call_target="tpu_custom_call" | custom-call | flops 1 | bytes 1 | tf_op jit(solution)/shard_map/pallas_call | solution.py:68
  41.2 6.0 %shard_map.60 = (bf16[3,2,256,128]{3,2,1,0:T(8,128)(2,1)}, f32[3,2,256,128]{3,2,1,0:T(8,128)S(1)}, bf16[3,2,128,1024]{3,2,1,0:T(8,128)(2,1)S(1)}) custom-call(s32[3]{0:T(128)S(1)} %broadcast_xor_fusion.picks_ref, s32[1]{0:T(128)} %bitcast.2.half_ref, bf16[2,512,1024]{2,1,0:T(8,128)(2,1)S(1)} %bitcast.8, f32[3,2,1024]{2,1,0:T(2,128)S(1)} %copy-done.9, ...), custom_call_target="tpu_custom_call" | custom-call | flops 1 | bytes 1 | tf_op jit(solution)/shard_map/pallas_call | solution.py:68
  48.4 2.6 %collective-permute-done.3 = bf16[3,2,256,128]{3,2,1,0:T(8,128)(2,1)} collective-permute-done((bf16[3,2,256,128]{3,2,1,0:T(8,128)(2,1)}, bf16[3,2,256,128]{3,2,1,0:T(8,128)(2,1)}, u32[]{:S(2)}, u32[]{:S(2)}) %collective-permute-start.3) | collective-permute-done | bytes 393248 | tf_op jit(solution)/shard_map/ppermute | solution.py:22
  52.7 2.6 %collective-permute-done.5.refs_2_ = bf16[2,256,1024]{2,1,0:T(8,128)(2,1)S(1)} collective-permute-done((bf16[2,256,1024]{2,1,0:T(8,128)(2,1)}, bf16[2,256,1024]{2,1,0:T(8,128)(2,1)S(1)}, u32[]{:S(2)}, u32[]{:S(2)}) %collective-permute-start.5) | collective-permute-done | bytes 1048608 | tf_op jit(solution)/shard_map/ppermute | solution.py:22
  55.3 1.8 %collective-permute-start.8 = (bf16[3,2,256,128]{3,2,1,0:T(8,128)(2,1)}, bf16[3,2,256,128]{3,2,1,0:T(8,128)(2,1)}, u32[]{:S(2)}, u32[]{:S(2)}) collective-permute-start(bf16[3,2,256,128]{3,2,1,0:T(8,128)(2,1)} %get-tuple-element.50), channel_id=1, source_target_pairs={{0,1},{1,0},{2,3},{3,2},{4,5},{5,4},{6,7},{7,6},{8,9},{9,8},{10,11... | collective-permute-start | bytes 1179656 | tf_op jit(solution)/shard_map/ppermute | solution.py:22
  58.9 5.7 %shard_map.61 = (bf16[3,2,256,128]{3,2,1,0:T(8,128)(2,1)}, f32[3,2,256,128]{3,2,1,0:T(8,128)S(1)}, bf16[3,2,128,1024]{3,2,1,0:T(8,128)(2,1)S(1)}) custom-call(s32[3]{0:T(128)S(1)} %broadcast_xor_fusion.picks_ref, s32[1]{0:T(128)} %bitcast.2.half_ref, bf16[2,512,1024]{2,1,0:T(8,128)(2,1)S(1)} %bitcast.10, f32[3,2,1024]{2,1,0:T(2,128)S(1)} %copy-done.9, ...), custom_call_target="tpu_custom_call" | custom-call | flops 1 | bytes 1 | tf_op jit(solution)/shard_map/pallas_call | solution.py:68
  68.1 1.9 %collective-permute-start.9 = (bf16[3,2,128,128]{3,2,1,0:T(8,128)(2,1)S(1)}, bf16[3,2,128,128]{3,2,1,0:T(8,128)(2,1)S(1)}, u32[]{:S(2)}, u32[]{:S(2)}) collective-permute-start(bf16[3,2,128,128]{3,2,1,0:T(8,128)(2,1)S(1)} %add_convert_fusion.5), channel_id=1, source_target_pairs={{0,2},{1,3},{2,0},{3,1},{4,6},{5,7},{6,4},{7,5},{8,10},{9,11},{10,... | collective-permute-start | bytes 589832 | tf_op jit(solution)/shard_map/ppermute | solution.py:22
  70.1 2.6 %collective-permute-start.7 = (bf16[3,2,128,128]{3,2,1,0:T(8,128)(2,1)S(1)}, bf16[3,2,128,128]{3,2,1,0:T(8,128)(2,1)S(1)}, u32[]{:S(2)}, u32[]{:S(2)}) collective-permute-start(bf16[3,2,128,128]{3,2,1,0:T(8,128)(2,1)S(1)} %add_convert_fusion.6), channel_id=1, source_target_pairs={{0,4},{1,5},{2,6},{3,7},{4,0},{5,1},{6,2},{7,3},{8,12},{9,13},{10,... | collective-permute-start | bytes 589832 | tf_op jit(solution)/shard_map/ppermute | solution.py:22
  74.2 5.0 %shard_map.62 = (bf16[3,2,256,128]{3,2,1,0:T(8,128)(2,1)S(1)}, f32[3,2,256,128]{3,2,1,0:T(8,128)S(1)}, bf16[3,2,128,1024]{3,2,1,0:T(8,128)(2,1)S(1)}) custom-call(s32[3]{0:T(128)S(1)} %broadcast_xor_fusion.picks_ref, s32[1]{0:T(128)} %bitcast.2.half_ref, bf16[2,512,1024]{2,1,0:T(8,128)(2,1)S(1)} %bitcast.12, f32[3,2,1024]{2,1,0:T(2,128)S(1)} %copy-done.9, ...), custom_call_target="tpu_custom_call" | custom-call | flops 1 | bytes 1 | tf_op jit(solution)/shard_map/pallas_call | solution.py:68
  83.6 2.5 %collective-permute-start.13 = (bf16[3,2,128,128]{3,2,1,0:T(8,128)(2,1)S(1)}, bf16[3,2,128,128]{3,2,1,0:T(8,128)(2,1)S(1)}, u32[]{:S(2)}, u32[]{:S(2)}) collective-permute-start(bf16[3,2,128,128]{3,2,1,0:T(8,128)(2,1)S(1)} %add_convert_fusion.4), channel_id=1, source_target_pairs={{0,4},{1,5},{2,6},{3,7},{4,0},{5,1},{6,2},{7,3},{8,12},{9,13},{10,... | collective-permute-start | bytes 589832 | tf_op jit(solution)/shard_map/ppermute | solution.py:22
  87.4 6.6 %collective-permute-done.10 = bf16[3,2,128,128]{3,2,1,0:T(8,128)(2,1)S(1)} collective-permute-done((bf16[3,2,128,128]{3,2,1,0:T(8,128)(2,1)S(1)}, bf16[3,2,128,128]{3,2,1,0:T(8,128)(2,1)S(1)}, u32[]{:S(2)}, u32[]{:S(2)}) %collective-permute-start.10) | collective-permute-done | bytes 196640 | tf_op jit(solution)/shard_map/ppermute | solution.py:22
  94.8 3.3 %collective-permute-done.16 = bf16[3,2,128,128]{3,2,1,0:T(8,128)(2,1)S(1)} collective-permute-done((bf16[3,2,128,128]{3,2,1,0:T(8,128)(2,1)S(1)}, bf16[3,2,128,128]{3,2,1,0:T(8,128)(2,1)S(1)}, u32[]{:S(2)}, u32[]{:S(2)}) %collective-permute-start.16) | collective-permute-done | bytes 196640 | tf_op jit(solution)/shard_map/ppermute | solution.py:22
  100.5 5.3 %collective-permute-done.14 = bf16[3,2,128,128]{3,2,1,0:T(8,128)(2,1)S(1)} collective-permute-done((bf16[3,2,128,128]{3,2,1,0:T(8,128)(2,1)S(1)}, bf16[3,2,128,128]{3,2,1,0:T(8,128)(2,1)S(1)}, u32[]{:S(2)}, u32[]{:S(2)}) %collective-permute-start.14) | collective-permute-done | bytes 196640 | tf_op jit(solution)/shard_map/ppermute | solution.py:22
  107.0 2.3 %collective-permute-done.19 = bf16[3,2,128,128]{3,2,1,0:T(8,128)(2,1)S(1)} collective-permute-done((bf16[3,2,128,128]{3,2,1,0:T(8,128)(2,1)S(1)}, bf16[3,2,128,128]{3,2,1,0:T(8,128)(2,1)S(1)}, u32[]{:S(2)}, u32[]{:S(2)}) %collective-permute-start.19) | collective-permute-done | bytes 196640 | tf_op jit(solution)/shard_map/ppermute | solution.py:22
  111.2 6.0 %collective-permute-done.20 = bf16[3,2,128,128]{3,2,1,0:T(8,128)(2,1)S(1)} collective-permute-done((bf16[3,2,128,128]{3,2,1,0:T(8,128)(2,1)S(1)}, bf16[3,2,128,128]{3,2,1,0:T(8,128)(2,1)S(1)}, u32[]{:S(2)}, u32[]{:S(2)}) %collective-permute-start.20) | collective-permute-done | bytes 196640 | tf_op jit(solution)/shard_map/ppermute | solution.py:22
  117.3 2.5 %collective-permute-start.21 = (bf16[3,2,256,128]{3,2,1,0:T(8,128)(2,1)S(1)}, bf16[3,2,256,128]{3,2,1,0:T(8,128)(2,1)S(1)}, u32[]{:S(2)}, u32[]{:S(2)}) collective-permute-start(bf16[3,2,256,128]{3,2,1,0:T(8,128)(2,1)S(1)} %pad_maximum_fusion.2), channel_id=1, source_target_pairs={{0,1},{1,0},{2,3},{3,2},{4,5},{5,4},{6,7},{7,6},{8,9},{9,8},{10,11... | collective-permute-start | bytes 1179656 | tf_op jit(solution)/shard_map/ppermute | solution.py:22
  120.2 5.5 %collective-permute-done.23 = bf16[3,2,128,128]{3,2,1,0:T(8,128)(2,1)S(1)} collective-permute-done((bf16[3,2,128,128]{3,2,1,0:T(8,128)(2,1)S(1)}, bf16[3,2,128,128]{3,2,1,0:T(8,128)(2,1)S(1)}, u32[]{:S(2)}, u32[]{:S(2)}) %collective-permute-start.23) | collective-permute-done | bytes 196640 | tf_op jit(solution)/shard_map/ppermute | solution.py:22
  125.8 2.1 %collective-permute-start.25 = (bf16[1,2,256,128]{3,2,1,0:T(8,128)(2,1)S(1)}, bf16[1,2,256,128]{3,2,1,0:T(8,128)(2,1)S(1)}, u32[]{:S(2)}, u32[]{:S(2)}) collective-permute-start(bf16[1,2,256,128]{3,2,1,0:T(8,128)(2,1)S(1)} %get-tuple-element.105), channel_id=1, source_target_pairs={{0,1},{1,0},{2,3},{3,2},{4,5},{5,4},{6,7},{7,6},{8,9},{9,8},{10,11... | collective-permute-start | bytes 393224 | tf_op jit(solution)/shard_map/ppermute | solution.py:22
  128.0 3.4 %collective-permute-done.26 = bf16[1,2,256,128]{3,2,1,0:T(8,128)(2,1)S(1)} collective-permute-done((bf16[1,2,256,128]{3,2,1,0:T(8,128)(2,1)S(1)}, bf16[1,2,256,128]{3,2,1,0:T(8,128)(2,1)S(1)}, u32[]{:S(2)}, u32[]{:S(2)}) %collective-permute-start.26) | collective-permute-done | bytes 131104 | tf_op jit(solution)/shard_map/ppermute | solution.py:22
  131.8 5.3 %shard_map.63 = (bf16[3,1,2,512,1024]{4,3,2,1,0:T(8,128)(2,1)}, f32[1,1024]{1,0:T(1,128)S(1)}) custom-call(s32[1]{0:T(128)} %bitcast.count_ref, f32[3,2,1024]{2,1,0:T(2,128)S(1)} %copy-done.9, bf16[2,512,1024]{2,1,0:T(8,128)(2,1)S(1)} %bitcast.14, bf16[1,2,512,128]{3,2,1,0:T(8,128)(2,1)S(1)} %get-tuple-element.94.refs_0_, ...), custom_call_target="tpu_custom_call" | custom-call | flops 1 | bytes 1 | tf_op jit(solution)/shard_map/pallas_call | solution.py:154
  137.1 5.3 %shard_map.64 = (bf16[3,1,2,512,1024]{4,3,2,1,0:T(8,128)(2,1)}, f32[1,1024]{1,0:T(1,128)S(1)}) custom-call(s32[1]{0:T(128)} %bitcast.count_ref, f32[3,2,1024]{2,1,0:T(2,128)S(1)} %copy-done.9, bf16[2,512,1024]{2,1,0:T(8,128)(2,1)S(1)} %bitcast.15, bf16[1,2,512,128]{3,2,1,0:T(8,128)(2,1)S(1)} %get-tuple-element.96.refs_0_, ...), custom_call_target="tpu_custom_call", output_to_operand_aliasing={{0}: (11, {})} | custom-call | flops 1 | bytes 1 | tf_op jit(solution)/shard_map/pallas_call | solution.py:154
  142.4 5.3 %shard_map.65 = (bf16[3,1,2,512,1024]{4,3,2,1,0:T(8,128)(2,1)}, f32[1,1024]{1,0:T(1,128)S(1)}) custom-call(s32[1]{0:T(128)} %bitcast.count_ref, f32[3,2,1024]{2,1,0:T(2,128)S(1)} %copy-done.9, bf16[2,512,1024]{2,1,0:T(8,128)(2,1)S(1)} %bitcast.16, bf16[1,2,512,128]{3,2,1,0:T(8,128)(2,1)S(1)} %get-tuple-element.95.refs_0_, ...), custom_call_target="tpu_custom_call", output_to_operand_aliasing={{0}: (11, {})} | custom-call | flops 1 | bytes 1 | tf_op jit(solution)/shard_map/pallas_call | solution.py:154
  (131 shorter events, 36.9 us)
Async XLA Ops:
  2.1 26.3 %collective-permute-start.1 = (bf16[2,256,1024]{2,1,0:T(8,128)(2,1)S(1)}, bf16[2,256,1024]{2,1,0:T(8,128)(2,1)}, u32[]{:S(2)}, u32[]{:S(2)}) collective-permute-start(bf16[2,256,1024]{2,1,0:T(8,128)(2,1)S(1)} %slice.56), channel_id=1, source_target_pairs={{0,16},{8,24},{16,0},{24,8},{1,17},{9,25},{17,1},{25,9},{2,18},{10... | collective-permute-start | bytes 3145736 | tf_op jit(solution)/shard_map/ppermute | solution.py:22
  5.1 26.3 %collective-permute-start = (bf16[2,512,1024]{2,1,0:T(8,128)(2,1)S(1)}, bf16[2,512,1024]{2,1,0:T(8,128)(2,1)}, u32[]{:S(2)}, u32[]{:S(2)}) collective-permute-start(bf16[2,512,1024]{2,1,0:T(8,128)(2,1)S(1)} %bitcast.4), channel_id=1, source_target_pairs={{0,8},{8,0},{16,24},{24,16},{1,9},{9,1},{17,25},{25,17},{2,10},{10... | collective-permute-start | bytes 6291464 | tf_op jit(solution)/shard_map/ppermute | solution.py:22
  29.5 25.8 %collective-permute-start.5 = (bf16[2,256,1024]{2,1,0:T(8,128)(2,1)}, bf16[2,256,1024]{2,1,0:T(8,128)(2,1)S(1)}, u32[]{:S(2)}, u32[]{:S(2)}) collective-permute-start(bf16[2,256,1024]{2,1,0:T(8,128)(2,1)} %slice.43), channel_id=1, source_target_pairs={{0,16},{8,24},{16,0},{24,8},{1,17},{9,25},{17,1},{25,9},{2,18},{10... | collective-permute-start | bytes 3145736 | tf_op jit(solution)/shard_map/ppermute | solution.py:22
  39.4 11.6 %collective-permute-start.3 = (bf16[3,2,256,128]{3,2,1,0:T(8,128)(2,1)}, bf16[3,2,256,128]{3,2,1,0:T(8,128)(2,1)}, u32[]{:S(2)}, u32[]{:S(2)}) collective-permute-start(bf16[3,2,256,128]{3,2,1,0:T(8,128)(2,1)} %get-tuple-element.48), channel_id=1, source_target_pairs={{0,1},{1,0},{2,3},{3,2},{4,5},{5,4},{6,7},{7,6},{8,9},{9,8},{10,11... | collective-permute-start | bytes 1179656 | tf_op jit(solution)/shard_map/ppermute | solution.py:22
  55.3 11.9 %collective-permute-start.8 = (bf16[3,2,256,128]{3,2,1,0:T(8,128)(2,1)}, bf16[3,2,256,128]{3,2,1,0:T(8,128)(2,1)}, u32[]{:S(2)}, u32[]{:S(2)}) collective-permute-start(bf16[3,2,256,128]{3,2,1,0:T(8,128)(2,1)} %get-tuple-element.50), channel_id=1, source_target_pairs={{0,1},{1,0},{2,3},{3,2},{4,5},{5,4},{6,7},{7,6},{8,9},{9,8},{10,11... | collective-permute-start | bytes 1179656 | tf_op jit(solution)/shard_map/ppermute | solution.py:22
  57.1 7.5 %collective-permute-start.4 = (bf16[3,2,128,128]{3,2,1,0:T(8,128)(2,1)}, bf16[3,2,128,128]{3,2,1,0:T(8,128)(2,1)S(1)}, u32[]{:S(2)}, u32[]{:S(2)}) collective-permute-start(bf16[3,2,128,128]{3,2,1,0:T(8,128)(2,1)} %add_convert_fusion.7), channel_id=1, source_target_pairs={{0,2},{1,3},{2,0},{3,1},{4,6},{5,7},{6,4},{7,5},{8,10},{9,11},{10,... | collective-permute-start | bytes 589832 | tf_op jit(solution)/shard_map/ppermute | solution.py:22
  68.1 13.2 %collective-permute-start.9 = (bf16[3,2,128,128]{3,2,1,0:T(8,128)(2,1)S(1)}, bf16[3,2,128,128]{3,2,1,0:T(8,128)(2,1)S(1)}, u32[]{:S(2)}, u32[]{:S(2)}) collective-permute-start(bf16[3,2,128,128]{3,2,1,0:T(8,128)(2,1)S(1)} %add_convert_fusion.5), channel_id=1, source_target_pairs={{0,2},{1,3},{2,0},{3,1},{4,6},{5,7},{6,4},{7,5},{8,10},{9,11},{10,... | collective-permute-start | bytes 589832 | tf_op jit(solution)/shard_map/ppermute | solution.py:22
  70.1 12.4 %collective-permute-start.7 = (bf16[3,2,128,128]{3,2,1,0:T(8,128)(2,1)S(1)}, bf16[3,2,128,128]{3,2,1,0:T(8,128)(2,1)S(1)}, u32[]{:S(2)}, u32[]{:S(2)}) collective-permute-start(bf16[3,2,128,128]{3,2,1,0:T(8,128)(2,1)S(1)} %add_convert_fusion.6), channel_id=1, source_target_pairs={{0,4},{1,5},{2,6},{3,7},{4,0},{5,1},{6,2},{7,3},{8,12},{9,13},{10,... | collective-permute-start | bytes 589832 | tf_op jit(solution)/shard_map/ppermute | solution.py:22
  72.7 13.5 %collective-permute-start.11 = (bf16[3,2,256,128]{3,2,1,0:T(8,128)(2,1)}, bf16[3,2,256,128]{3,2,1,0:T(8,128)(2,1)}, u32[]{:S(2)}, u32[]{:S(2)}) collective-permute-start(bf16[3,2,256,128]{3,2,1,0:T(8,128)(2,1)} %get-tuple-element.55), channel_id=1, source_target_pairs={{0,1},{1,0},{2,3},{3,2},{4,5},{5,4},{6,7},{7,6},{8,9},{9,8},{10,11... | collective-permute-start | bytes 1179656 | tf_op jit(solution)/shard_map/ppermute | solution.py:22
  82.6 11.3 %collective-permute-start.10 = (bf16[3,2,128,128]{3,2,1,0:T(8,128)(2,1)S(1)}, bf16[3,2,128,128]{3,2,1,0:T(8,128)(2,1)S(1)}, u32[]{:S(2)}, u32[]{:S(2)}) collective-permute-start(bf16[3,2,128,128]{3,2,1,0:T(8,128)(2,1)S(1)} %select_convert_fusion.3), channel_id=1, source_target_pairs={{0,2},{1,3},{2,0},{3,1},{4,6},{5,7},{6,4},{7,5},{8,10},{9,11},{10,... | collective-permute-start | bytes 589832 | tf_op jit(solution)/shard_map/ppermute | solution.py:22
  83.1 16.9 %collective-permute-start.15 = (bf16[3,2,256,128]{3,2,1,0:T(8,128)(2,1)}, bf16[3,2,256,128]{3,2,1,0:T(8,128)(2,1)S(1)}, u32[]{:S(2)}, u32[]{:S(2)}) collective-permute-start(bf16[3,2,256,128]{3,2,1,0:T(8,128)(2,1)} %copy-done.19), channel_id=1, source_target_pairs={{0,1},{1,0},{2,3},{3,2},{4,5},{5,4},{6,7},{7,6},{8,9},{9,8},{10,11... | collective-permute-start | bytes 1179656 | tf_op jit(solution)/shard_map/ppermute | solution.py:22
  83.6 10.6 %collective-permute-start.13 = (bf16[3,2,128,128]{3,2,1,0:T(8,128)(2,1)S(1)}, bf16[3,2,128,128]{3,2,1,0:T(8,128)(2,1)S(1)}, u32[]{:S(2)}, u32[]{:S(2)}) collective-permute-start(bf16[3,2,128,128]{3,2,1,0:T(8,128)(2,1)S(1)} %add_convert_fusion.4), channel_id=1, source_target_pairs={{0,4},{1,5},{2,6},{3,7},{4,0},{5,1},{6,2},{7,3},{8,12},{9,13},{10,... | collective-permute-start | bytes 589832 | tf_op jit(solution)/shard_map/ppermute | solution.py:22
  87.2 10.9 %collective-permute-start.16 = (bf16[3,2,128,128]{3,2,1,0:T(8,128)(2,1)S(1)}, bf16[3,2,128,128]{3,2,1,0:T(8,128)(2,1)S(1)}, u32[]{:S(2)}, u32[]{:S(2)}) collective-permute-start(bf16[3,2,128,128]{3,2,1,0:T(8,128)(2,1)S(1)} %add_convert_fusion.3), channel_id=1, source_target_pairs={{0,2},{1,3},{2,0},{3,1},{4,6},{5,7},{6,4},{7,5},{8,10},{9,11},{10,... | collective-permute-start | bytes 589832 | tf_op jit(solution)/shard_map/ppermute | solution.py:22
  94.0 17.0 %collective-permute-start.12 = (bf16[3,2,256,128]{3,2,1,0:T(8,128)(2,1)S(1)}, bf16[3,2,256,128]{3,2,1,0:T(8,128)(2,1)S(1)}, u32[]{:S(2)}, u32[]{:S(2)}) collective-permute-start(bf16[3,2,256,128]{3,2,1,0:T(8,128)(2,1)S(1)} %pad_maximum_fusion), channel_id=1, source_target_pairs={{0,1},{1,0},{2,3},{3,2},{4,5},{5,4},{6,7},{7,6},{8,9},{9,8},{10,11... | collective-permute-start | bytes 1179656 | tf_op jit(solution)/shard_map/ppermute | solution.py:22
  94.3 11.6 %collective-permute-start.14 = (bf16[3,2,128,128]{3,2,1,0:T(8,128)(2,1)S(1)}, bf16[3,2,128,128]{3,2,1,0:T(8,128)(2,1)S(1)}, u32[]{:S(2)}, u32[]{:S(2)}) collective-permute-start(bf16[3,2,128,128]{3,2,1,0:T(8,128)(2,1)S(1)} %select_convert_fusion.2), channel_id=1, source_target_pairs={{0,2},{1,3},{2,0},{3,1},{4,6},{5,7},{6,4},{7,5},{8,10},{9,11},{10,... | collective-permute-start | bytes 589832 | tf_op jit(solution)/shard_map/ppermute | solution.py:22
  99.2 11.2 %collective-permute-start.18 = (bf16[3,2,128,128]{3,2,1,0:T(8,128)(2,1)S(1)}, bf16[3,2,128,128]{3,2,1,0:T(8,128)(2,1)S(1)}, u32[]{:S(2)}, u32[]{:S(2)}) collective-permute-start(bf16[3,2,128,128]{3,2,1,0:T(8,128)(2,1)S(1)} %add_convert_fusion.2), channel_id=1, source_target_pairs={{0,4},{1,5},{2,6},{3,7},{4,0},{5,1},{6,2},{7,3},{8,12},{9,13},{10,... | collective-permute-start | bytes 589832 | tf_op jit(solution)/shard_map/ppermute | solution.py:22
  100.0 9.3 %collective-permute-start.19 = (bf16[3,2,128,128]{3,2,1,0:T(8,128)(2,1)S(1)}, bf16[3,2,128,128]{3,2,1,0:T(8,128)(2,1)S(1)}, u32[]{:S(2)}, u32[]{:S(2)}) collective-permute-start(bf16[3,2,128,128]{3,2,1,0:T(8,128)(2,1)S(1)} %add_convert_fusion.1), channel_id=1, source_target_pairs={{0,2},{1,3},{2,0},{3,1},{4,6},{5,7},{6,4},{7,5},{8,10},{9,11},{10,... | collective-permute-start | bytes 589832 | tf_op jit(solution)/shard_map/ppermute | solution.py:22
  105.9 14.0 %collective-permute-start.17 = (bf16[3,2,256,128]{3,2,1,0:T(8,128)(2,1)S(1)}, bf16[3,2,256,128]{3,2,1,0:T(8,128)(2,1)S(1)}, u32[]{:S(2)}, u32[]{:S(2)}) collective-permute-start(bf16[3,2,256,128]{3,2,1,0:T(8,128)(2,1)S(1)} %pad_maximum_fusion.1), channel_id=1, source_target_pairs={{0,1},{1,0},{2,3},{3,2},{4,5},{5,4},{6,7},{7,6},{8,9},{9,8},{10,11... | collective-permute-start | bytes 1179656 | tf_op jit(solution)/shard_map/ppermute | solution.py:22
  109.4 10.4 %collective-permute-start.22 = (bf16[3,2,128,128]{3,2,1,0:T(8,128)(2,1)S(1)}, bf16[3,2,128,128]{3,2,1,0:T(8,128)(2,1)S(1)}, u32[]{:S(2)}, u32[]{:S(2)}) collective-permute-start(bf16[3,2,128,128]{3,2,1,0:T(8,128)(2,1)S(1)} %add_convert_fusion), channel_id=1, source_target_pairs={{0,4},{1,5},{2,6},{3,7},{4,0},{5,1},{6,2},{7,3},{8,12},{9,13},{10,... | collective-permute-start | bytes 589832 | tf_op jit(solution)/shard_map/ppermute | solution.py:22
  110.4 6.8 %collective-permute-start.20 = (bf16[3,2,128,128]{3,2,1,0:T(8,128)(2,1)S(1)}, bf16[3,2,128,128]{3,2,1,0:T(8,128)(2,1)S(1)}, u32[]{:S(2)}, u32[]{:S(2)}) collective-permute-start(bf16[3,2,128,128]{3,2,1,0:T(8,128)(2,1)S(1)} %select_convert_fusion.1), channel_id=1, source_target_pairs={{0,2},{1,3},{2,0},{3,1},{4,6},{5,7},{6,4},{7,5},{8,10},{9,11},{10,... | collective-permute-start | bytes 589832 | tf_op jit(solution)/shard_map/ppermute | solution.py:22
  117.3 14.2 %collective-permute-start.21 = (bf16[3,2,256,128]{3,2,1,0:T(8,128)(2,1)S(1)}, bf16[3,2,256,128]{3,2,1,0:T(8,128)(2,1)S(1)}, u32[]{:S(2)}, u32[]{:S(2)}) collective-permute-start(bf16[3,2,256,128]{3,2,1,0:T(8,128)(2,1)S(1)} %pad_maximum_fusion.2), channel_id=1, source_target_pairs={{0,1},{1,0},{2,3},{3,2},{4,5},{5,4},{6,7},{7,6},{8,9},{9,8},{10,11... | collective-permute-start | bytes 1179656 | tf_op jit(solution)/shard_map/ppermute | solution.py:22
  119.9 5.7 %collective-permute-start.23 = (bf16[3,2,128,128]{3,2,1,0:T(8,128)(2,1)S(1)}, bf16[3,2,128,128]{3,2,1,0:T(8,128)(2,1)S(1)}, u32[]{:S(2)}, u32[]{:S(2)}) collective-permute-start(bf16[3,2,128,128]{3,2,1,0:T(8,128)(2,1)S(1)} %select_convert_fusion), channel_id=1, source_target_pairs={{0,2},{1,3},{2,0},{3,1},{4,6},{5,7},{6,4},{7,5},{8,10},{9,11},{10,... | collective-permute-start | bytes 589832 | tf_op jit(solution)/shard_map/ppermute | solution.py:22
  125.8 11.2 %collective-permute-start.25 = (bf16[1,2,256,128]{3,2,1,0:T(8,128)(2,1)S(1)}, bf16[1,2,256,128]{3,2,1,0:T(8,128)(2,1)S(1)}, u32[]{:S(2)}, u32[]{:S(2)}) collective-permute-start(bf16[1,2,256,128]{3,2,1,0:T(8,128)(2,1)S(1)} %get-tuple-element.105), channel_id=1, source_target_pairs={{0,1},{1,0},{2,3},{3,2},{4,5},{5,4},{6,7},{7,6},{8,9},{9,8},{10,11... | collective-permute-start | bytes 393224 | tf_op jit(solution)/shard_map/ppermute | solution.py:22
  127.9 14.4 %collective-permute-start.24 = (bf16[1,2,256,128]{3,2,1,0:T(8,128)(2,1)S(1)}, bf16[1,2,256,128]{3,2,1,0:T(8,128)(2,1)S(1)}, u32[]{:S(2)}, u32[]{:S(2)}) collective-permute-start(bf16[1,2,256,128]{3,2,1,0:T(8,128)(2,1)S(1)} %get-tuple-element.104), channel_id=1, source_target_pairs={{0,1},{1,0},{2,3},{3,2},{4,5},{5,4},{6,7},{7,6},{8,9},{9,8},{10,11... | collective-permute-start | bytes 393224 | tf_op jit(solution)/shard_map/ppermute | solution.py:22
  (28 other events, 211.7 us)

commit v4 on v3

--- a/solution.py
+++ b/solution.py
@@ -8,12 +8,15 @@
 from jax.sharding import PartitionSpec as P
 
 SMALL_COST = pl.CostEstimate(flops=1, bytes_accessed=1, transcendentals=0)
-VMEM_LIMIT = 24 * 1024 * 1024
+OVERLAP_VMEM = 8
+MIX_VMEM = 14
 TRANSFERS = (2, 2)
 KERNEL, NEAR, FAR, LATENCY = 0.4, 0.4, 0.8, 0.25
 EARLY = 0.1
+WAIT = 0.4
+PIECES, STEPS = 2, 2
+KERNEL_SUMS = 1
 TIES = (1, 1, 1)
-WAIT = 0.4
 TURNED = ()
 
 
@@ -90,15 +93,42 @@
             jax.ShapeDtypeStruct((q_count, 2, rows, width), jnp.float32),
             jax.ShapeDtypeStruct((q_count, 2, width, points), jnp.bfloat16),
         ],
-        compiler_params=pltpu.CompilerParams(vmem_limit_bytes=VMEM_LIMIT),
+        compiler_params=pltpu.CompilerParams(vmem_limit_bytes=OVERLAP_VMEM << 20),
         cost_estimate=SMALL_COST,
     )(picks, half, *arrays)
+
+
+def sum_kernel(half_ref, keep_ref, arriving_ref, *outs):
+    if len(outs) == 1:
+        outs[0][...] = (keep_ref[...] + arriving_ref[...].astype(jnp.float32)).astype(jnp.bfloat16)
+        return
+    rows = outs[0].shape[2]
+    for out, part in zip(outs, (half_ref[0], 1 - half_ref[0])):
+        at = pl.ds(pl.multiple_of(part * rows, rows), rows)
+        out[...] = (keep_ref[:, :, at, :] + arriving_ref[:, :, at, :].astype(jnp.float32)).astype(out.dtype)
+
+
+def partial_sum(keep, arriving, half, full):
+    count, two, rows, width = keep.shape
+    part = rows if full else rows // 2
+    whole = pl.BlockSpec((1, two, rows, width), lambda q, h: (q, 0, 0, 0))
+    out = pl.BlockSpec((1, two, part, width), lambda q, h: (q, 0, 0, 0))
+    types = [jnp.bfloat16] if full else [jnp.bfloat16, jnp.float32]
+    return pl.pallas_call(
+        sum_kernel,
+        grid_spec=pltpu.PrefetchScalarGridSpec(
+            num_scalar_prefetch=1, grid=(count,), in_specs=[whole, whole], out_specs=[out] * len(types)
+        ),
+        out_shape=[jax.ShapeDtypeStruct((count, two, part, width), dtype) for dtype in types],
+        compiler_params=pltpu.CompilerParams(vmem_limit_bytes=OVERLAP_VMEM << 20),
+        cost_estimate=SMALL_COST,
+    )(half, keep, arriving)
 
 
 def mix_kernel(places, density_scale, count_ref, field_ref, own_ref, *refs):
     weights = refs[:len(places)]
     partners = refs[len(places):2 * len(places)]
-    source_ref, density_ref, left_real, left_imag, right = refs[-5:]
+    source_ref, density_ref, left, right = refs[-4:]
     bands = own_ref.shape[1]
 
     @pl.when(pl.program_id(0) == 0)
@@ -108,10 +138,10 @@
             width = weight.shape[3]
             near, far = pl.ds(start, width), pl.ds(start + width, width)
             start += 2 * width
-            left_real[:, near] = weight[0, 0]
-            left_real[:, far] = -weight[0, 1]
-            left_imag[:, near] = weight[0, 1]
-            left_imag[:, far] = weight[0, 0]
+            left[:bands, near] = weight[0, 0]
+            left[:bands, far] = -weight[0, 1]
+            left[bands:, near] = weight[0, 1]
+            left[bands:, far] = weight[0, 0]
 
     start = 0
     block = right.shape[1]
@@ -120,24 +150,28 @@
         width = 2 * partner.shape[2]
         right[pl.ds(start, width), :] = partner[at, :, :, here].reshape(width, block)
         start += width
-    u, v = field_ref[0, 0:1], field_ref[0, 1:2]
-    a, b = own_ref[0, :, here].astype(jnp.float32), own_ref[1, :, here].astype(jnp.float32)
-    applied_real = (u * a - v * b).astype(jnp.bfloat16).astype(jnp.float32)
-    applied_imag = (u * b + v * a).astype(jnp.bfloat16).astype(jnp.float32)
-    real = applied_real - jnp.dot(left_real[...], right[...], preferred_element_type=jnp.float32)
-    imag = applied_imag - jnp.dot(left_imag[...], right[...], preferred_element_type=jnp.float32)
-    source_ref[0, 0, 0] = real.astype(jnp.bfloat16)
-    source_ref[0, 0, 1] = imag.astype(jnp.bfloat16)
-    term = a * real + b * imag
-    ids = lax.broadcasted_iota(jnp.int32, (bands, 1), 0)
-    term = jnp.where(ids < count_ref[0], term, 0.0)
-    density_ref[...] = density_scale * jnp.sum(term, axis=0, keepdims=True)
+    piece = block // PIECES
+    keep = lax.broadcasted_iota(jnp.int32, (bands, 1), 0) < count_ref[0]
+    for n in range(PIECES):
+        at = pl.ds(n * piece, piece)
+        there = pl.ds(pl.multiple_of(pl.program_id(0) * block + n * piece, piece), piece)
+        u, v = field_ref[0, 0:1, at], field_ref[0, 1:2, at]
+        a, b = own_ref[0, :, there].astype(jnp.float32), own_ref[1, :, there].astype(jnp.float32)
+        applied_real = (u * a - v * b).astype(jnp.bfloat16).astype(jnp.float32)
+        applied_imag = (u * b + v * a).astype(jnp.bfloat16).astype(jnp.float32)
+        mixed = jnp.dot(left[...], right[:, at], preferred_element_type=jnp.float32)
+        real = applied_real - mixed[:bands]
+        imag = applied_imag - mixed[bands:]
+        source_ref[0, 0, 0, :, at] = real.astype(jnp.bfloat16)
+        source_ref[0, 0, 1, :, at] = imag.astype(jnp.bfloat16)
+        term = jnp.where(keep, a * real + b * imag, 0.0)
+        density_ref[:, at] = density_scale * jnp.sum(term, axis=0, keepdims=True)
 
 
 def mix(q, count, potential, orbitals, partners, weights, buffer, density_scale):
     q_total = potential.shape[0]
     _, bands, points = orbitals.shape
-    block = points // 2
+    block = points // STEPS
     in_vmem = pl.BlockSpec(memory_space=pltpu.VMEM)
     specs = [
         pl.BlockSpec((1, 2, block), lambda i, c: (q, 0, i)),
@@ -161,15 +195,17 @@
                 pl.BlockSpec((1, 1, 2, bands, block), lambda i, c: (q, 0, 0, 0, i)),
                 pl.BlockSpec((1, block), lambda i, c: (0, i)),
             ],
-            scratch_shapes=[pltpu.VMEM((bands, 2 * bands), jnp.bfloat16)] * 2
-            + [pltpu.VMEM((2 * bands, block), jnp.bfloat16)],
+            scratch_shapes=[
+                pltpu.VMEM((2 * bands, 2 * bands), jnp.bfloat16),
+                pltpu.VMEM((2 * bands, block), jnp.bfloat16),
+            ],
         ),
         out_shape=[
             jax.ShapeDtypeStruct((q_total, 1, 2, bands, points), jnp.bfloat16),
             jax.ShapeDtypeStruct((1, points), jnp.float32),
         ],
         input_output_aliases=aliases,
-        compiler_params=pltpu.CompilerParams(vmem_limit_bytes=VMEM_LIMIT),
+        compiler_params=pltpu.CompilerParams(vmem_limit_bytes=MIX_VMEM << 20),
         cost_estimate=SMALL_COST,
     )(count, *arrays)
 
@@ -251,7 +287,10 @@
                 arriving, which * half, half, 2
             ).astype(jnp.float32)
 
-        if full:
+        if (KERNEL_SUMS >> full) & 1:
+            leaving, *rest = partial_sum(keep, arriving, 1 - mine[None], full)
+            kept = rest[0] if rest else leaving
+        elif full:
             leaving = (keep + arriving.astype(jnp.float32)).astype(jnp.bfloat16)
             kept = leaving
         else:

time: 153 us -> 152 us (level)
  other arithmetic: 10.3 us -> 3.22 us
  starting transfers between devices: 31.3 us -> 34.4 us
  local copies, waits for them, and re-layouts: 7.84 us -> 10.8 us
  Pallas kernels: 38.5 us -> 41.3 us
  waiting for transfers between devices: 64 us -> 61.2 us
    pallas_call x0 -> x4, Pallas kernels: none -> 4 us  [partial_sum(): pl.pallas_call(sum_kernel, grid_spec=pltpu.PrefetchScalarGridSpec(num_sca...]
    convert_element_type x4 -> x0, other arithmetic: 3.77 us -> none  [run_scatter(): leaving = part(1 - mine).astype(jnp.bfloat16)]
    convert_element_type x4, other arithmetic: 3.49 us -> 0.18 us  [run_scatter(): leaving = (keep + arriving.astype(jnp.float32)).astype(jnp.bfloat16)]
    ppermute x30, starting transfers between devices: 31.3 us -> 34.4 us  [swap(): return lax.ppermute(value, axis, [(i, i ^ bit) for i in range(size)])]
    unnamed x44 -> x38, local copies, waits for them, and re-layouts: 5.29 us -> 8.29 us
    ppermute x30, waiting for transfers between devices: 64 us -> 61.2 us  [swap(): return lax.ppermute(value, axis, [(i, i ^ bit) for i in range(size)])]
  transfers between devices with their start and end apart: 30 -> 30, of which waited for: 13 -> 13; matrix products, arithmetic and copies ran while one was open for 6% -> 2% of each run, Pallas kernels for 22% -> 24%
where the time goes in v4:
time: 152 us
  waiting for transfers between devices  61.2 us (40%)
  Pallas kernels  41.3 us (27%)
  starting transfers between devices  34.4 us (23%)
  local copies, waits for them, and re-layouts  10.8 us (7%)
  other arithmetic  3.22 us (2%)
    ppermute x30, waiting for transfers between devices, swap(): return lax.ppermute(value, axis, [(i, i ^ bit) for i in range(size)])  61.2 us
    ppermute x30, starting transfers between devices, swap(): return lax.ppermute(value, axis, [(i, i ^ bit) for i in range(size)])  34.4 us
    pallas_call x4, Pallas kernels, overlap(): pl.pallas_call(functools.partial(overlap_kernel, [offset for _, offset in...  21.6 us
    pallas_call x3, Pallas kernels, mix(): pl.pallas_call(functools.partial(mix_kernel, [at for at, _ in partners],...  15.8 us
    unnamed x38, local copies, waits for them, and re-layouts  8.29 us
    pallas_call x4, Pallas kernels, partial_sum(): pl.pallas_call(sum_kernel, grid_spec=pltpu.PrefetchScalarGridSpec(num_sca...  4 us
  transfers between devices with their start and end apart: 30, of which 13 were waited for; matrix products, arithmetic and copies ran while one was open for 2% of the time, Pallas kernels for 24%

profile of v4, /device:TPU:0, one launch (start us, length us, event | category | flops | bytes accessed | tf_op | source)
XLA Modules:
  0.0 152.0 jit_solution(8547186242868493249)
XLA Ops:
  2.1 3.0 %collective-permute-start.1 = (bf16[2,256,1024]{2,1,0:T(8,128)(2,1)S(1)}, bf16[2,256,1024]{2,1,0:T(8,128)(2,1)}, u32[]{:S(2)}, u32[]{:S(2)}) collective-permute-start(bf16[2,256,1024]{2,1,0:T(8,128)(2,1)S(1)} %slice.56), channel_id=1, source_target_pairs={{0,16},{8,24},{16,0},{24,8},{1,17},{9,25},{17,1},{25,9},{2,18},{10... | collective-permute-start | bytes 3145736 | tf_op jit(solution)/shard_map/ppermute | solution.py:25
  5.8 22.6 %collective-permute-done.1.refs_2_ = bf16[2,256,1024]{2,1,0:T(8,128)(2,1)} collective-permute-done((bf16[2,256,1024]{2,1,0:T(8,128)(2,1)S(1)}, bf16[2,256,1024]{2,1,0:T(8,128)(2,1)}, u32[]{:S(2)}, u32[]{:S(2)}) %collective-permute-start.1) | collective-permute-done | bytes 1048608 | tf_op jit(solution)/shard_map/ppermute | solution.py:25
  31.4 6.0 %shard_map.59 = (bf16[3,2,256,128]{3,2,1,0:T(8,128)(2,1)}, f32[3,2,256,128]{3,2,1,0:T(8,128)S(1)}, bf16[3,2,128,1024]{3,2,1,0:T(8,128)(2,1)S(1)}) custom-call(s32[3]{0:T(128)S(1)} %broadcast_xor_fusion.picks_ref, s32[1]{0:T(128)} %bitcast.3.half_ref, bf16[2,512,1024]{2,1,0:T(8,128)(2,1)S(1)} %bitcast.7, f32[3,2,1024]{2,1,0:T(2,128)S(1)} %copy-done.9, ...), custom_call_target="tpu_custom_call" | custom-call | flops 1 | bytes 1 | tf_op jit(solution)/shard_map/pallas_call | solution.py:71
  41.2 5.3 %shard_map.60 = (bf16[3,2,256,128]{3,2,1,0:T(8,128)(2,1)S(1)}, f32[3,2,256,128]{3,2,1,0:T(8,128)S(1)}, bf16[3,2,128,1024]{3,2,1,0:T(8,128)(2,1)S(1)}) custom-call(s32[3]{0:T(128)S(1)} %broadcast_xor_fusion.picks_ref, s32[1]{0:T(128)} %bitcast.3.half_ref, bf16[2,512,1024]{2,1,0:T(8,128)(2,1)S(1)} %bitcast.9, f32[3,2,1024]{2,1,0:T(2,128)S(1)} %copy-done.9, ...), custom_call_target="tpu_custom_call" | custom-call | flops 1 | bytes 1 | tf_op jit(solution)/shard_map/pallas_call | solution.py:71
  47.7 3.3 %collective-permute-done.3.arriving_ref = bf16[3,2,256,128]{3,2,1,0:T(8,128)(2,1)} collective-permute-done((bf16[3,2,256,128]{3,2,1,0:T(8,128)(2,1)}, bf16[3,2,256,128]{3,2,1,0:T(8,128)(2,1)}, u32[]{:S(2)}, u32[]{:S(2)}) %collective-permute-start.3) | collective-permute-done | bytes 393248 | tf_op jit(solution)/shard_map/ppermute | solution.py:25
  51.0 1.9 %shard_map.61 = (bf16[3,2,128,128]{3,2,1,0:T(8,128)(2,1)S(1)}, f32[3,2,128,128]{3,2,1,0:T(8,128)S(1)}) custom-call(s32[1]{0:T(128)} %bitcast.2.half_ref, f32[3,2,256,128]{3,2,1,0:T(8,128)S(1)} %copy-done.15, bf16[3,2,256,128]{3,2,1,0:T(8,128)(2,1)} %collective-permute-done.3.arriving_ref), custom_call_target="tpu_custom_call" | custom-call | flops 1 | bytes 1 | tf_op jit(solution)/shard_map/pallas_call | solution.py:117
  52.9 2.4 %collective-permute-done.5.refs_2_ = bf16[2,256,1024]{2,1,0:T(8,128)(2,1)S(1)} collective-permute-done((bf16[2,256,1024]{2,1,0:T(8,128)(2,1)}, bf16[2,256,1024]{2,1,0:T(8,128)(2,1)S(1)}, u32[]{:S(2)}, u32[]{:S(2)}) %collective-permute-start.5) | collective-permute-done | bytes 1048608 | tf_op jit(solution)/shard_map/ppermute | solution.py:25
  58.8 5.4 %shard_map.62 = (bf16[3,2,256,128]{3,2,1,0:T(8,128)(2,1)}, f32[3,2,256,128]{3,2,1,0:T(8,128)S(1)}, bf16[3,2,128,1024]{3,2,1,0:T(8,128)(2,1)S(1)}) custom-call(s32[3]{0:T(128)S(1)} %broadcast_xor_fusion.picks_ref, s32[1]{0:T(128)} %bitcast.3.half_ref, bf16[2,512,1024]{2,1,0:T(8,128)(2,1)S(1)} %bitcast.11, f32[3,2,1024]{2,1,0:T(2,128)S(1)} %copy-done.9, ...), custom_call_target="tpu_custom_call" | custom-call | flops 1 | bytes 1 | tf_op jit(solution)/shard_map/pallas_call | solution.py:71
  66.9 1.9 %collective-permute-start.9 = (bf16[3,2,128,128]{3,2,1,0:T(8,128)(2,1)S(1)}, bf16[3,2,128,128]{3,2,1,0:T(8,128)(2,1)S(1)}, u32[]{:S(2)}, u32[]{:S(2)}) collective-permute-start(bf16[3,2,128,128]{3,2,1,0:T(8,128)(2,1)S(1)} %get-tuple-element.70), channel_id=1, source_target_pairs={{0,2},{1,3},{2,0},{3,1},{4,6},{5,7},{6,4},{7,5},{8,10},{9,11},{10,... | collective-permute-start | bytes 589832 | tf_op jit(solution)/shard_map/ppermute | solution.py:25
  68.9 2.6 %collective-permute-start.7 = (bf16[3,2,128,128]{3,2,1,0:T(8,128)(2,1)S(1)}, bf16[3,2,128,128]{3,2,1,0:T(8,128)(2,1)S(1)}, u32[]{:S(2)}, u32[]{:S(2)}) collective-permute-start(bf16[3,2,128,128]{3,2,1,0:T(8,128)(2,1)S(1)} %add_convert_fusion.3), channel_id=1, source_target_pairs={{0,4},{1,5},{2,6},{3,7},{4,0},{5,1},{6,2},{7,3},{8,12},{9,13},{10,... | collective-permute-start | bytes 589832 | tf_op jit(solution)/shard_map/ppermute | solution.py:25
  73.0 4.8 %shard_map.64 = (bf16[3,2,256,128]{3,2,1,0:T(8,128)(2,1)S(1)}, f32[3,2,256,128]{3,2,1,0:T(8,128)S(1)}, bf16[3,2,128,1024]{3,2,1,0:T(8,128)(2,1)S(1)}) custom-call(s32[3]{0:T(128)S(1)} %broadcast_xor_fusion.picks_ref, s32[1]{0:T(128)} %bitcast.3.half_ref, bf16[2,512,1024]{2,1,0:T(8,128)(2,1)S(1)} %bitcast.13, f32[3,2,1024]{2,1,0:T(2,128)S(1)} %copy-done.9, ...), custom_call_target="tpu_custom_call" | custom-call | flops 1 | bytes 1 | tf_op jit(solution)/shard_map/pallas_call | solution.py:71
  82.4 2.7 %collective-permute-start.13 = (bf16[3,2,128,128]{3,2,1,0:T(8,128)(2,1)S(1)}, bf16[3,2,128,128]{3,2,1,0:T(8,128)(2,1)S(1)}, u32[]{:S(2)}, u32[]{:S(2)}) collective-permute-start(bf16[3,2,128,128]{3,2,1,0:T(8,128)(2,1)S(1)} %add_convert_fusion.2), channel_id=1, source_target_pairs={{0,4},{1,5},{2,6},{3,7},{4,0},{5,1},{6,2},{7,3},{8,12},{9,13},{10,... | collective-permute-start | bytes 589832 | tf_op jit(solution)/shard_map/ppermute | solution.py:25
  86.2 1.9 %shard_map.65 = (bf16[3,2,128,128]{3,2,1,0:T(8,128)(2,1)S(1)}, f32[3,2,128,128]{3,2,1,0:T(8,128)S(1)}) custom-call(s32[1]{0:T(128)} %bitcast.2.half_ref, f32[3,2,256,128]{3,2,1,0:T(8,128)S(1)} %copy-done.13, bf16[3,2,256,128]{3,2,1,0:T(8,128)(2,1)} %collective-permute-done.11.arriving_ref), custom_call_target="tpu_custom_call" | custom-call | flops 1 | bytes 1 | tf_op jit(solution)/shard_map/pallas_call | solution.py:117
  88.3 3.9 %collective-permute-done.10 = bf16[3,2,128,128]{3,2,1,0:T(8,128)(2,1)S(1)} collective-permute-done((bf16[3,2,128,128]{3,2,1,0:T(8,128)(2,1)S(1)}, bf16[3,2,128,128]{3,2,1,0:T(8,128)(2,1)S(1)}, u32[]{:S(2)}, u32[]{:S(2)}) %collective-permute-start.10) | collective-permute-done | bytes 196640 | tf_op jit(solution)/shard_map/ppermute | solution.py:25
  93.5 2.9 %collective-permute-done.16 = bf16[3,2,128,128]{3,2,1,0:T(8,128)(2,1)S(1)} collective-permute-done((bf16[3,2,128,128]{3,2,1,0:T(8,128)(2,1)S(1)}, bf16[3,2,128,128]{3,2,1,0:T(8,128)(2,1)S(1)}, u32[]{:S(2)}, u32[]{:S(2)}) %collective-permute-start.16) | collective-permute-done | bytes 196640 | tf_op jit(solution)/shard_map/ppermute | solution.py:25
  98.3 6.8 %collective-permute-done.14 = bf16[3,2,128,128]{3,2,1,0:T(8,128)(2,1)S(1)} collective-permute-done((bf16[3,2,128,128]{3,2,1,0:T(8,128)(2,1)S(1)}, bf16[3,2,128,128]{3,2,1,0:T(8,128)(2,1)S(1)}, u32[]{:S(2)}, u32[]{:S(2)}) %collective-permute-start.14) | collective-permute-done | bytes 196640 | tf_op jit(solution)/shard_map/ppermute | solution.py:25
  109.7 5.8 %collective-permute-done.20 = bf16[3,2,128,128]{3,2,1,0:T(8,128)(2,1)S(1)} collective-permute-done((bf16[3,2,128,128]{3,2,1,0:T(8,128)(2,1)S(1)}, bf16[3,2,128,128]{3,2,1,0:T(8,128)(2,1)S(1)}, u32[]{:S(2)}, u32[]{:S(2)}) %collective-permute-start.20) | collective-permute-done | bytes 196640 | tf_op jit(solution)/shard_map/ppermute | solution.py:25
  115.5 3.4 %collective-permute-start.21 = (bf16[3,2,256,128]{3,2,1,0:T(8,128)(2,1)S(1)}, bf16[3,2,256,128]{3,2,1,0:T(8,128)(2,1)S(1)}, u32[]{:S(2)}, u32[]{:S(2)}) collective-permute-start(bf16[3,2,256,128]{3,2,1,0:T(8,128)(2,1)S(1)} %pad_maximum_fusion.2), channel_id=1, source_target_pairs={{0,1},{1,0},{2,3},{3,2},{4,5},{5,4},{6,7},{7,6},{8,9},{9,8},{10,11... | collective-permute-start | bytes 1179656 | tf_op jit(solution)/shard_map/ppermute | solution.py:25
  119.5 5.3 %collective-permute-done.23 = bf16[3,2,128,128]{3,2,1,0:T(8,128)(2,1)S(1)} collective-permute-done((bf16[3,2,128,128]{3,2,1,0:T(8,128)(2,1)S(1)}, bf16[3,2,128,128]{3,2,1,0:T(8,128)(2,1)S(1)}, u32[]{:S(2)}, u32[]{:S(2)}) %collective-permute-start.23) | collective-permute-done | bytes 196640 | tf_op jit(solution)/shard_map/ppermute | solution.py:25
  125.1 2.1 %collective-permute-start.25 = (bf16[1,2,256,128]{3,2,1,0:T(8,128)(2,1)S(1)}, bf16[1,2,256,128]{3,2,1,0:T(8,128)(2,1)S(1)}, u32[]{:S(2)}, u32[]{:S(2)}) collective-permute-start(bf16[1,2,256,128]{3,2,1,0:T(8,128)(2,1)S(1)} %get-tuple-element.121), channel_id=1, source_target_pairs={{0,1},{1,0},{2,3},{3,2},{4,5},{5,4},{6,7},{7,6},{8,9},{9,8},{10,11... | collective-permute-start | bytes 393224 | tf_op jit(solution)/shard_map/ppermute | solution.py:25
  127.2 3.1 %collective-permute-done.26 = bf16[1,2,256,128]{3,2,1,0:T(8,128)(2,1)S(1)} collective-permute-done((bf16[1,2,256,128]{3,2,1,0:T(8,128)(2,1)S(1)}, bf16[1,2,256,128]{3,2,1,0:T(8,128)(2,1)S(1)}, u32[]{:S(2)}, u32[]{:S(2)}) %collective-permute-start.26) | collective-permute-done | bytes 131104 | tf_op jit(solution)/shard_map/ppermute | solution.py:25
  130.7 5.3 %shard_map.67 = (bf16[3,1,2,512,1024]{4,3,2,1,0:T(8,128)(2,1)}, f32[1,1024]{1,0:T(1,128)S(1)}) custom-call(s32[1]{0:T(128)} %bitcast.count_ref, f32[3,2,1024]{2,1,0:T(2,128)S(1)} %copy-done.9, bf16[2,512,1024]{2,1,0:T(8,128)(2,1)S(1)} %bitcast.15, bf16[1,2,512,128]{3,2,1,0:T(8,128)(2,1)S(1)} %get-tuple-element.110.refs_0_, ...), custom_call_target="tpu_custom_call" | custom-call | flops 1 | bytes 1 | tf_op jit(solution)/shard_map/pallas_call | solution.py:188
  136.0 5.3 %shard_map.68 = (bf16[3,1,2,512,1024]{4,3,2,1,0:T(8,128)(2,1)}, f32[1,1024]{1,0:T(1,128)S(1)}) custom-call(s32[1]{0:T(128)} %bitcast.count_ref, f32[3,2,1024]{2,1,0:T(2,128)S(1)} %copy-done.9, bf16[2,512,1024]{2,1,0:T(8,128)(2,1)S(1)} %bitcast.16, bf16[1,2,512,128]{3,2,1,0:T(8,128)(2,1)S(1)} %get-tuple-element.112.refs_0_, ...), custom_call_target="tpu_custom_call", output_to_operand_aliasing={{0}: (11, {})} | custom-call | flops 1 | bytes 1 | tf_op jit(solution)/shard_map/pallas_call | solution.py:188
  141.3 5.3 %shard_map.69 = (bf16[3,1,2,512,1024]{4,3,2,1,0:T(8,128)(2,1)}, f32[1,1024]{1,0:T(1,128)S(1)}) custom-call(s32[1]{0:T(128)} %bitcast.count_ref, f32[3,2,1024]{2,1,0:T(2,128)S(1)} %copy-done.9, bf16[2,512,1024]{2,1,0:T(8,128)(2,1)S(1)} %bitcast.17, bf16[1,2,512,128]{3,2,1,0:T(8,128)(2,1)S(1)} %get-tuple-element.111.refs_0_, ...), custom_call_target="tpu_custom_call", output_to_operand_aliasing={{0}: (11, {})} | custom-call | flops 1 | bytes 1 | tf_op jit(solution)/shard_map/pallas_call | solution.py:188
  (125 shorter events, 38.0 us)
Async XLA Ops:
  2.1 26.3 %collective-permute-start.1 = (bf16[2,256,1024]{2,1,0:T(8,128)(2,1)S(1)}, bf16[2,256,1024]{2,1,0:T(8,128)(2,1)}, u32[]{:S(2)}, u32[]{:S(2)}) collective-permute-start(bf16[2,256,1024]{2,1,0:T(8,128)(2,1)S(1)} %slice.56), channel_id=1, source_target_pairs={{0,16},{8,24},{16,0},{24,8},{1,17},{9,25},{17,1},{25,9},{2,18},{10... | collective-permute-start | bytes 3145736 | tf_op jit(solution)/shard_map/ppermute | solution.py:25
  5.1 26.3 %collective-permute-start = (bf16[2,512,1024]{2,1,0:T(8,128)(2,1)S(1)}, bf16[2,512,1024]{2,1,0:T(8,128)(2,1)}, u32[]{:S(2)}, u32[]{:S(2)}) collective-permute-start(bf16[2,512,1024]{2,1,0:T(8,128)(2,1)S(1)} %bitcast.5), channel_id=1, source_target_pairs={{0,8},{8,0},{16,24},{24,16},{1,9},{9,1},{17,25},{25,17},{2,10},{10... | collective-permute-start | bytes 6291464 | tf_op jit(solution)/shard_map/ppermute | solution.py:25
  29.5 25.8 %collective-permute-start.5 = (bf16[2,256,1024]{2,1,0:T(8,128)(2,1)}, bf16[2,256,1024]{2,1,0:T(8,128)(2,1)S(1)}, u32[]{:S(2)}, u32[]{:S(2)}) collective-permute-start(bf16[2,256,1024]{2,1,0:T(8,128)(2,1)} %slice.43), channel_id=1, source_target_pairs={{0,16},{8,24},{16,0},{24,8},{1,17},{9,25},{17,1},{25,9},{2,18},{10... | collective-permute-start | bytes 3145736 | tf_op jit(solution)/shard_map/ppermute | solution.py:25
  39.4 11.6 %collective-permute-start.3 = (bf16[3,2,256,128]{3,2,1,0:T(8,128)(2,1)}, bf16[3,2,256,128]{3,2,1,0:T(8,128)(2,1)}, u32[]{:S(2)}, u32[]{:S(2)}) collective-permute-start(bf16[3,2,256,128]{3,2,1,0:T(8,128)(2,1)} %get-tuple-element.56), channel_id=1, source_target_pairs={{0,1},{1,0},{2,3},{3,2},{4,5},{5,4},{6,7},{7,6},{8,9},{9,8},{10,11... | collective-permute-start | bytes 1179656 | tf_op jit(solution)/shard_map/ppermute | solution.py:25
  55.3 11.6 %collective-permute-start.8 = (bf16[3,2,256,128]{3,2,1,0:T(8,128)(2,1)S(1)}, bf16[3,2,256,128]{3,2,1,0:T(8,128)(2,1)S(1)}, u32[]{:S(2)}, u32[]{:S(2)}) collective-permute-start(bf16[3,2,256,128]{3,2,1,0:T(8,128)(2,1)S(1)} %get-tuple-element.58), channel_id=1, source_target_pairs={{0,1},{1,0},{2,3},{3,2},{4,5},{5,4},{6,7},{7,6},{8,9},{9,8},{10,11... | collective-permute-start | bytes 1179656 | tf_op jit(solution)/shard_map/ppermute | solution.py:25
  57.0 8.4 %collective-permute-start.4 = (bf16[3,2,128,128]{3,2,1,0:T(8,128)(2,1)S(1)}, bf16[3,2,128,128]{3,2,1,0:T(8,128)(2,1)S(1)}, u32[]{:S(2)}, u32[]{:S(2)}) collective-permute-start(bf16[3,2,128,128]{3,2,1,0:T(8,128)(2,1)S(1)} %get-tuple-element.61), channel_id=1, source_target_pairs={{0,2},{1,3},{2,0},{3,1},{4,6},{5,7},{6,4},{7,5},{8,10},{9,11},{10,... | collective-permute-start | bytes 589832 | tf_op jit(solution)/shard_map/ppermute | solution.py:25
  66.9 13.6 %collective-permute-start.9 = (bf16[3,2,128,128]{3,2,1,0:T(8,128)(2,1)S(1)}, bf16[3,2,128,128]{3,2,1,0:T(8,128)(2,1)S(1)}, u32[]{:S(2)}, u32[]{:S(2)}) collective-permute-start(bf16[3,2,128,128]{3,2,1,0:T(8,128)(2,1)S(1)} %get-tuple-element.70), channel_id=1, source_target_pairs={{0,2},{1,3},{2,0},{3,1},{4,6},{5,7},{6,4},{7,5},{8,10},{9,11},{10,... | collective-permute-start | bytes 589832 | tf_op jit(solution)/shard_map/ppermute | solution.py:25
  68.9 11.8 %collective-permute-start.7 = (bf16[3,2,128,128]{3,2,1,0:T(8,128)(2,1)S(1)}, bf16[3,2,128,128]{3,2,1,0:T(8,128)(2,1)S(1)}, u32[]{:S(2)}, u32[]{:S(2)}) collective-permute-start(bf16[3,2,128,128]{3,2,1,0:T(8,128)(2,1)S(1)} %add_convert_fusion.3), channel_id=1, source_target_pairs={{0,4},{1,5},{2,6},{3,7},{4,0},{5,1},{6,2},{7,3},{8,12},{9,13},{10,... | collective-permute-start | bytes 589832 | tf_op jit(solution)/shard_map/ppermute | solution.py:25
  71.5 13.6 %collective-permute-start.11 = (bf16[3,2,256,128]{3,2,1,0:T(8,128)(2,1)}, bf16[3,2,256,128]{3,2,1,0:T(8,128)(2,1)}, u32[]{:S(2)}, u32[]{:S(2)}) collective-permute-start(bf16[3,2,256,128]{3,2,1,0:T(8,128)(2,1)} %get-tuple-element.65), channel_id=1, source_target_pairs={{0,1},{1,0},{2,3},{3,2},{4,5},{5,4},{6,7},{7,6},{8,9},{9,8},{10,11... | collective-permute-start | bytes 1179656 | tf_op jit(solution)/shard_map/ppermute | solution.py:25
  80.8 11.5 %collective-permute-start.10 = (bf16[3,2,128,128]{3,2,1,0:T(8,128)(2,1)S(1)}, bf16[3,2,128,128]{3,2,1,0:T(8,128)(2,1)S(1)}, u32[]{:S(2)}, u32[]{:S(2)}) collective-permute-start(bf16[3,2,128,128]{3,2,1,0:T(8,128)(2,1)S(1)} %select_convert_fusion.3), channel_id=1, source_target_pairs={{0,2},{1,3},{2,0},{3,1},{4,6},{5,7},{6,4},{7,5},{8,10},{9,11},{10,... | collective-permute-start | bytes 589832 | tf_op jit(solution)/shard_map/ppermute | solution.py:25
  81.3 16.4 %collective-permute-start.15 = (bf16[3,2,256,128]{3,2,1,0:T(8,128)(2,1)}, bf16[3,2,256,128]{3,2,1,0:T(8,128)(2,1)S(1)}, u32[]{:S(2)}, u32[]{:S(2)}) collective-permute-start(bf16[3,2,256,128]{3,2,1,0:T(8,128)(2,1)} %copy-done.16), channel_id=1, source_target_pairs={{0,1},{1,0},{2,3},{3,2},{4,5},{5,4},{6,7},{7,6},{8,9},{9,8},{10,11... | collective-permute-start | bytes 1179656 | tf_op jit(solution)/shard_map/ppermute | solution.py:25
  82.4 10.6 %collective-permute-start.13 = (bf16[3,2,128,128]{3,2,1,0:T(8,128)(2,1)S(1)}, bf16[3,2,128,128]{3,2,1,0:T(8,128)(2,1)S(1)}, u32[]{:S(2)}, u32[]{:S(2)}) collective-permute-start(bf16[3,2,128,128]{3,2,1,0:T(8,128)(2,1)S(1)} %add_convert_fusion.2), channel_id=1, source_target_pairs={{0,4},{1,5},{2,6},{3,7},{4,0},{5,1},{6,2},{7,3},{8,12},{9,13},{10,... | collective-permute-start | bytes 589832 | tf_op jit(solution)/shard_map/ppermute | solution.py:25
  88.1 8.3 %collective-permute-start.16 = (bf16[3,2,128,128]{3,2,1,0:T(8,128)(2,1)S(1)}, bf16[3,2,128,128]{3,2,1,0:T(8,128)(2,1)S(1)}, u32[]{:S(2)}, u32[]{:S(2)}) collective-permute-start(bf16[3,2,128,128]{3,2,1,0:T(8,128)(2,1)S(1)} %get-tuple-element.77), channel_id=1, source_target_pairs={{0,2},{1,3},{2,0},{3,1},{4,6},{5,7},{6,4},{7,5},{8,10},{9,11},{10,... | collective-permute-start | bytes 589832 | tf_op jit(solution)/shard_map/ppermute | solution.py:25
  92.3 17.1 %collective-permute-start.12 = (bf16[3,2,256,128]{3,2,1,0:T(8,128)(2,1)S(1)}, bf16[3,2,256,128]{3,2,1,0:T(8,128)(2,1)S(1)}, u32[]{:S(2)}, u32[]{:S(2)}) collective-permute-start(bf16[3,2,256,128]{3,2,1,0:T(8,128)(2,1)S(1)} %pad_maximum_fusion), channel_id=1, source_target_pairs={{0,1},{1,0},{2,3},{3,2},{4,5},{5,4},{6,7},{7,6},{8,9},{9,8},{10,11... | collective-permute-start | bytes 1179656 | tf_op jit(solution)/shard_map/ppermute | solution.py:25
  93.0 12.0 %collective-permute-start.14 = (bf16[3,2,128,128]{3,2,1,0:T(8,128)(2,1)S(1)}, bf16[3,2,128,128]{3,2,1,0:T(8,128)(2,1)S(1)}, u32[]{:S(2)}, u32[]{:S(2)}) collective-permute-start(bf16[3,2,128,128]{3,2,1,0:T(8,128)(2,1)S(1)} %select_convert_fusion.2), channel_id=1, source_target_pairs={{0,2},{1,3},{2,0},{3,1},{4,6},{5,7},{6,4},{7,5},{8,10},{9,11},{10,... | collective-permute-start | bytes 589832 | tf_op jit(solution)/shard_map/ppermute | solution.py:25
  96.5 11.9 %collective-permute-start.18 = (bf16[3,2,128,128]{3,2,1,0:T(8,128)(2,1)S(1)}, bf16[3,2,128,128]{3,2,1,0:T(8,128)(2,1)S(1)}, u32[]{:S(2)}, u32[]{:S(2)}) collective-permute-start(bf16[3,2,128,128]{3,2,1,0:T(8,128)(2,1)S(1)} %add_convert_fusion.1), channel_id=1, source_target_pairs={{0,4},{1,5},{2,6},{3,7},{4,0},{5,1},{6,2},{7,3},{8,12},{9,13},{10,... | collective-permute-start | bytes 589832 | tf_op jit(solution)/shard_map/ppermute | solution.py:25
  97.8 9.7 %collective-permute-start.19 = (bf16[3,2,128,128]{3,2,1,0:T(8,128)(2,1)S(1)}, bf16[3,2,128,128]{3,2,1,0:T(8,128)(2,1)S(1)}, u32[]{:S(2)}, u32[]{:S(2)}) collective-permute-start(bf16[3,2,128,128]{3,2,1,0:T(8,128)(2,1)S(1)} %get-tuple-element.84), channel_id=1, source_target_pairs={{0,2},{1,3},{2,0},{3,1},{4,6},{5,7},{6,4},{7,5},{8,10},{9,11},{10,... | collective-permute-start | bytes 589832 | tf_op jit(solution)/shard_map/ppermute | solution.py:25
  105.1 14.2 %collective-permute-start.17 = (bf16[3,2,256,128]{3,2,1,0:T(8,128)(2,1)S(1)}, bf16[3,2,256,128]{3,2,1,0:T(8,128)(2,1)S(1)}, u32[]{:S(2)}, u32[]{:S(2)}) collective-permute-start(bf16[3,2,256,128]{3,2,1,0:T(8,128)(2,1)S(1)} %pad_maximum_fusion.1), channel_id=1, source_target_pairs={{0,1},{1,0},{2,3},{3,2},{4,5},{5,4},{6,7},{7,6},{8,9},{9,8},{10,11... | collective-permute-start | bytes 1179656 | tf_op jit(solution)/shard_map/ppermute | solution.py:25
  107.6 11.4 %collective-permute-start.22 = (bf16[3,2,128,128]{3,2,1,0:T(8,128)(2,1)S(1)}, bf16[3,2,128,128]{3,2,1,0:T(8,128)(2,1)S(1)}, u32[]{:S(2)}, u32[]{:S(2)}) collective-permute-start(bf16[3,2,128,128]{3,2,1,0:T(8,128)(2,1)S(1)} %add_convert_fusion), channel_id=1, source_target_pairs={{0,4},{1,5},{2,6},{3,7},{4,0},{5,1},{6,2},{7,3},{8,12},{9,13},{10,... | collective-permute-start | bytes 589832 | tf_op jit(solution)/shard_map/ppermute | solution.py:25
  108.4 7.0 %collective-permute-start.20 = (bf16[3,2,128,128]{3,2,1,0:T(8,128)(2,1)S(1)}, bf16[3,2,128,128]{3,2,1,0:T(8,128)(2,1)S(1)}, u32[]{:S(2)}, u32[]{:S(2)}) collective-permute-start(bf16[3,2,128,128]{3,2,1,0:T(8,128)(2,1)S(1)} %select_convert_fusion.1), channel_id=1, source_target_pairs={{0,2},{1,3},{2,0},{3,1},{4,6},{5,7},{6,4},{7,5},{8,10},{9,11},{10,... | collective-permute-start | bytes 589832 | tf_op jit(solution)/shard_map/ppermute | solution.py:25
  115.5 14.9 %collective-permute-start.21 = (bf16[3,2,256,128]{3,2,1,0:T(8,128)(2,1)S(1)}, bf16[3,2,256,128]{3,2,1,0:T(8,128)(2,1)S(1)}, u32[]{:S(2)}, u32[]{:S(2)}) collective-permute-start(bf16[3,2,256,128]{3,2,1,0:T(8,128)(2,1)S(1)} %pad_maximum_fusion.2), channel_id=1, source_target_pairs={{0,1},{1,0},{2,3},{3,2},{4,5},{5,4},{6,7},{7,6},{8,9},{9,8},{10,11... | collective-permute-start | bytes 1179656 | tf_op jit(solution)/shard_map/ppermute | solution.py:25
  119.1 5.7 %collective-permute-start.23 = (bf16[3,2,128,128]{3,2,1,0:T(8,128)(2,1)S(1)}, bf16[3,2,128,128]{3,2,1,0:T(8,128)(2,1)S(1)}, u32[]{:S(2)}, u32[]{:S(2)}) collective-permute-start(bf16[3,2,128,128]{3,2,1,0:T(8,128)(2,1)S(1)} %select_convert_fusion), channel_id=1, source_target_pairs={{0,2},{1,3},{2,0},{3,1},{4,6},{5,7},{6,4},{7,5},{8,10},{9,11},{10,... | collective-permute-start | bytes 589832 | tf_op jit(solution)/shard_map/ppermute | solution.py:25
  125.1 10.9 %collective-permute-start.25 = (bf16[1,2,256,128]{3,2,1,0:T(8,128)(2,1)S(1)}, bf16[1,2,256,128]{3,2,1,0:T(8,128)(2,1)S(1)}, u32[]{:S(2)}, u32[]{:S(2)}) collective-permute-start(bf16[1,2,256,128]{3,2,1,0:T(8,128)(2,1)S(1)} %get-tuple-element.121), channel_id=1, source_target_pairs={{0,1},{1,0},{2,3},{3,2},{4,5},{5,4},{6,7},{7,6},{8,9},{9,8},{10,11... | collective-permute-start | bytes 393224 | tf_op jit(solution)/shard_map/ppermute | solution.py:25
  127.1 14.1 %collective-permute-start.24 = (bf16[1,2,256,128]{3,2,1,0:T(8,128)(2,1)S(1)}, bf16[1,2,256,128]{3,2,1,0:T(8,128)(2,1)S(1)}, u32[]{:S(2)}, u32[]{:S(2)}) collective-permute-start(bf16[1,2,256,128]{3,2,1,0:T(8,128)(2,1)S(1)} %get-tuple-element.120), channel_id=1, source_target_pairs={{0,1},{1,0},{2,3},{3,2},{4,5},{5,4},{6,7},{7,6},{8,9},{9,8},{10,11... | collective-permute-start | bytes 393224 | tf_op jit(solution)/shard_map/ppermute | solution.py:25
  (25 other events, 151.2 us)

commit v5 on v4

--- a/solution.py
+++ b/solution.py
@@ -322,8 +322,11 @@
             return
         previous = piece
         if i == len(groups) - 1 and bit == order_of(i)[0]:
-            parts = [piece[q:q + 1] for q in range(piece.shape[0])]
-            state[i] = [(part, swap(part, "grid", bit)) for part in parts]
+            state[i] = []
+            for part in (piece[:1], piece[1:]):
+                if part.shape[0]:
+                    other = swap(part, "grid", bit)
+                    state[i] += [(part[q:q + 1], other[q:q + 1]) for q in range(part.shape[0])]
         else:
             state[i] = (piece, swap(piece, "grid", bit))
 

time: 152 us -> 153 us (level)
    ppermute x30 -> x29, waiting for transfers between devices: 61.2 us -> 61.9 us  [swap(): return lax.ppermute(value, axis, [(i, i ^ bit) for i in range(size)])]
    ppermute x30 -> x29, starting transfers between devices: 34.4 us -> 34.3 us  [swap(): return lax.ppermute(value, axis, [(i, i ^ bit) for i in range(size)])]
  transfers between devices with their start and end apart: 30 -> 29, of which waited for: 13 -> 13; matrix products, arithmetic and copies ran while one was open for 2% -> 2% of each run, Pallas kernels for 24% -> 20%
where the time goes in v5:
time: 153 us
  waiting for transfers between devices  61.9 us (40%)
  Pallas kernels  41.4 us (27%)
  starting transfers between devices  34.3 us (22%)
  local copies, waits for them, and re-layouts  10.9 us (7%)
  other arithmetic  3.28 us (2%)
    ppermute x29, waiting for transfers between devices, swap(): return lax.ppermute(value, axis, [(i, i ^ bit) for i in range(size)])  61.9 us
    ppermute x29, starting transfers between devices, swap(): return lax.ppermute(value, axis, [(i, i ^ bit) for i in range(size)])  34.3 us
    pallas_call x4, Pallas kernels, overlap(): pl.pallas_call(functools.partial(overlap_kernel, [offset for _, offset in...  21.6 us
    pallas_call x3, Pallas kernels, mix(): pl.pallas_call(functools.partial(mix_kernel, [at for at, _ in partners],...  15.8 us
    unnamed x38, local copies, waits for them, and re-layouts  8.31 us
    pallas_call x4, Pallas kernels, partial_sum(): pl.pallas_call(sum_kernel, grid_spec=pltpu.PrefetchScalarGridSpec(num_sca...  4 us
  transfers between devices with their start and end apart: 29, of which 13 were waited for; matrix products, arithmetic and copies ran while one was open for 2% of the time, Pallas kernels for 20%

profile of v5, /device:TPU:0, one launch (start us, length us, event | category | flops | bytes accessed | tf_op | source)
XLA Modules:
  0.0 152.8 jit_solution(3892546215803495634)
XLA Ops:
  2.1 3.0 %collective-permute-start.1 = (bf16[2,256,1024]{2,1,0:T(8,128)(2,1)S(1)}, bf16[2,256,1024]{2,1,0:T(8,128)(2,1)}, u32[]{:S(2)}, u32[]{:S(2)}) collective-permute-start(bf16[2,256,1024]{2,1,0:T(8,128)(2,1)S(1)} %slice.70), channel_id=1, source_target_pairs={{0,16},{8,24},{16,0},{24,8},{1,17},{9,25},{17,1},{25,9},{2,18},{10... | collective-permute-start | bytes 3145736 | tf_op jit(solution)/shard_map/ppermute | solution.py:25
  5.8 22.6 %collective-permute-done.1.refs_2_ = bf16[2,256,1024]{2,1,0:T(8,128)(2,1)} collective-permute-done((bf16[2,256,1024]{2,1,0:T(8,128)(2,1)S(1)}, bf16[2,256,1024]{2,1,0:T(8,128)(2,1)}, u32[]{:S(2)}, u32[]{:S(2)}) %collective-permute-start.1) | collective-permute-done | bytes 1048608 | tf_op jit(solution)/shard_map/ppermute | solution.py:25
  31.4 6.0 %shard_map.59 = (bf16[3,2,256,128]{3,2,1,0:T(8,128)(2,1)}, f32[3,2,256,128]{3,2,1,0:T(8,128)S(1)}, bf16[3,2,128,1024]{3,2,1,0:T(8,128)(2,1)S(1)}) custom-call(s32[3]{0:T(128)S(1)} %broadcast_xor_fusion.picks_ref, s32[1]{0:T(128)} %bitcast.3.half_ref, bf16[2,512,1024]{2,1,0:T(8,128)(2,1)S(1)} %bitcast.7, f32[3,2,1024]{2,1,0:T(2,128)S(1)} %copy-done.9, ...), custom_call_target="tpu_custom_call" | custom-call | flops 1 | bytes 1 | tf_op jit(solution)/shard_map/pallas_call | solution.py:71
  41.2 5.3 %shard_map.60 = (bf16[3,2,256,128]{3,2,1,0:T(8,128)(2,1)S(1)}, f32[3,2,256,128]{3,2,1,0:T(8,128)S(1)}, bf16[3,2,128,1024]{3,2,1,0:T(8,128)(2,1)S(1)}) custom-call(s32[3]{0:T(128)S(1)} %broadcast_xor_fusion.picks_ref, s32[1]{0:T(128)} %bitcast.3.half_ref, bf16[2,512,1024]{2,1,0:T(8,128)(2,1)S(1)} %bitcast.9, f32[3,2,1024]{2,1,0:T(2,128)S(1)} %copy-done.9, ...), custom_call_target="tpu_custom_call" | custom-call | flops 1 | bytes 1 | tf_op jit(solution)/shard_map/pallas_call | solution.py:71
  47.7 3.3 %collective-permute-done.3.arriving_ref = bf16[3,2,256,128]{3,2,1,0:T(8,128)(2,1)} collective-permute-done((bf16[3,2,256,128]{3,2,1,0:T(8,128)(2,1)}, bf16[3,2,256,128]{3,2,1,0:T(8,128)(2,1)}, u32[]{:S(2)}, u32[]{:S(2)}) %collective-permute-start.3) | collective-permute-done | bytes 393248 | tf_op jit(solution)/shard_map/ppermute | solution.py:25
  51.0 1.9 %shard_map.61 = (bf16[3,2,128,128]{3,2,1,0:T(8,128)(2,1)S(1)}, f32[3,2,128,128]{3,2,1,0:T(8,128)S(1)}) custom-call(s32[1]{0:T(128)} %bitcast.2.half_ref, f32[3,2,256,128]{3,2,1,0:T(8,128)S(1)} %copy-done.15, bf16[3,2,256,128]{3,2,1,0:T(8,128)(2,1)} %collective-permute-done.3.arriving_ref), custom_call_target="tpu_custom_call" | custom-call | flops 1 | bytes 1 | tf_op jit(solution)/shard_map/pallas_call | solution.py:117
  52.9 2.4 %collective-permute-done.5.refs_2_ = bf16[2,256,1024]{2,1,0:T(8,128)(2,1)S(1)} collective-permute-done((bf16[2,256,1024]{2,1,0:T(8,128)(2,1)}, bf16[2,256,1024]{2,1,0:T(8,128)(2,1)S(1)}, u32[]{:S(2)}, u32[]{:S(2)}) %collective-permute-start.5) | collective-permute-done | bytes 1048608 | tf_op jit(solution)/shard_map/ppermute | solution.py:25
  58.8 5.4 %shard_map.62 = (bf16[3,2,256,128]{3,2,1,0:T(8,128)(2,1)}, f32[3,2,256,128]{3,2,1,0:T(8,128)S(1)}, bf16[3,2,128,1024]{3,2,1,0:T(8,128)(2,1)S(1)}) custom-call(s32[3]{0:T(128)S(1)} %broadcast_xor_fusion.picks_ref, s32[1]{0:T(128)} %bitcast.3.half_ref, bf16[2,512,1024]{2,1,0:T(8,128)(2,1)S(1)} %bitcast.11, f32[3,2,1024]{2,1,0:T(2,128)S(1)} %copy-done.9, ...), custom_call_target="tpu_custom_call" | custom-call | flops 1 | bytes 1 | tf_op jit(solution)/shard_map/pallas_call | solution.py:71
  68.9 2.6 %collective-permute-start.7 = (bf16[3,2,128,128]{3,2,1,0:T(8,128)(2,1)S(1)}, bf16[3,2,128,128]{3,2,1,0:T(8,128)(2,1)S(1)}, u32[]{:S(2)}, u32[]{:S(2)}) collective-permute-start(bf16[3,2,128,128]{3,2,1,0:T(8,128)(2,1)S(1)} %add_convert_fusion.3), channel_id=1, source_target_pairs={{0,4},{1,5},{2,6},{3,7},{4,0},{5,1},{6,2},{7,3},{8,12},{9,13},{10,... | collective-permute-start | bytes 589832 | tf_op jit(solution)/shard_map/ppermute | solution.py:25
  73.0 4.8 %shard_map.64 = (bf16[3,2,256,128]{3,2,1,0:T(8,128)(2,1)S(1)}, f32[3,2,256,128]{3,2,1,0:T(8,128)S(1)}, bf16[3,2,128,1024]{3,2,1,0:T(8,128)(2,1)S(1)}) custom-call(s32[3]{0:T(128)S(1)} %broadcast_xor_fusion.picks_ref, s32[1]{0:T(128)} %bitcast.3.half_ref, bf16[2,512,1024]{2,1,0:T(8,128)(2,1)S(1)} %bitcast.13, f32[3,2,1024]{2,1,0:T(2,128)S(1)} %copy-done.9, ...), custom_call_target="tpu_custom_call" | custom-call | flops 1 | bytes 1 | tf_op jit(solution)/shard_map/pallas_call | solution.py:71
  82.4 2.7 %collective-permute-start.13 = (bf16[3,2,128,128]{3,2,1,0:T(8,128)(2,1)S(1)}, bf16[3,2,128,128]{3,2,1,0:T(8,128)(2,1)S(1)}, u32[]{:S(2)}, u32[]{:S(2)}) collective-permute-start(bf16[3,2,128,128]{3,2,1,0:T(8,128)(2,1)S(1)} %add_convert_fusion.2), channel_id=1, source_target_pairs={{0,4},{1,5},{2,6},{3,7},{4,0},{5,1},{6,2},{7,3},{8,12},{9,13},{10,... | collective-permute-start | bytes 589832 | tf_op jit(solution)/shard_map/ppermute | solution.py:25
  86.2 1.9 %shard_map.65 = (bf16[3,2,128,128]{3,2,1,0:T(8,128)(2,1)S(1)}, f32[3,2,128,128]{3,2,1,0:T(8,128)S(1)}) custom-call(s32[1]{0:T(128)} %bitcast.2.half_ref, f32[3,2,256,128]{3,2,1,0:T(8,128)S(1)} %copy-done.13, bf16[3,2,256,128]{3,2,1,0:T(8,128)(2,1)} %collective-permute-done.11.arriving_ref), custom_call_target="tpu_custom_call" | custom-call | flops 1 | bytes 1 | tf_op jit(solution)/shard_map/pallas_call | solution.py:117
  88.3 3.9 %collective-permute-done.10 = bf16[3,2,128,128]{3,2,1,0:T(8,128)(2,1)S(1)} collective-permute-done((bf16[3,2,128,128]{3,2,1,0:T(8,128)(2,1)S(1)}, bf16[3,2,128,128]{3,2,1,0:T(8,128)(2,1)S(1)}, u32[]{:S(2)}, u32[]{:S(2)}) %collective-permute-start.10) | collective-permute-done | bytes 196640 | tf_op jit(solution)/shard_map/ppermute | solution.py:25
  93.5 2.9 %collective-permute-done.16 = bf16[3,2,128,128]{3,2,1,0:T(8,128)(2,1)S(1)} collective-permute-done((bf16[3,2,128,128]{3,2,1,0:T(8,128)(2,1)S(1)}, bf16[3,2,128,128]{3,2,1,0:T(8,128)(2,1)S(1)}, u32[]{:S(2)}, u32[]{:S(2)}) %collective-permute-start.16) | collective-permute-done | bytes 196640 | tf_op jit(solution)/shard_map/ppermute | solution.py:25
  98.3 6.8 %collective-permute-done.14 = bf16[3,2,128,128]{3,2,1,0:T(8,128)(2,1)S(1)} collective-permute-done((bf16[3,2,128,128]{3,2,1,0:T(8,128)(2,1)S(1)}, bf16[3,2,128,128]{3,2,1,0:T(8,128)(2,1)S(1)}, u32[]{:S(2)}, u32[]{:S(2)}) %collective-permute-start.14) | collective-permute-done | bytes 196640 | tf_op jit(solution)/shard_map/ppermute | solution.py:25
  109.7 5.8 %collective-permute-done.20 = bf16[3,2,128,128]{3,2,1,0:T(8,128)(2,1)S(1)} collective-permute-done((bf16[3,2,128,128]{3,2,1,0:T(8,128)(2,1)S(1)}, bf16[3,2,128,128]{3,2,1,0:T(8,128)(2,1)S(1)}, u32[]{:S(2)}, u32[]{:S(2)}) %collective-permute-start.20) | collective-permute-done | bytes 196640 | tf_op jit(solution)/shard_map/ppermute | solution.py:25
  115.5 3.4 %collective-permute-start.21 = (bf16[3,2,256,128]{3,2,1,0:T(8,128)(2,1)S(1)}, bf16[3,2,256,128]{3,2,1,0:T(8,128)(2,1)S(1)}, u32[]{:S(2)}, u32[]{:S(2)}) collective-permute-start(bf16[3,2,256,128]{3,2,1,0:T(8,128)(2,1)S(1)} %pad_maximum_fusion.2), channel_id=1, source_target_pairs={{0,1},{1,0},{2,3},{3,2},{4,5},{5,4},{6,7},{7,6},{8,9},{9,8},{10,11... | collective-permute-start | bytes 1179656 | tf_op jit(solution)/shard_map/ppermute | solution.py:25
  119.5 5.3 %collective-permute-done.23 = bf16[3,2,128,128]{3,2,1,0:T(8,128)(2,1)S(1)} collective-permute-done((bf16[3,2,128,128]{3,2,1,0:T(8,128)(2,1)S(1)}, bf16[3,2,128,128]{3,2,1,0:T(8,128)(2,1)S(1)}, u32[]{:S(2)}, u32[]{:S(2)}) %collective-permute-start.23) | collective-permute-done | bytes 196640 | tf_op jit(solution)/shard_map/ppermute | solution.py:25
  125.1 2.1 %collective-permute-start.24 = (bf16[2,2,256,128]{3,2,1,0:T(8,128)(2,1)S(1)}, bf16[2,2,256,128]{3,2,1,0:T(8,128)(2,1)S(1)}, u32[]{:S(2)}, u32[]{:S(2)}) collective-permute-start(bf16[2,2,256,128]{3,2,1,0:T(8,128)(2,1)S(1)} %fusion), channel_id=1, source_target_pairs={{0,1},{1,0},{2,3},{3,2},{4,5},{5,4},{6,7},{7,6},{8,9},{9,8},{10,11... | collective-permute-start | bytes 786440 | tf_op jit(solution)/shard_map/ppermute | solution.py:25
  127.1 3.2 %collective-permute-done.25 = bf16[1,2,256,128]{3,2,1,0:T(8,128)(2,1)S(1)} collective-permute-done((bf16[1,2,256,128]{3,2,1,0:T(8,128)(2,1)S(1)}, bf16[1,2,256,128]{3,2,1,0:T(8,128)(2,1)S(1)}, u32[]{:S(2)}, u32[]{:S(2)}) %collective-permute-start.25) | collective-permute-done | bytes 131104 | tf_op jit(solution)/shard_map/ppermute | solution.py:25
  130.7 5.3 %shard_map.67 = (bf16[3,1,2,512,1024]{4,3,2,1,0:T(8,128)(2,1)}, f32[1,1024]{1,0:T(1,128)S(1)}) custom-call(s32[1]{0:T(128)} %bitcast.count_ref, f32[3,2,1024]{2,1,0:T(2,128)S(1)} %copy-done.9, bf16[2,512,1024]{2,1,0:T(8,128)(2,1)S(1)} %bitcast.15, bf16[1,2,512,128]{3,2,1,0:T(8,128)(2,1)S(1)} %get-tuple-element.110.refs_0_, ...), custom_call_target="tpu_custom_call" | custom-call | flops 1 | bytes 1 | tf_op jit(solution)/shard_map/pallas_call | solution.py:188
  136.1 5.2 %shard_map.68 = (bf16[3,1,2,512,1024]{4,3,2,1,0:T(8,128)(2,1)}, f32[1,1024]{1,0:T(1,128)S(1)}) custom-call(s32[1]{0:T(128)} %bitcast.count_ref, f32[3,2,1024]{2,1,0:T(2,128)S(1)} %copy-done.9, bf16[2,512,1024]{2,1,0:T(8,128)(2,1)S(1)} %bitcast.16, bf16[1,2,512,128]{3,2,1,0:T(8,128)(2,1)S(1)} %get-tuple-element.112.refs_0_, ...), custom_call_target="tpu_custom_call", output_to_operand_aliasing={{0}: (11, {})} | custom-call | flops 1 | bytes 1 | tf_op jit(solution)/shard_map/pallas_call | solution.py:188
  141.4 5.3 %shard_map.69 = (bf16[3,1,2,512,1024]{4,3,2,1,0:T(8,128)(2,1)}, f32[1,1024]{1,0:T(1,128)S(1)}) custom-call(s32[1]{0:T(128)} %bitcast.count_ref, f32[3,2,1024]{2,1,0:T(2,128)S(1)} %copy-done.9, bf16[2,512,1024]{2,1,0:T(8,128)(2,1)S(1)} %bitcast.17, bf16[1,2,512,128]{3,2,1,0:T(8,128)(2,1)S(1)} %get-tuple-element.111.refs_0_, ...), custom_call_target="tpu_custom_call", output_to_operand_aliasing={{0}: (11, {})} | custom-call | flops 1 | bytes 1 | tf_op jit(solution)/shard_map/pallas_call | solution.py:188
  150.0 2.1 %collective-permute-done.26 = f32[3,1024]{1,0:T(4,128)S(1)} collective-permute-done((f32[3,1024]{1,0:T(4,128)S(1)}, f32[3,1024]{1,0:T(4,128)S(1)}, u32[]{:S(2)}, u32[]{:S(2)}) %collective-permute-start.26) | collective-permute-done | bytes 12320 | tf_op jit(solution)/shard_map/ppermute | solution.py:25
  (125 shorter events, 38.4 us)
Async XLA Ops:
  2.1 26.3 %collective-permute-start.1 = (bf16[2,256,1024]{2,1,0:T(8,128)(2,1)S(1)}, bf16[2,256,1024]{2,1,0:T(8,128)(2,1)}, u32[]{:S(2)}, u32[]{:S(2)}) collective-permute-start(bf16[2,256,1024]{2,1,0:T(8,128)(2,1)S(1)} %slice.70), channel_id=1, source_target_pairs={{0,16},{8,24},{16,0},{24,8},{1,17},{9,25},{17,1},{25,9},{2,18},{10... | collective-permute-start | bytes 3145736 | tf_op jit(solution)/shard_map/ppermute | solution.py:25
  5.1 26.3 %collective-permute-start = (bf16[2,512,1024]{2,1,0:T(8,128)(2,1)S(1)}, bf16[2,512,1024]{2,1,0:T(8,128)(2,1)}, u32[]{:S(2)}, u32[]{:S(2)}) collective-permute-start(bf16[2,512,1024]{2,1,0:T(8,128)(2,1)S(1)} %bitcast.5), channel_id=1, source_target_pairs={{0,8},{8,0},{16,24},{24,16},{1,9},{9,1},{17,25},{25,17},{2,10},{10... | collective-permute-start | bytes 6291464 | tf_op jit(solution)/shard_map/ppermute | solution.py:25
  29.5 25.8 %collective-permute-start.5 = (bf16[2,256,1024]{2,1,0:T(8,128)(2,1)}, bf16[2,256,1024]{2,1,0:T(8,128)(2,1)S(1)}, u32[]{:S(2)}, u32[]{:S(2)}) collective-permute-start(bf16[2,256,1024]{2,1,0:T(8,128)(2,1)} %slice.54), channel_id=1, source_target_pairs={{0,16},{8,24},{16,0},{24,8},{1,17},{9,25},{17,1},{25,9},{2,18},{10... | collective-permute-start | bytes 3145736 | tf_op jit(solution)/shard_map/ppermute | solution.py:25
  39.5 11.6 %collective-permute-start.3 = (bf16[3,2,256,128]{3,2,1,0:T(8,128)(2,1)}, bf16[3,2,256,128]{3,2,1,0:T(8,128)(2,1)}, u32[]{:S(2)}, u32[]{:S(2)}) collective-permute-start(bf16[3,2,256,128]{3,2,1,0:T(8,128)(2,1)} %get-tuple-element.56), channel_id=1, source_target_pairs={{0,1},{1,0},{2,3},{3,2},{4,5},{5,4},{6,7},{7,6},{8,9},{9,8},{10,11... | collective-permute-start | bytes 1179656 | tf_op jit(solution)/shard_map/ppermute | solution.py:25
  55.3 11.6 %collective-permute-start.8 = (bf16[3,2,256,128]{3,2,1,0:T(8,128)(2,1)S(1)}, bf16[3,2,256,128]{3,2,1,0:T(8,128)(2,1)S(1)}, u32[]{:S(2)}, u32[]{:S(2)}) collective-permute-start(bf16[3,2,256,128]{3,2,1,0:T(8,128)(2,1)S(1)} %get-tuple-element.58), channel_id=1, source_target_pairs={{0,1},{1,0},{2,3},{3,2},{4,5},{5,4},{6,7},{7,6},{8,9},{9,8},{10,11... | collective-permute-start | bytes 1179656 | tf_op jit(solution)/shard_map/ppermute | solution.py:25
  57.1 8.4 %collective-permute-start.4 = (bf16[3,2,128,128]{3,2,1,0:T(8,128)(2,1)S(1)}, bf16[3,2,128,128]{3,2,1,0:T(8,128)(2,1)S(1)}, u32[]{:S(2)}, u32[]{:S(2)}) collective-permute-start(bf16[3,2,128,128]{3,2,1,0:T(8,128)(2,1)S(1)} %get-tuple-element.61), channel_id=1, source_target_pairs={{0,2},{1,3},{2,0},{3,1},{4,6},{5,7},{6,4},{7,5},{8,10},{9,11},{10,... | collective-permute-start | bytes 589832 | tf_op jit(solution)/shard_map/ppermute | solution.py:25
  67.0 13.7 %collective-permute-start.9 = (bf16[3,2,128,128]{3,2,1,0:T(8,128)(2,1)S(1)}, bf16[3,2,128,128]{3,2,1,0:T(8,128)(2,1)S(1)}, u32[]{:S(2)}, u32[]{:S(2)}) collective-permute-start(bf16[3,2,128,128]{3,2,1,0:T(8,128)(2,1)S(1)} %get-tuple-element.70), channel_id=1, source_target_pairs={{0,2},{1,3},{2,0},{3,1},{4,6},{5,7},{6,4},{7,5},{8,10},{9,11},{10,... | collective-permute-start | bytes 589832 | tf_op jit(solution)/shard_map/ppermute | solution.py:25
  68.9 11.8 %collective-permute-start.7 = (bf16[3,2,128,128]{3,2,1,0:T(8,128)(2,1)S(1)}, bf16[3,2,128,128]{3,2,1,0:T(8,128)(2,1)S(1)}, u32[]{:S(2)}, u32[]{:S(2)}) collective-permute-start(bf16[3,2,128,128]{3,2,1,0:T(8,128)(2,1)S(1)} %add_convert_fusion.3), channel_id=1, source_target_pairs={{0,4},{1,5},{2,6},{3,7},{4,0},{5,1},{6,2},{7,3},{8,12},{9,13},{10,... | collective-permute-start | bytes 589832 | tf_op jit(solution)/shard_map/ppermute | solution.py:25
  71.5 13.6 %collective-permute-start.11 = (bf16[3,2,256,128]{3,2,1,0:T(8,128)(2,1)}, bf16[3,2,256,128]{3,2,1,0:T(8,128)(2,1)}, u32[]{:S(2)}, u32[]{:S(2)}) collective-permute-start(bf16[3,2,256,128]{3,2,1,0:T(8,128)(2,1)} %get-tuple-element.65), channel_id=1, source_target_pairs={{0,1},{1,0},{2,3},{3,2},{4,5},{5,4},{6,7},{7,6},{8,9},{9,8},{10,11... | collective-permute-start | bytes 1179656 | tf_op jit(solution)/shard_map/ppermute | solution.py:25
  80.8 11.5 %collective-permute-start.10 = (bf16[3,2,128,128]{3,2,1,0:T(8,128)(2,1)S(1)}, bf16[3,2,128,128]{3,2,1,0:T(8,128)(2,1)S(1)}, u32[]{:S(2)}, u32[]{:S(2)}) collective-permute-start(bf16[3,2,128,128]{3,2,1,0:T(8,128)(2,1)S(1)} %select_convert_fusion.3), channel_id=1, source_target_pairs={{0,2},{1,3},{2,0},{3,1},{4,6},{5,7},{6,4},{7,5},{8,10},{9,11},{10,... | collective-permute-start | bytes 589832 | tf_op jit(solution)/shard_map/ppermute | solution.py:25
  81.3 16.4 %collective-permute-start.15 = (bf16[3,2,256,128]{3,2,1,0:T(8,128)(2,1)}, bf16[3,2,256,128]{3,2,1,0:T(8,128)(2,1)S(1)}, u32[]{:S(2)}, u32[]{:S(2)}) collective-permute-start(bf16[3,2,256,128]{3,2,1,0:T(8,128)(2,1)} %copy-done.16), channel_id=1, source_target_pairs={{0,1},{1,0},{2,3},{3,2},{4,5},{5,4},{6,7},{7,6},{8,9},{9,8},{10,11... | collective-permute-start | bytes 1179656 | tf_op jit(solution)/shard_map/ppermute | solution.py:25
  82.4 10.6 %collective-permute-start.13 = (bf16[3,2,128,128]{3,2,1,0:T(8,128)(2,1)S(1)}, bf16[3,2,128,128]{3,2,1,0:T(8,128)(2,1)S(1)}, u32[]{:S(2)}, u32[]{:S(2)}) collective-permute-start(bf16[3,2,128,128]{3,2,1,0:T(8,128)(2,1)S(1)} %add_convert_fusion.2), channel_id=1, source_target_pairs={{0,4},{1,5},{2,6},{3,7},{4,0},{5,1},{6,2},{7,3},{8,12},{9,13},{10,... | collective-permute-start | bytes 589832 | tf_op jit(solution)/shard_map/ppermute | solution.py:25
  88.1 8.3 %collective-permute-start.16 = (bf16[3,2,128,128]{3,2,1,0:T(8,128)(2,1)S(1)}, bf16[3,2,128,128]{3,2,1,0:T(8,128)(2,1)S(1)}, u32[]{:S(2)}, u32[]{:S(2)}) collective-permute-start(bf16[3,2,128,128]{3,2,1,0:T(8,128)(2,1)S(1)} %get-tuple-element.77), channel_id=1, source_target_pairs={{0,2},{1,3},{2,0},{3,1},{4,6},{5,7},{6,4},{7,5},{8,10},{9,11},{10,... | collective-permute-start | bytes 589832 | tf_op jit(solution)/shard_map/ppermute | solution.py:25
  92.3 17.1 %collective-permute-start.12 = (bf16[3,2,256,128]{3,2,1,0:T(8,128)(2,1)S(1)}, bf16[3,2,256,128]{3,2,1,0:T(8,128)(2,1)S(1)}, u32[]{:S(2)}, u32[]{:S(2)}) collective-permute-start(bf16[3,2,256,128]{3,2,1,0:T(8,128)(2,1)S(1)} %pad_maximum_fusion), channel_id=1, source_target_pairs={{0,1},{1,0},{2,3},{3,2},{4,5},{5,4},{6,7},{7,6},{8,9},{9,8},{10,11... | collective-permute-start | bytes 1179656 | tf_op jit(solution)/shard_map/ppermute | solution.py:25
  93.1 12.0 %collective-permute-start.14 = (bf16[3,2,128,128]{3,2,1,0:T(8,128)(2,1)S(1)}, bf16[3,2,128,128]{3,2,1,0:T(8,128)(2,1)S(1)}, u32[]{:S(2)}, u32[]{:S(2)}) collective-permute-start(bf16[3,2,128,128]{3,2,1,0:T(8,128)(2,1)S(1)} %select_convert_fusion.2), channel_id=1, source_target_pairs={{0,2},{1,3},{2,0},{3,1},{4,6},{5,7},{6,4},{7,5},{8,10},{9,11},{10,... | collective-permute-start | bytes 589832 | tf_op jit(solution)/shard_map/ppermute | solution.py:25
  96.5 11.9 %collective-permute-start.18 = (bf16[3,2,128,128]{3,2,1,0:T(8,128)(2,1)S(1)}, bf16[3,2,128,128]{3,2,1,0:T(8,128)(2,1)S(1)}, u32[]{:S(2)}, u32[]{:S(2)}) collective-permute-start(bf16[3,2,128,128]{3,2,1,0:T(8,128)(2,1)S(1)} %add_convert_fusion.1), channel_id=1, source_target_pairs={{0,4},{1,5},{2,6},{3,7},{4,0},{5,1},{6,2},{7,3},{8,12},{9,13},{10,... | collective-permute-start | bytes 589832 | tf_op jit(solution)/shard_map/ppermute | solution.py:25
  97.8 9.7 %collective-permute-start.19 = (bf16[3,2,128,128]{3,2,1,0:T(8,128)(2,1)S(1)}, bf16[3,2,128,128]{3,2,1,0:T(8,128)(2,1)S(1)}, u32[]{:S(2)}, u32[]{:S(2)}) collective-permute-start(bf16[3,2,128,128]{3,2,1,0:T(8,128)(2,1)S(1)} %get-tuple-element.84), channel_id=1, source_target_pairs={{0,2},{1,3},{2,0},{3,1},{4,6},{5,7},{6,4},{7,5},{8,10},{9,11},{10,... | collective-permute-start | bytes 589832 | tf_op jit(solution)/shard_map/ppermute | solution.py:25
  105.1 14.2 %collective-permute-start.17 = (bf16[3,2,256,128]{3,2,1,0:T(8,128)(2,1)S(1)}, bf16[3,2,256,128]{3,2,1,0:T(8,128)(2,1)S(1)}, u32[]{:S(2)}, u32[]{:S(2)}) collective-permute-start(bf16[3,2,256,128]{3,2,1,0:T(8,128)(2,1)S(1)} %pad_maximum_fusion.1), channel_id=1, source_target_pairs={{0,1},{1,0},{2,3},{3,2},{4,5},{5,4},{6,7},{7,6},{8,9},{9,8},{10,11... | collective-permute-start | bytes 1179656 | tf_op jit(solution)/shard_map/ppermute | solution.py:25
  107.6 11.4 %collective-permute-start.22 = (bf16[3,2,128,128]{3,2,1,0:T(8,128)(2,1)S(1)}, bf16[3,2,128,128]{3,2,1,0:T(8,128)(2,1)S(1)}, u32[]{:S(2)}, u32[]{:S(2)}) collective-permute-start(bf16[3,2,128,128]{3,2,1,0:T(8,128)(2,1)S(1)} %add_convert_fusion), channel_id=1, source_target_pairs={{0,4},{1,5},{2,6},{3,7},{4,0},{5,1},{6,2},{7,3},{8,12},{9,13},{10,... | collective-permute-start | bytes 589832 | tf_op jit(solution)/shard_map/ppermute | solution.py:25
  108.5 7.0 %collective-permute-start.20 = (bf16[3,2,128,128]{3,2,1,0:T(8,128)(2,1)S(1)}, bf16[3,2,128,128]{3,2,1,0:T(8,128)(2,1)S(1)}, u32[]{:S(2)}, u32[]{:S(2)}) collective-permute-start(bf16[3,2,128,128]{3,2,1,0:T(8,128)(2,1)S(1)} %select_convert_fusion.1), channel_id=1, source_target_pairs={{0,2},{1,3},{2,0},{3,1},{4,6},{5,7},{6,4},{7,5},{8,10},{9,11},{10,... | collective-permute-start | bytes 589832 | tf_op jit(solution)/shard_map/ppermute | solution.py:25
  115.5 14.9 %collective-permute-start.21 = (bf16[3,2,256,128]{3,2,1,0:T(8,128)(2,1)S(1)}, bf16[3,2,256,128]{3,2,1,0:T(8,128)(2,1)S(1)}, u32[]{:S(2)}, u32[]{:S(2)}) collective-permute-start(bf16[3,2,256,128]{3,2,1,0:T(8,128)(2,1)S(1)} %pad_maximum_fusion.2), channel_id=1, source_target_pairs={{0,1},{1,0},{2,3},{3,2},{4,5},{5,4},{6,7},{7,6},{8,9},{9,8},{10,11... | collective-permute-start | bytes 1179656 | tf_op jit(solution)/shard_map/ppermute | solution.py:25
  119.1 5.7 %collective-permute-start.23 = (bf16[3,2,128,128]{3,2,1,0:T(8,128)(2,1)S(1)}, bf16[3,2,128,128]{3,2,1,0:T(8,128)(2,1)S(1)}, u32[]{:S(2)}, u32[]{:S(2)}) collective-permute-start(bf16[3,2,128,128]{3,2,1,0:T(8,128)(2,1)S(1)} %select_convert_fusion), channel_id=1, source_target_pairs={{0,2},{1,3},{2,0},{3,1},{4,6},{5,7},{6,4},{7,5},{8,10},{9,11},{10,... | collective-permute-start | bytes 589832 | tf_op jit(solution)/shard_map/ppermute | solution.py:25
  124.9 5.5 %collective-permute-start.25 = (bf16[1,2,256,128]{3,2,1,0:T(8,128)(2,1)S(1)}, bf16[1,2,256,128]{3,2,1,0:T(8,128)(2,1)S(1)}, u32[]{:S(2)}, u32[]{:S(2)}) collective-permute-start(bf16[1,2,256,128]{3,2,1,0:T(8,128)(2,1)S(1)} %fusion.8), channel_id=1, source_target_pairs={{0,1},{1,0},{2,3},{3,2},{4,5},{5,4},{6,7},{7,6},{8,9},{9,8},{10,11... | collective-permute-start | bytes 393224 | tf_op jit(solution)/shard_map/ppermute | solution.py:25
  125.1 10.9 %collective-permute-start.24 = (bf16[2,2,256,128]{3,2,1,0:T(8,128)(2,1)S(1)}, bf16[2,2,256,128]{3,2,1,0:T(8,128)(2,1)S(1)}, u32[]{:S(2)}, u32[]{:S(2)}) collective-permute-start(bf16[2,2,256,128]{3,2,1,0:T(8,128)(2,1)S(1)} %fusion), channel_id=1, source_target_pairs={{0,1},{1,0},{2,3},{3,2},{4,5},{5,4},{6,7},{7,6},{8,9},{9,8},{10,11... | collective-permute-start | bytes 786440 | tf_op jit(solution)/shard_map/ppermute | solution.py:25
  (24 other events, 149.8 us)
